TPU v7x, 256 devices: a whole 4x4x8 slice. The times are simulated.
256 devices in a mesh: row: 64 (over z, x, core), rep: 4 (over y).
Axes of the slice: x: 4, y: 4, z: 8, core: 2. Of those that a mesh axis runs over, the one named last changes fastest.
Arguments:
- features: bfloat16 [32768, 128], P(('row', 'rep')), may hold values from -6 to 6
- weight: bfloat16 [128, 128], replicated, may hold values from -0.5 to 0.5
- bias_terms: float32 [128], replicated, may hold values from -3 to 3
- cotangent: bfloat16 [32768, 128], P(('row', 'rep')), may hold values from -6 to 6
- tile_values: bfloat16 [64, 4, 128, 128, 128], P('row', 'rep'), may hold values from 0 to 0.026977539
- tile_rows: int32 [64, 4, 128], P('row', 'rep'), may hold values from 0 to 3, as said below
- tile_cols: int32 [64, 4, 128], P('row', 'rep'), may hold values from 0 to 63
- tile_count: int32 [64, 4], P('row', 'rep'), may hold values from 64 to 128, as said below
Outputs:
- output: bfloat16 [32768, 128], P(('row', 'rep'))
- grad_input: bfloat16 [32768, 128], P(('row', 'rep'))
- weight_grad: float32 [128, 128], replicated
- bias_grad: float32 [128], replicated
Inputs may be any that keep to these rules, and one draw needn't show every extreme that they name: Within one device the pairs (tile_rows, tile_cols) of its 128 slots are distinct. `tile_count`: some device has all 128 slots live.
All inputs are finite; a program needn't handle non-finite values.
Results may differ from a plain program's by a relative error of at most 0.008.
Values may be sent and summed in bfloat16 or wider, within the bound.
No kernel may reach another device: no remote copies, remote signals or barrier semaphores. Data moves between devices by JAX's collectives and lax.ppermute only.
A program may use at most 64 MiB of HBM per device.

v0:
```python
import jax
import jax.numpy as jnp
from jax import lax
from jax.sharding import PartitionSpec as P


def body(features, weight, bias_terms, cotangent, tile_values, tile_rows, tile_cols, tile_count):
    tile_block = tile_values[0, 0]
    tile_row = tile_rows[0, 0]
    tile_col = tile_cols[0, 0]
    live_count = tile_count[0, 0]
    tile_size = tile_block.shape[-1]
    slot_total = tile_block.shape[0]
    rep_count = lax.axis_size("rep")
    row_count = features.shape[0]
    panel_tiles = rep_count * row_count // tile_size
    width = features.shape[1]
    live_slots = (jnp.arange(slot_total) < live_count).astype(jnp.float32)
    highest = lax.Precision.HIGHEST
    gathered = lax.all_gather(features, "row", axis=0, tiled=True)
    column_tiles = gathered.shape[0] // tile_size
    column_blocks = gathered.reshape(column_tiles, tile_size, width)
    picked = jnp.take(column_blocks, tile_col, axis=0)
    products = jnp.einsum("kij,kjf->kif", tile_block, picked, preferred_element_type=jnp.float32)
    chooser = (tile_row[None, :] == jnp.arange(panel_tiles)[:, None]).astype(
        jnp.float32
    ) * live_slots[None, :]
    partial_value = jnp.einsum("pk,kif->pif", chooser, products, precision=highest).reshape(
        panel_tiles * tile_size, width
    )
    grad_scale = (row_count * lax.axis_size("row") * rep_count) ** (-0.5)
    own_rows = lax.psum_scatter(partial_value, "rep", scatter_dimension=0, tiled=True)
    aggregated = own_rows.astype(jnp.bfloat16)
    preact = jnp.dot(aggregated, weight, preferred_element_type=jnp.float32) + bias_terms
    output = jax.nn.silu(preact).astype(jnp.bfloat16)
    sigmoid_pre = jax.nn.sigmoid(preact)
    grad_pre = (
        cotangent.astype(jnp.float32) * sigmoid_pre * (1.0 + preact * (1.0 - sigmoid_pre))
    ).astype(jnp.bfloat16)
    weight_terms = jnp.einsum("nf,nh->fh", aggregated, grad_pre, preferred_element_type=jnp.float32)
    bias_part = jnp.sum(grad_pre.astype(jnp.float32), axis=0)
    weight_grad, bias_grad = lax.psum((weight_terms, bias_part), ("row", "rep"))
    back_rows = jnp.dot(grad_pre, weight.T, preferred_element_type=jnp.float32).astype(jnp.bfloat16)
    back_panel = lax.all_gather(back_rows, "rep", axis=0, tiled=True)
    panel_blocks = back_panel.reshape(panel_tiles, tile_size, width)
    picked_back = jnp.take(panel_blocks, tile_row, axis=0)
    back_products = jnp.einsum(
        "kji,kjf->kif", tile_block, picked_back, preferred_element_type=jnp.float32
    )
    col_chooser = (tile_col[None, :] == jnp.arange(column_tiles)[:, None]).astype(
        jnp.float32
    ) * live_slots[None, :]
    contrib = jnp.einsum("ck,kif->cif", col_chooser, back_products, precision=highest)
    grad_rows = lax.psum_scatter(
        contrib.reshape(column_tiles * tile_size, width), "row", scatter_dimension=0, tiled=True
    )
    grad_input = grad_rows.astype(jnp.bfloat16)
    return (output, grad_input, weight_grad * grad_scale, bias_grad * grad_scale)


def solution(mesh):
    return jax.shard_map(
        body,
        mesh=mesh,
        in_specs=(
            P(("row", "rep"), None),
            P(),
            P(),
            P(("row", "rep"), None),
            P("row", "rep", None, None, None),
            P("row", "rep", None),
            P("row", "rep", None),
            P("row", "rep"),
        ),
        out_specs=(P(("row", "rep"), None), P(("row", "rep"), None), P(), P()),
        check_vma=False,
    )
```

profile of v0, /device:TPU:3, one launch (start us, length us, event | category | flops | bytes accessed | tf_op | source)
XLA Modules:
  0.0 534.2 jit_solution(4647840296945119416)
XLA Ops:
  7.2 0.0 copy-start
  7.2 0.0 all-gather.2.cloned.1.call-start
  7.2 0.7 all-gather.2.cloned.1.call-update
  7.9 0.0 reduce-scatter.3.cloned.1.call-start
  8.6 0.7 fusion.27
  9.3 0.7 compare_and_fusion.1
  9.9 80.5 %all-gather.2.cloned.1.call-done = bf16[8192,128]{1,0:T(8,128)(2,1)} async-done(((bf16[128,128]{1,0:T(8,128)(2,1)}), bf16[8192,128]{1,0:T(8,128)(2,1)}) %all-gather.2.cloned.1.call-update) | async-done | bytes 2097168 | tf_op jit(solution)/shard_map/all_gather | solution.py:20
  90.5 4.6 gather_fusion
  95.1 9.9 %fusion.6 = f32[128,128,128]{2,1,0:T(8,128)} fusion(bf16[1,1,128,128,128]{4,3,2,1,0:T(8,128)(2,1)} %param.12, bf16[128,128,128]{2,1,0:T(8,128)(2,1)} %gather_fusion, pred[128]{0:T(512)(128)(4,1)S(1)} %compare_and_fusion.1), kind=kOutput, calls=%fused_computation.8 | convolution fusion | flops 538968064 | bytes 16777344 | tf_op jit(solution)/shard_map/kij,kjf->kif/dot_general | solution.py:24
  105.0 0.0 copy-start.1
  105.0 9.3 %copy.14 = f32[128,128,128]{1,0,2:T(8,128)} copy(f32[128,128,128]{2,1,0:T(8,128)} %fusion.6) | data formatting | bytes 16777216 | tf_op jit(solution)/shard_map/kij,kjf->kif/dot_general | solution.py:24
  114.3 0.0 copy-done.1
  114.3 0.0 copy-start.3
  114.3 0.0 copy-start.4
  114.3 6.4 %fusion.2 = f32[4,128,128]{2,0,1:T(4,128)S(1)} fusion(f32[128,128,128]{1,0,2:T(8,128)} %copy.14, f32[128]{0:T(128)S(1)} %compare_convert_fusion, s32[128]{0:T(128)S(1)} %bitcast.43), kind=kOutput, calls=%fused_computation.4 | convolution fusion | flops 100664320 | bytes 8651776 | tf_op jit(solution)/shard_map/pk,kif->pif/dot_general | solution.py:28
  120.7 0.7 copy.12
  121.4 0.0 reduce-scatter.3.cloned.1.call-update
  121.4 0.0 all-reduce.2.cloned.1.call-start
  121.5 19.2 %reduce-scatter.3.cloned.1.call-done = f32[128,128]{1,0:T(8,128)} async-done(((f32[512,128]{1,0:T(8,128)}), f32[128,128]{1,0:T(8,128)}) %reduce-scatter.3.cloned.1.call-update) | async-done | bytes 65552 | tf_op jit(solution)/shard_map/reduce_scatter | solution.py:32
  140.7 0.0 copy-done
  140.7 0.0 copy-done.3
  140.7 0.0 copy-done.4
  140.7 1.6 convert_reduce_fusion
  142.3 0.1 convolution_convert_fusion
  142.5 1.7 fusion.19
  144.1 0.0 all-reduce.2.cloned.1.call-update
  144.2 0.0 reduce-scatter.5.cloned.1.call-start
  144.2 9.3 %all_gather.7 = bf16[512,128]{1,0:T(8,128)(2,1)S(1)} all-gather(bf16[128,128]{1,0:T(8,128)(2,1)S(1)} %convolution_convert_fusion), channel_id=1, replica_groups=mesh['row'=64,'rep'=4] {'rep'}, dimensions={0}, use_global_device_ids=true | all-gather | bytes 163840 | tf_op jit(solution)/shard_map/all_gather | solution.py:44
  153.5 3.0 gather_fusion.1
  156.5 8.4 %fusion.4 = f32[128,128,128]{2,1,0:T(8,128)} fusion(bf16[1,1,128,128,128]{4,3,2,1,0:T(8,128)(2,1)} %param.12, bf16[128,128,128]{2,1,0:T(8,128)(2,1)} %gather_fusion.1, pred[128]{0:T(512)(128)(4,1)S(1)} %compare_and_fusion), kind=kOutput, calls=%fused_computation.6 | convolution fusion | flops 538968064 | bytes 16777344 | tf_op jit(solution)/shard_map/kji,kjf->kif/dot_general | solution.py:47
  164.9 0.0 copy-start.2
  164.9 9.3 %copy.15 = f32[128,128,128]{1,0,2:T(8,128)} copy(f32[128,128,128]{2,1,0:T(8,128)} %fusion.4) | data formatting | bytes 16777216 | tf_op jit(solution)/shard_map/kji,kjf->kif/dot_general | solution.py:47
  174.2 0.0 copy-done.2
  174.2 6.8 %fusion = f32[64,128,128]{2,0,1:T(8,128)S(1)} fusion(f32[128,128,128]{1,0,2:T(8,128)} %copy.15, f32[128]{0:T(128)S(1)} %compare_convert_fusion, s32[128]{0:T(128)S(1)} %bitcast.44), kind=kOutput, calls=%fused_computation.2 | convolution fusion | flops 1610629120 | bytes 12583936 | tf_op jit(solution)/shard_map/ck,kif->cif/dot_general | solution.py:53
  181.0 4.4 copy.13
  185.4 0.0 reduce-scatter.5.cloned.1.call-update
  185.4 79.6 %psum.15 = f32[128]{0:T(128)S(1)} all-reduce(f32[128]{0:T(128)S(1)} %get-tuple-element.4), channel_id=1, replica_groups=mesh['row'=64,'rep'=4] {'row','rep'}, use_global_device_ids=true, to_apply=%region_4.5 | all-reduce | flops 128 | bytes 1024 | tf_op jit(solution)/shard_map/psum | solution.py:42
  265.0 0.5 broadcast_multiply_fusion.1
  265.5 121.5 %all-reduce.2.cloned.1.call-done = f32[128,128]{1,0:T(8,128)} async-done(((f32[128,128]{1,0:T(8,128)}), f32[128,128]{1,0:T(8,128)}) %all-reduce.2.cloned.1.call-update) | async-done | bytes 65552 | tf_op jit(solution)/shard_map/psum | solution.py:42
  387.0 1.5 broadcast_multiply_fusion
  388.5 137.7 %reduce-scatter.5.cloned.1.call-done = f32[128,128]{1,0:T(8,128)} async-done(((f32[8192,128]{1,0:T(8,128)}), f32[128,128]{1,0:T(8,128)}) %reduce-scatter.5.cloned.1.call-update) | async-done | bytes 65552 | tf_op jit(solution)/shard_map/reduce_scatter | solution.py:54
  526.2 1.5 convert_element_type.36
  (5 shorter events, 0.0 us)
Async XLA Ops:
  7.2 133.5 %copy-start = (bf16[128,128]{1,0:T(8,128)(2,1)S(1)}, bf16[128,128]{1,0:T(8,128)(2,1)}, u32[]{:S(2)}) copy-start(bf16[128,128]{1,0:T(8,128)(2,1)} %param.9) | copy-start | bytes 98308
  7.2 83.3 %all-gather.2.cloned.1.call-start = ((), (), s32[]{:S(2)}) async-start(), calls=%async_computation.2 | async-start | bytes 2129920 | tf_op jit(solution)/shard_map/all_gather | solution.py:20
  7.9 132.8 %reduce-scatter.3.cloned.1.call-start = ((), (), s32[]{:S(2)}) async-start(), calls=%async_computation.3 | async-start | bytes 327680 | tf_op jit(solution)/shard_map/reduce_scatter | solution.py:32
  105.0 9.3 %copy-start.1 = (s32[1,1,128]{2,1,0:T(1,128)S(1)}, s32[1,1,128]{2,1,0:T(1,128)}, u32[]{:S(2)}) copy-start(s32[1,1,128]{2,1,0:T(1,128)} %param.13) | copy-start | bytes 1540
  114.3 26.4 %copy-start.3 = (bf16[128,128]{1,0:T(8,128)(2,1)S(1)}, bf16[128,128]{1,0:T(8,128)(2,1)}, u32[]{:S(2)}) copy-start(bf16[128,128]{1,0:T(8,128)(2,1)} %param.11) | copy-start | bytes 98308
  114.3 26.4 %copy-start.4 = (f32[128]{0:T(128)S(1)}, f32[128]{0:T(128)}, u32[]{:S(2)}) copy-start(f32[128]{0:T(128)} %param.10) | copy-start | bytes 1540
  121.4 265.6 %all-reduce.2.cloned.1.call-start = ((), (), s32[]{:S(2)}) async-start(), calls=%async_computation.5 | async-start | bytes 131072 | tf_op jit(solution)/shard_map/psum | solution.py:42
  144.2 382.1 %reduce-scatter.5.cloned.1.call-start = ((), (), s32[]{:S(2)}) async-start(), calls=%async_computation.4 | async-start | bytes 4259840 | tf_op jit(solution)/shard_map/reduce_scatter | solution.py:54
  164.9 9.3 %copy-start.2 = (s32[1,1,128]{2,1,0:T(1,128)S(1)}, s32[1,1,128]{2,1,0:T(1,128)}, u32[]{:S(2)}) copy-start(s32[1,1,128]{2,1,0:T(1,128)} %param.14) | copy-start | bytes 1540
Sparse Core Ops, SparseCore 0:
  10.8 79.6 all-gather.1
  121.5 19.1 reduce-scatter.2
  147.7 239.2 all-reduce.1
  391.6 134.6 reduce-scatter.4
where the time goes:
time: 541 us; the launch traced here: 534 us
  waiting for transfers between devices  360 us (67%)
  blocking collectives  88.9 us (16%)
  matrix products  34.9 us (6%)
  local copies, waits for them, and re-layouts  31.3 us (6%)
  between operations  14.5 us (3%)
    reduce_scatter x1, waiting for transfers between devices, body(): lax.psum_scatter(contrib.reshape(column_tiles * tile_size, width), 'row',...  138 us
    psum x1, waiting for transfers between devices, body(): weight_grad, bias_grad = lax.psum((weight_terms, bias_part), ('row', 'rep'))  122 us
    all_gather x1, waiting for transfers between devices, body(): gathered = lax.all_gather(features, 'row', axis=0, tiled=True)  80.5 us
    psum x1, blocking collectives, body(): weight_grad, bias_grad = lax.psum((weight_terms, bias_part), ('row', 'rep'))  79.6 us
    reduce_scatter x1, waiting for transfers between devices, body(): lax.psum_scatter(partial_value, 'rep', scatter_dimension=0, tiled=True)  19.2 us
  transfers between devices with their start and end apart: 4, of which 4 were waited for; matrix products, arithmetic and copies ran while one was open for 7% of the time, Pallas kernels for 0%

commit v1 on v0

v1 whole, which is shorter than its diff:
```python
import jax
import jax.numpy as jnp
from jax import lax
from jax.experimental import pallas as pl
from jax.experimental.pallas import tpu as pltpu
from jax.sharding import Mesh
from jax.sharding import PartitionSpec as P

Z, X, C, Q = 8, 4, 2, 4
T = 128
PANEL = Q * T
SLOTS = 128
HALF = T // 2
PAY = HALF + 16
MSG = Z * T + PAY
BLK = T + PAY
F32 = jnp.float32
BF16 = jnp.bfloat16
ROW = ("z", "x", "core")
ALL = ("z", "x", "core", "rep")
SCALE = (Z * X * C * Q * T) ** -0.5

VMEM = pl.BlockSpec(memory_space=pltpu.VMEM)
SMEM = pl.BlockSpec(memory_space=pltpu.SMEM)


def params(mib):
    return pltpu.CompilerParams(vmem_limit_bytes=mib * 2**20)


def shift(axis, size, by):
    return [(i, (i + by) % size) for i in range(size)]


def send(array, axis, size, by):
    return lax.ppermute(array, axis, shift(axis, size, by))


def densify_kernel(rows_ref, cols_ref, count_ref, me_ref, tiles_ref, dense_ref):
    def clear(p, carry):
        dense_ref[p] = jnp.zeros((PANEL, T), BF16)
        return carry

    lax.fori_loop(0, Z * X * C, clear, 0)
    x, core = me_ref[0], me_ref[1]

    def place(k, carry):
        col = cols_ref[k]
        z_col = col // (X * C)
        x_col = (col // C) % X
        core_col = col % C
        offset = (x - x_col + X) % X
        other = (core + core_col) % C
        position = (offset * C + other) * Z + z_col
        row = pl.multiple_of(rows_ref[k] * T, T)
        dense_ref[position, pl.ds(row, T), :] = tiles_ref[k]
        return carry

    lax.fori_loop(0, count_ref[0], place, 0)


def densify(rows, cols, count, me, tiles):
    return pl.pallas_call(
        densify_kernel,
        in_specs=[SMEM, SMEM, SMEM, SMEM, VMEM],
        out_specs=VMEM,
        out_shape=jax.ShapeDtypeStruct((Z * X * C, PANEL, T), BF16),
        compiler_params=params(16),
        name="densify",
    )(rows, cols, count, me, tiles)


def forward(dense, gathered):
    def kernel(dense_ref, *refs):
        sources, out_ref, total = refs[:-2], refs[-2], refs[-1]
        for n, source in enumerate(sources):
            panel = jnp.concatenate([dense_ref[n * Z + z] for z in range(Z)], axis=1)
            part = jnp.dot(panel, source[...].reshape(Z * T, T), preferred_element_type=F32)
            if n == 0:
                total[...] = part
            else:
                total[...] += part
        out_ref[...] = total[...].astype(BF16)

    return pl.pallas_call(
        kernel,
        in_specs=[VMEM] * (1 + len(gathered)),
        out_specs=VMEM,
        out_shape=jax.ShapeDtypeStruct((PANEL, T), BF16),
        scratch_shapes=[pltpu.VMEM((PANEL, T), F32)],
        compiler_params=params(16),
        name="forward",
    )(dense, *gathered)


def split(value):
    high = value.astype(BF16)
    low = (value - high.astype(F32)).astype(BF16)
    return high, low


def pack_bias(ref, start, value):
    high, low = split(value)
    rows = lax.broadcasted_iota(jnp.int32, (16, T), 0)
    packed = jnp.where(rows == 0, high.astype(F32), jnp.where(rows == 1, low.astype(F32), 0.0))
    ref[start:start + 16, :] = packed.astype(BF16)


def middle_kernel(me_ref, p0, p1, p2, p3, c0, c1, c2, c3, weight_ref, bias_ref,
                  out_ref, back_ref, keep_ref, pay_ref, cot, pre, wsum):
    rep, core = me_ref[2], me_ref[1]
    for n, source in enumerate((c0, c1, c2, c3)):
        cot[(rep - n + Q) % Q] = source[...]
    total = (p0[...].astype(F32) + p2[...].astype(F32)) + (p1[...].astype(F32) + p3[...].astype(F32))
    aggregated = total.astype(BF16)
    preact = jnp.dot(aggregated, weight_ref[...], preferred_element_type=F32) + bias_ref[...]
    pre[...] = preact.reshape(Q, T, T)
    sig = jax.nn.sigmoid(preact)
    cotangent = cot[...].reshape(PANEL, T).astype(F32)
    grad_pre = (cotangent * sig * (1.0 + preact * (1.0 - sig))).astype(BF16)
    own = pre[rep]
    out_ref[...] = (own * jax.nn.sigmoid(own)).astype(BF16)
    back = lax.dot_general(weight_ref[...], grad_pre, (((1,), (1,)), ((), ())), preferred_element_type=F32)
    back_ref[...] = back.astype(BF16)
    terms = lax.dot_general(aggregated, grad_pre, (((0,), (0,)), ((), ())), preferred_element_type=F32)
    wsum[...] = terms.reshape(C, HALF, T)
    bias_sum = jnp.sum(grad_pre.astype(F32), axis=0, keepdims=True)
    keep_ref[:HALF] = wsum[core]
    high, low = split(bias_sum)
    keep_ref[HALF:HALF + 1] = high.astype(F32) + low.astype(F32)
    keep_ref[HALF + 1:] = jnp.zeros((15, T), F32)
    pay_ref[:HALF] = wsum[1 - core].astype(BF16)
    pack_bias(pay_ref, HALF, bias_sum)


def middle(me, partials, cotangents, weight, bias):
    return pl.pallas_call(
        middle_kernel,
        in_specs=[SMEM] + [VMEM] * 10,
        out_specs=[VMEM] * 4,
        out_shape=[
            jax.ShapeDtypeStruct((T, T), BF16),
            jax.ShapeDtypeStruct((T, PANEL), BF16),
            jax.ShapeDtypeStruct((PAY, T), F32),
            jax.ShapeDtypeStruct((PAY, T), BF16),
        ],
        scratch_shapes=[
            pltpu.VMEM((Q, T, T), BF16),
            pltpu.VMEM((Q, T, T), F32),
            pltpu.VMEM((C, HALF, T), F32),
        ],
        compiler_params=params(16),
        name="middle",
    )(me, *partials, *cotangents, weight, bias)


def backward(dense, back, chunk):
    def kernel(dense_ref, back_ref, mine_ref, theirs_ref):
        for n, ref in enumerate((mine_ref, theirs_ref)):
            for z in range(0, Z, 2):
                at = (chunk * C + n) * Z + z
                pair = jnp.concatenate([dense_ref[at], dense_ref[at + 1]], axis=1)
                part = jnp.dot(back_ref[...], pair, preferred_element_type=F32).astype(BF16)
                ref[z] = part[:, :T]
                ref[z + 1] = part[:, T:]

    return pl.pallas_call(
        kernel,
        in_specs=[VMEM] * 2,
        out_specs=[VMEM] * 2,
        out_shape=[jax.ShapeDtypeStruct((Z, T, T), BF16)] * 2,
        compiler_params=params(16),
        name="backward",
    )(dense, back)


def bias_of(ref, start):
    return ref[start:start + 1, :].astype(F32) + ref[start + 1:start + 2, :].astype(F32)


def pair_sum(mine, theirs, keep, pay):
    def kernel(mine_ref, theirs_ref, keep_ref, pay_ref, out_ref):
        total = mine_ref[...].astype(F32) + theirs_ref[...].astype(F32)
        out_ref[:Z * T] = total.astype(BF16).reshape(Z * T, T)
        out_ref[Z * T:Z * T + HALF] = (keep_ref[:HALF] + pay_ref[:HALF].astype(F32)).astype(BF16)
        pack_bias(out_ref, Z * T + HALF, keep_ref[HALF:HALF + 1] + bias_of(pay_ref, HALF))

    return pl.pallas_call(
        kernel,
        in_specs=[VMEM] * 4,
        out_specs=VMEM,
        out_shape=jax.ShapeDtypeStruct((MSG, T), BF16),
        compiler_params=params(16),
        name="pair_sum",
    )(mine, theirs, keep, pay)


def line_sum(s0, s1, s2, s3):
    def kernel(r0, r1, r2, r3, out_ref):
        def add(a, b):
            get = lambda r: r[a:b].astype(F32)
            return (get(r0) + get(r2)) + (get(r1) + get(r3))

        terms = add(Z * T, Z * T + HALF).astype(BF16)
        at = Z * T + HALF
        bias = (bias_of(r0, at) + bias_of(r2, at)) + (bias_of(r1, at) + bias_of(r3, at))
        for z in range(Z):
            out_ref[z, :T] = add(z * T, z * T + T).astype(BF16)
            out_ref[z, T:T + HALF] = terms
            pack_bias(out_ref.at[z], T + HALF, bias)

    return pl.pallas_call(
        kernel,
        in_specs=[VMEM] * 4,
        out_specs=VMEM,
        out_shape=jax.ShapeDtypeStruct((Z, BLK, T), BF16),
        compiler_params=params(16),
        name="line_sum",
    )(s0, s1, s2, s3)


def finish(received):
    def kernel(in_ref, grad_ref, half_ref, bias_ref):
        total = in_ref[0, :T + HALF].astype(F32)
        bias = bias_of(in_ref.at[0], T + HALF)
        for z in range(1, Z):
            total += in_ref[z, :T + HALF].astype(F32)
            bias += bias_of(in_ref.at[z], T + HALF)
        grad_ref[...] = total[:T].T.astype(BF16)
        half_ref[...] = total[T:] * SCALE
        bias_ref[...] = bias * SCALE

    return pl.pallas_call(
        kernel,
        in_specs=[VMEM],
        out_specs=[VMEM] * 3,
        out_shape=[
            jax.ShapeDtypeStruct((T, T), BF16),
            jax.ShapeDtypeStruct((HALF, T), F32),
            jax.ShapeDtypeStruct((1, T), F32),
        ],
        compiler_params=params(16),
        name="finish",
    )(received)


def body(features, weight, bias_terms, cotangent, tile_values, tile_rows, tile_cols, tile_count):
    x, core, rep = lax.axis_index("x"), lax.axis_index("core"), lax.axis_index("rep")
    me = jnp.stack([x, core, rep]).astype(jnp.int32)
    cotangents = [cotangent] + [send(cotangent, "rep", Q, n) for n in range(1, Q)]

    spread = jnp.broadcast_to(features, (Z, T, T))
    line = lax.all_to_all(spread, "z", 0, 0, tiled=True)
    lines = [line] + [send(line, "x", X, n) for n in range(1, X)]
    gathered = []
    for block in lines:
        gathered += [block, send(block, "core", C, 1)]
    dense = densify(tile_rows[0, 0], tile_cols[0, 0], tile_count[0], me, tile_values[0, 0])
    partial = forward(dense, gathered)

    partials = [partial] + [send(partial, "rep", Q, n) for n in range(1, Q)]
    output, back, keep, pay = middle(me, partials, cotangents, weight, bias_terms.reshape(1, T))
    paid = send(pay, "core", C, 1)

    sums = {}
    for n in (2, 1, 3, 0):
        mine, theirs = backward(dense, back, n)
        theirs = send(theirs, "core", C, 1)
        total = pair_sum(mine, theirs, keep, paid)
        sums[n] = send(total, "x", X, -n) if n else total
    blocks = line_sum(sums[0], sums[1], sums[2], sums[3])
    received = lax.all_to_all(blocks, "z", 0, 0, tiled=True)
    grad_input, half, bias_grad = finish(received)
    other = send(half, "core", C, 1)
    weight_grad = jnp.where(core == 0, jnp.concatenate([half, other]), jnp.concatenate([other, half]))
    return output, grad_input, weight_grad, bias_grad.reshape(T)


def solution(mesh):
    fine = Mesh(mesh.devices.reshape(Z, X, C, Q), ALL)
    return jax.shard_map(
        body,
        mesh=fine,
        in_specs=(
            P(ALL, None),
            P(),
            P(),
            P(ALL, None),
            P(ROW, "rep", None, None, None),
            P(ROW, "rep", None),
            P(ROW, "rep", None),
            P(ROW, "rep"),
        ),
        out_specs=(P(ALL, None), P(ALL, None), P(), P()),
        check_vma=False,
    )
```

time: 541 us -> 107 us (0.20); the launches traced: 534 us -> 107 us
  waiting for transfers between devices: 360 us -> 22.8 us
  blocking collectives: 88.9 us -> 35.6 us
  matrix products: 34.9 us -> 0 us
  starting transfers between devices: 0.16 us -> 30.7 us
  local copies, waits for them, and re-layouts: 31.3 us -> 4.31 us
  between operations: 14.5 us -> 1.44 us
  Pallas kernels: 0 us -> 11.6 us
    reduce_scatter x2 -> x0, waiting for transfers between devices: 157 us -> none  [the longest x1 138 us: body(): lax.psum_scatter(contrib.reshape(column_tiles * tile_size, width), 'row',...]
    psum x1 -> x0, waiting for transfers between devices: 122 us -> none  [body(): weight_grad, bias_grad = lax.psum((weight_terms, bias_part), ('row', 'rep'))]
    all_gather x1 -> x0, waiting for transfers between devices: 80.5 us -> none  [body(): gathered = lax.all_gather(features, 'row', axis=0, tiled=True)]
    psum x1 -> x0, blocking collectives: 79.6 us -> none  [body(): weight_grad, bias_grad = lax.psum((weight_terms, bias_part), ('row', 'rep'))]
    all_to_all x0 -> x2, blocking collectives: none -> 35.6 us  [the longest x1 18.4 us: body(): line = lax.all_to_all(spread, 'z', 0, 0, tiled=True)]
    dot_general x7 -> x0, matrix products: 34.9 us -> none  [the longest x1 9.91 us: body(): jnp.einsum('kij,kjf->kif', tile_block, picked, preferred_element_type=jnp...]
    ppermute x0 -> x22, starting transfers between devices: none -> 30.7 us  [send(): return lax.ppermute(array, axis, shift(axis, size, by))]
    dot_general x4 -> x0, local copies, waits for them, and re-layouts: 23.6 us -> none  [the longest x1 9.27 us: body(): jnp.einsum('kji,kjf->kif', tile_block, picked_back, preferred_element_typ...]
  transfers between devices with their start and end apart: 4 -> 22, of which waited for: 4 -> 9; matrix products, arithmetic and copies ran while one was open for 7% -> 0% of each run, Pallas kernels for 0% -> 6%
where the time goes in v1:
time: 107 us
  blocking collectives  35.6 us (33%)
  starting transfers between devices  30.7 us (29%)
  waiting for transfers between devices  22.8 us (21%)
  Pallas kernels  11.6 us (11%)
  local copies, waits for them, and re-layouts  4.31 us (4%)
  between operations  1.44 us (1%)
    ppermute x22, starting transfers between devices, send(): return lax.ppermute(array, axis, shift(axis, size, by))  30.7 us
    ppermute x22, waiting for transfers between devices, send(): return lax.ppermute(array, axis, shift(axis, size, by))  22.8 us
    all_to_all x1, blocking collectives, body(): line = lax.all_to_all(spread, 'z', 0, 0, tiled=True)  18.4 us
    all_to_all x1, blocking collectives, body(): received = lax.all_to_all(blocks, 'z', 0, 0, tiled=True)  17.2 us
    pallas_call x1, Pallas kernels, densify(): pl.pallas_call(densify_kernel, in_specs=[SMEM, SMEM, SMEM, SMEM, VMEM], o...  4.89 us
    unnamed x12, local copies, waits for them, and re-layouts  3.52 us
    pallas_call x1, Pallas kernels, forward(): pl.pallas_call(kernel, in_specs=[VMEM] * (1 + len(gathered)), out_specs=V...  2.33 us
  transfers between devices with their start and end apart: 22, of which 9 were waited for; matrix products, arithmetic and copies ran while one was open for 0% of the time, Pallas kernels for 6%

profile of v1, /device:TPU:3, one launch (start us, length us, event | category | flops | bytes accessed | tf_op | source)
XLA Modules:
  0.0 107.1 jit_solution(7554377528642505112)
XLA Ops:
  0.6 0.8 broadcast_in_dim.3
  1.4 18.4 %all_to_all.10.refs_0_ = bf16[8,128,128]{2,1,0:T(8,128)(2,1)S(1)} all-to-all(bf16[8,128,128]{2,1,0:T(8,128)(2,1)S(1)} %broadcast_in_dim.3), channel_id=1, replica_groups=mesh['z'=8,'x'=4,'core'=2,'rep'=4] {'z'}, dimensions={0} | all-to-all | bytes 524288 | tf_op jit(solution)/shard_map/all_to_all | solution.py:253
  19.8 1.2 %collective-permute-start.1 = (bf16[8,128,128]{2,1,0:T(8,128)(2,1)S(1)}, bf16[8,128,128]{2,1,0:T(8,128)(2,1)S(1)}, u32[]{:S(2)}, u32[]{:S(2)}) collective-permute-start(bf16[8,128,128]{2,1,0:T(8,128)(2,1)S(1)} %all_to_all.10.refs_0_), channel_id=1, source_target_pairs={{0,8},{8,16},{16,24},{24,0},{1,9},{9,17},{17,25},{25,1},{2,10},{10... | collective-permute-start | bytes 786440 | tf_op jit(solution)/shard_map/ppermute | solution.py:36
  21.0 0.8 collective-permute-start.3
  21.8 1.9 %collective-permute-start.5 = (bf16[8,128,128]{2,1,0:T(8,128)(2,1)S(1)}, bf16[8,128,128]{2,1,0:T(8,128)(2,1)S(1)}, u32[]{:S(2)}, u32[]{:S(2)}) collective-permute-start(bf16[8,128,128]{2,1,0:T(8,128)(2,1)S(1)} %all_to_all.10.refs_0_), channel_id=1, source_target_pairs={{0,24},{8,0},{16,8},{24,16},{1,25},{9,1},{17,9},{25,17},{2,26},{10... | collective-permute-start | bytes 786440 | tf_op jit(solution)/shard_map/ppermute | solution.py:36
  23.7 3.3 %collective-permute-start = (bf16[8,128,128]{2,1,0:T(8,128)(2,1)S(1)}, bf16[8,128,128]{2,1,0:T(8,128)(2,1)S(1)}, u32[]{:S(2)}, u32[]{:S(2)}) collective-permute-start(bf16[8,128,128]{2,1,0:T(8,128)(2,1)S(1)} %all_to_all.10.refs_0_), channel_id=1, source_target_pairs={{0,4},{4,0},{1,5},{5,1},{2,6},{6,2},{3,7},{7,3},{8,12},{12,8},{9,1... | collective-permute-start | bytes 786440 | tf_op jit(solution)/shard_map/ppermute | solution.py:36
  27.0 4.3 %collective-permute-start.2 = (bf16[8,128,128]{2,1,0:T(8,128)(2,1)S(1)}, bf16[8,128,128]{2,1,0:T(8,128)(2,1)S(1)}, u32[]{:S(2)}, u32[]{:S(2)}) collective-permute-start(bf16[8,128,128]{2,1,0:T(8,128)(2,1)S(1)} %collective-permute-done.1.refs_2_), channel_id=1, source_target_pairs={{0,4},{4,0},{1,5},{5,1},{2,6},{6,2},{3,7},{7,3},{8,12},{12,8},{9,1... | collective-permute-start | bytes 786440 | tf_op jit(solution)/shard_map/ppermute | solution.py:36
  31.3 2.8 %collective-permute-start.4 = (bf16[8,128,128]{2,1,0:T(8,128)(2,1)S(1)}, bf16[8,128,128]{2,1,0:T(8,128)(2,1)S(1)}, u32[]{:S(2)}, u32[]{:S(2)}) collective-permute-start(bf16[8,128,128]{2,1,0:T(8,128)(2,1)S(1)} %collective-permute-done.3.refs_4_), channel_id=1, source_target_pairs={{0,4},{4,0},{1,5},{5,1},{2,6},{6,2},{3,7},{7,3},{8,12},{12,8},{9,1... | collective-permute-start | bytes 786440 | tf_op jit(solution)/shard_map/ppermute | solution.py:36
  34.1 0.8 collective-permute-done.5.refs_6_
  34.9 1.2 %collective-permute-start.6 = (bf16[8,128,128]{2,1,0:T(8,128)(2,1)S(1)}, bf16[8,128,128]{2,1,0:T(8,128)(2,1)S(1)}, u32[]{:S(2)}, u32[]{:S(2)}) collective-permute-start(bf16[8,128,128]{2,1,0:T(8,128)(2,1)S(1)} %collective-permute-done.5.refs_6_), channel_id=1, source_target_pairs={{0,4},{4,0},{1,5},{5,1},{2,6},{6,2},{3,7},{7,3},{8,12},{12,8},{9,1... | collective-permute-start | bytes 786440 | tf_op jit(solution)/shard_map/ppermute | solution.py:36
  36.8 0.1 pad_add_fusion.me_ref
  36.9 2.2 %copy-done = bf16[1,1,128,128,128]{4,3,2,1,0:T(8,128)(2,1)S(1)} copy-done((bf16[1,1,128,128,128]{4,3,2,1,0:T(8,128)(2,1)S(1)}, bf16[1,1,128,128,128]{4,3,2,1,0:T(8,128)(2,1)}, u32[]{:S(2)}) %copy-start) | copy-done | bytes 4194328
  39.1 0.7 copy-done.4
  39.7 0.7 copy-done.5
  40.4 4.9 %densify.1.dense_ref = bf16[64,512,128]{2,1,0:T(8,128)(2,1)S(1)} custom-call(s32[128]{0:T(128)S(1)} %bitcast.12, s32[128]{0:T(128)S(1)} %bitcast.13, s32[1]{0:T(128)} %bitcast.9.count_ref, s32[3]{0:T(128)S(1)} %pad_add_fusion.me_ref, bf16[128,128,128]{2,1,0:T(8,128)(2,1)S(1)} %bitcast.10), custom_call_target="tpu_custom_call" | custom-call | tf_op jit(solution)/shard_map/densify/pallas_call | solution.py:63
  45.4 2.3 %forward.1.p0 = bf16[512,128]{1,0:T(8,128)(2,1)S(1)} custom-call(bf16[64,512,128]{2,1,0:T(8,128)(2,1)S(1)} %densify.1.dense_ref, bf16[8,128,128]{2,1,0:T(8,128)(2,1)S(1)} %all_to_all.10.refs_0_, bf16[8,128,128]{2,1,0:T(8,128)(2,1)S(1)} %collective-permute-done.refs_1_, bf16[8,128,128]{2,1,0:T(8,128)(2,1)S(1)} %collective-permute-done.1.refs_2_, ...), custom_call_target="tpu_custom_call" | custom-call | tf_op jit(solution)/shard_map/forward/pallas_call | solution.py:85
  47.7 1.2 %collective-permute-start.7 = (bf16[512,128]{1,0:T(8,128)(2,1)S(1)}, bf16[512,128]{1,0:T(8,128)(2,1)S(1)}, u32[]{:S(2)}, u32[]{:S(2)}) collective-permute-start(bf16[512,128]{1,0:T(8,128)(2,1)S(1)} %forward.1.p0), channel_id=1, source_target_pairs={{0,1},{1,2},{2,3},{3,0},{4,5},{5,6},{6,7},{7,4},{8,9},{9,10},{10,1... | collective-permute-start | bytes 393224 | tf_op jit(solution)/shard_map/ppermute | solution.py:36
  48.9 2.0 %collective-permute-start.8 = (bf16[512,128]{1,0:T(8,128)(2,1)S(1)}, bf16[512,128]{1,0:T(8,128)(2,1)S(1)}, u32[]{:S(2)}, u32[]{:S(2)}) collective-permute-start(bf16[512,128]{1,0:T(8,128)(2,1)S(1)} %forward.1.p0), channel_id=1, source_target_pairs={{0,2},{1,3},{2,0},{3,1},{4,6},{5,7},{6,4},{7,5},{8,10},{9,11},{10,... | collective-permute-start | bytes 393224 | tf_op jit(solution)/shard_map/ppermute | solution.py:36
  50.9 2.0 %collective-permute-start.9 = (bf16[512,128]{1,0:T(8,128)(2,1)S(1)}, bf16[512,128]{1,0:T(8,128)(2,1)S(1)}, u32[]{:S(2)}, u32[]{:S(2)}) collective-permute-start(bf16[512,128]{1,0:T(8,128)(2,1)S(1)} %forward.1.p0), channel_id=1, source_target_pairs={{0,3},{1,0},{2,1},{3,2},{4,7},{5,4},{6,5},{7,6},{8,11},{9,8},{10,9... | collective-permute-start | bytes 393224 | tf_op jit(solution)/shard_map/ppermute | solution.py:36
  52.9 1.2 %collective-permute-start.11 = (bf16[128,128]{1,0:T(8,128)(2,1)S(1)}, bf16[128,128]{1,0:T(8,128)(2,1)S(1)}, u32[]{:S(2)}, u32[]{:S(2)}) collective-permute-start(bf16[128,128]{1,0:T(8,128)(2,1)S(1)} %copy-done.1), channel_id=1, source_target_pairs={{0,2},{1,3},{2,0},{3,1},{4,6},{5,7},{6,4},{7,5},{8,10},{9,11},{10,... | collective-permute-start | bytes 98312 | tf_op jit(solution)/shard_map/ppermute | solution.py:36
  54.1 4.7 %collective-permute-done.10.c1 = bf16[128,128]{1,0:T(8,128)(2,1)S(1)} collective-permute-done((bf16[128,128]{1,0:T(8,128)(2,1)S(1)}, bf16[128,128]{1,0:T(8,128)(2,1)S(1)}, u32[]{:S(2)}, u32[]{:S(2)}) %collective-permute-start.10) | collective-permute-done | bytes 32800 | tf_op jit(solution)/shard_map/ppermute | solution.py:36
  58.7 2.8 %collective-permute-done.12.c3 = bf16[128,128]{1,0:T(8,128)(2,1)S(1)} collective-permute-done((bf16[128,128]{1,0:T(8,128)(2,1)S(1)}, bf16[128,128]{1,0:T(8,128)(2,1)S(1)}, u32[]{:S(2)}, u32[]{:S(2)}) %collective-permute-start.12) | collective-permute-done | bytes 32800 | tf_op jit(solution)/shard_map/ppermute | solution.py:36
  61.5 1.4 %middle.1 = (bf16[128,128]{1,0:T(8,128)(2,1)}, bf16[128,512]{1,0:T(8,128)(2,1)S(1)}, f32[80,128]{1,0:T(8,128)S(1)}, bf16[80,128]{1,0:T(8,128)(2,1)S(1)}) custom-call(s32[3]{0:T(128)S(1)} %pad_add_fusion.me_ref, bf16[512,128]{1,0:T(8,128)(2,1)S(1)} %forward.1.p0, bf16[512,128]{1,0:T(8,128)(2,1)S(1)} %collective-permute-done.7.p1, ...), custom_call_target="tpu_custom_call" | custom-call | tf_op jit(solution)/shard_map/middle/pallas_call | solution.py:137
  62.9 0.5 backward.7
  63.4 1.6 %collective-permute-start.19 = (bf16[8,128,128]{2,1,0:T(8,128)(2,1)S(1)}, bf16[8,128,128]{2,1,0:T(8,128)(2,1)S(1)}, u32[]{:S(2)}, u32[]{:S(2)}) collective-permute-start(bf16[8,128,128]{2,1,0:T(8,128)(2,1)S(1)} %get-tuple-element.30), channel_id=1, source_target_pairs={{0,4},{4,0},{1,5},{5,1},{2,6},{6,2},{3,7},{7,3},{8,12},{12,8},{9,1... | collective-permute-start | bytes 786440 | tf_op jit(solution)/shard_map/ppermute | solution.py:36
  65.0 0.4 backward.6
  65.5 0.3 collective-permute-start.17
  65.8 0.5 backward.5
  66.2 0.6 collective-permute-start.15
  66.8 0.1 collective-permute-start.14
  66.9 1.1 %collective-permute-done.14.pay_ref = bf16[80,128]{1,0:T(8,128)(2,1)S(1)} collective-permute-done((bf16[80,128]{1,0:T(8,128)(2,1)S(1)}, bf16[80,128]{1,0:T(8,128)(2,1)S(1)}, u32[]{:S(2)}, u32[]{:S(2)}) %collective-permute-start.14) | collective-permute-done | bytes 20512 | tf_op jit(solution)/shard_map/ppermute | solution.py:36
  68.0 0.1 pair_sum.7
  68.1 1.7 %collective-permute-start.20 = (bf16[1104,128]{1,0:T(8,128)(2,1)S(1)}, bf16[1104,128]{1,0:T(8,128)(2,1)S(1)}, u32[]{:S(2)}, u32[]{:S(2)}) collective-permute-start(bf16[1104,128]{1,0:T(8,128)(2,1)S(1)} %pair_sum.7), channel_id=1, source_target_pairs={{0,8},{8,16},{16,24},{24,0},{1,9},{9,17},{17,25},{25,1},{2,10},{10... | collective-permute-start | bytes 847880 | tf_op jit(solution)/shard_map/ppermute | solution.py:36
  69.8 1.4 %collective-permute-start.18 = (bf16[1104,128]{1,0:T(8,128)(2,1)S(1)}, bf16[1104,128]{1,0:T(8,128)(2,1)S(1)}, u32[]{:S(2)}, u32[]{:S(2)}) collective-permute-start(bf16[1104,128]{1,0:T(8,128)(2,1)S(1)} %pair_sum.6), channel_id=1, source_target_pairs={{0,16},{8,24},{16,0},{24,8},{1,17},{9,25},{17,1},{25,9},{2,18},{10... | collective-permute-start | bytes 847880 | tf_op jit(solution)/shard_map/ppermute | solution.py:36
  71.3 0.6 collective-permute-start.16
  71.9 0.4 backward.4
  72.3 1.0 collective-permute-start.13
  73.4 1.2 %collective-permute-done.13.theirs_ref = bf16[8,128,128]{2,1,0:T(8,128)(2,1)S(1)} collective-permute-done((bf16[8,128,128]{2,1,0:T(8,128)(2,1)S(1)}, bf16[8,128,128]{2,1,0:T(8,128)(2,1)S(1)}, u32[]{:S(2)}, u32[]{:S(2)}) %collective-permute-start.13) | collective-permute-done | bytes 262176 | tf_op jit(solution)/shard_map/ppermute | solution.py:36
  74.5 0.1 pair_sum.4.r0
  74.6 1.5 %collective-permute-done.20.r3 = bf16[1104,128]{1,0:T(8,128)(2,1)S(1)} collective-permute-done((bf16[1104,128]{1,0:T(8,128)(2,1)S(1)}, bf16[1104,128]{1,0:T(8,128)(2,1)S(1)}, u32[]{:S(2)}, u32[]{:S(2)}) %collective-permute-start.20) | collective-permute-done | bytes 282656 | tf_op jit(solution)/shard_map/ppermute | solution.py:36
  76.1 3.0 %collective-permute-done.18.r2 = bf16[1104,128]{1,0:T(8,128)(2,1)S(1)} collective-permute-done((bf16[1104,128]{1,0:T(8,128)(2,1)S(1)}, bf16[1104,128]{1,0:T(8,128)(2,1)S(1)}, u32[]{:S(2)}, u32[]{:S(2)}) %collective-permute-start.18) | collective-permute-done | bytes 282656 | tf_op jit(solution)/shard_map/ppermute | solution.py:36
  79.1 6.9 %collective-permute-done.16.r1 = bf16[1104,128]{1,0:T(8,128)(2,1)S(1)} collective-permute-done((bf16[1104,128]{1,0:T(8,128)(2,1)S(1)}, bf16[1104,128]{1,0:T(8,128)(2,1)S(1)}, u32[]{:S(2)}, u32[]{:S(2)}) %collective-permute-start.16) | collective-permute-done | bytes 282656 | tf_op jit(solution)/shard_map/ppermute | solution.py:36
  86.0 0.1 line_sum.1
  86.2 17.2 %all_to_all.11.in_ref = bf16[8,208,128]{2,1,0:T(8,128)(2,1)S(1)} all-to-all(bf16[8,208,128]{2,1,0:T(8,128)(2,1)S(1)} %line_sum.1), channel_id=1, replica_groups=mesh['z'=8,'x'=4,'core'=2,'rep'=4] {'z'}, dimensions={0} | all-to-all | bytes 851968 | tf_op jit(solution)/shard_map/all_to_all | solution.py:272
  103.4 0.7 finish.1
  104.2 1.5 %collective-permute-start.21 = (f32[64,128]{1,0:T(8,128)S(1)}, f32[64,128]{1,0:T(8,128)S(1)}, u32[]{:S(2)}, u32[]{:S(2)}) collective-permute-start(f32[64,128]{1,0:T(8,128)S(1)} %get-tuple-element.32), channel_id=1, source_target_pairs={{0,4},{4,0},{1,5},{5,1},{2,6},{6,2},{3,7},{7,3},{8,12},{12,8},{9,1... | collective-permute-start | bytes 98312 | tf_op jit(solution)/shard_map/ppermute | solution.py:36
  105.6 0.9 collective-permute-done.21
  106.5 0.6 maximum_select_fusion
  (26 shorter events, 0.2 us)
Async XLA Ops:
  19.8 7.2 %collective-permute-start.1 = (bf16[8,128,128]{2,1,0:T(8,128)(2,1)S(1)}, bf16[8,128,128]{2,1,0:T(8,128)(2,1)S(1)}, u32[]{:S(2)}, u32[]{:S(2)}) collective-permute-start(bf16[8,128,128]{2,1,0:T(8,128)(2,1)S(1)} %all_to_all.10.refs_0_), channel_id=1, source_target_pairs={{0,8},{8,16},{16,24},{24,0},{1,9},{9,17},{17,25},{25,1},{2,10},{10... | collective-permute-start | bytes 786440 | tf_op jit(solution)/shard_map/ppermute | solution.py:36
  21.0 10.3 %collective-permute-start.3 = (bf16[8,128,128]{2,1,0:T(8,128)(2,1)S(1)}, bf16[8,128,128]{2,1,0:T(8,128)(2,1)S(1)}, u32[]{:S(2)}, u32[]{:S(2)}) collective-permute-start(bf16[8,128,128]{2,1,0:T(8,128)(2,1)S(1)} %all_to_all.10.refs_0_), channel_id=1, source_target_pairs={{0,16},{8,24},{16,0},{24,8},{1,17},{9,25},{17,1},{25,9},{2,18},{10... | collective-permute-start | bytes 786440 | tf_op jit(solution)/shard_map/ppermute | solution.py:36
  21.8 13.1 %collective-permute-start.5 = (bf16[8,128,128]{2,1,0:T(8,128)(2,1)S(1)}, bf16[8,128,128]{2,1,0:T(8,128)(2,1)S(1)}, u32[]{:S(2)}, u32[]{:S(2)}) collective-permute-start(bf16[8,128,128]{2,1,0:T(8,128)(2,1)S(1)} %all_to_all.10.refs_0_), channel_id=1, source_target_pairs={{0,24},{8,0},{16,8},{24,16},{1,25},{9,1},{17,9},{25,17},{2,26},{10... | collective-permute-start | bytes 786440 | tf_op jit(solution)/shard_map/ppermute | solution.py:36
  23.7 21.6 %collective-permute-start = (bf16[8,128,128]{2,1,0:T(8,128)(2,1)S(1)}, bf16[8,128,128]{2,1,0:T(8,128)(2,1)S(1)}, u32[]{:S(2)}, u32[]{:S(2)}) collective-permute-start(bf16[8,128,128]{2,1,0:T(8,128)(2,1)S(1)} %all_to_all.10.refs_0_), channel_id=1, source_target_pairs={{0,4},{4,0},{1,5},{5,1},{2,6},{6,2},{3,7},{7,3},{8,12},{12,8},{9,1... | collective-permute-start | bytes 786440 | tf_op jit(solution)/shard_map/ppermute | solution.py:36
  27.0 18.3 %collective-permute-start.2 = (bf16[8,128,128]{2,1,0:T(8,128)(2,1)S(1)}, bf16[8,128,128]{2,1,0:T(8,128)(2,1)S(1)}, u32[]{:S(2)}, u32[]{:S(2)}) collective-permute-start(bf16[8,128,128]{2,1,0:T(8,128)(2,1)S(1)} %collective-permute-done.1.refs_2_), channel_id=1, source_target_pairs={{0,4},{4,0},{1,5},{5,1},{2,6},{6,2},{3,7},{7,3},{8,12},{12,8},{9,1... | collective-permute-start | bytes 786440 | tf_op jit(solution)/shard_map/ppermute | solution.py:36
  31.3 14.0 %collective-permute-start.4 = (bf16[8,128,128]{2,1,0:T(8,128)(2,1)S(1)}, bf16[8,128,128]{2,1,0:T(8,128)(2,1)S(1)}, u32[]{:S(2)}, u32[]{:S(2)}) collective-permute-start(bf16[8,128,128]{2,1,0:T(8,128)(2,1)S(1)} %collective-permute-done.3.refs_4_), channel_id=1, source_target_pairs={{0,4},{4,0},{1,5},{5,1},{2,6},{6,2},{3,7},{7,3},{8,12},{12,8},{9,1... | collective-permute-start | bytes 786440 | tf_op jit(solution)/shard_map/ppermute | solution.py:36
  34.9 10.4 %collective-permute-start.6 = (bf16[8,128,128]{2,1,0:T(8,128)(2,1)S(1)}, bf16[8,128,128]{2,1,0:T(8,128)(2,1)S(1)}, u32[]{:S(2)}, u32[]{:S(2)}) collective-permute-start(bf16[8,128,128]{2,1,0:T(8,128)(2,1)S(1)} %collective-permute-done.5.refs_6_), channel_id=1, source_target_pairs={{0,4},{4,0},{1,5},{5,1},{2,6},{6,2},{3,7},{7,3},{8,12},{12,8},{9,1... | collective-permute-start | bytes 786440 | tf_op jit(solution)/shard_map/ppermute | solution.py:36
  36.9 2.2 %copy-start = (bf16[1,1,128,128,128]{4,3,2,1,0:T(8,128)(2,1)S(1)}, bf16[1,1,128,128,128]{4,3,2,1,0:T(8,128)(2,1)}, u32[]{:S(2)}) copy-start(bf16[1,1,128,128,128]{4,3,2,1,0:T(8,128)(2,1)} %param.12) | copy-start | bytes 12582916
  39.1 0.7 copy-start.4
  39.7 0.7 copy-start.5
  45.3 7.6 %copy-start.1 = (bf16[128,128]{1,0:T(8,128)(2,1)S(1)}, bf16[128,128]{1,0:T(8,128)(2,1)}, u32[]{:S(2)}) copy-start(bf16[128,128]{1,0:T(8,128)(2,1)} %c0.1) | copy-start | bytes 98308
  45.3 16.2 %copy-start.2 = (bf16[128,128]{1,0:T(8,128)(2,1)S(1)}, bf16[128,128]{1,0:T(8,128)(2,1)}, u32[]{:S(2)}) copy-start(bf16[128,128]{1,0:T(8,128)(2,1)} %weight_ref.1) | copy-start | bytes 98308
  45.3 16.2 %copy-start.3 = (f32[128]{0:T(128)S(1)}, f32[128]{0:T(128)}, u32[]{:S(2)}) copy-start(f32[128]{0:T(128)} %param.10) | copy-start | bytes 1540
  47.7 13.8 %collective-permute-start.7 = (bf16[512,128]{1,0:T(8,128)(2,1)S(1)}, bf16[512,128]{1,0:T(8,128)(2,1)S(1)}, u32[]{:S(2)}, u32[]{:S(2)}) collective-permute-start(bf16[512,128]{1,0:T(8,128)(2,1)S(1)} %forward.1.p0), channel_id=1, source_target_pairs={{0,1},{1,2},{2,3},{3,0},{4,5},{5,6},{6,7},{7,4},{8,9},{9,10},{10,1... | collective-permute-start | bytes 393224 | tf_op jit(solution)/shard_map/ppermute | solution.py:36
  48.9 12.6 %collective-permute-start.8 = (bf16[512,128]{1,0:T(8,128)(2,1)S(1)}, bf16[512,128]{1,0:T(8,128)(2,1)S(1)}, u32[]{:S(2)}, u32[]{:S(2)}) collective-permute-start(bf16[512,128]{1,0:T(8,128)(2,1)S(1)} %forward.1.p0), channel_id=1, source_target_pairs={{0,2},{1,3},{2,0},{3,1},{4,6},{5,7},{6,4},{7,5},{8,10},{9,11},{10,... | collective-permute-start | bytes 393224 | tf_op jit(solution)/shard_map/ppermute | solution.py:36
  50.9 10.6 %collective-permute-start.9 = (bf16[512,128]{1,0:T(8,128)(2,1)S(1)}, bf16[512,128]{1,0:T(8,128)(2,1)S(1)}, u32[]{:S(2)}, u32[]{:S(2)}) collective-permute-start(bf16[512,128]{1,0:T(8,128)(2,1)S(1)} %forward.1.p0), channel_id=1, source_target_pairs={{0,3},{1,0},{2,1},{3,2},{4,7},{5,4},{6,5},{7,6},{8,11},{9,8},{10,9... | collective-permute-start | bytes 393224 | tf_op jit(solution)/shard_map/ppermute | solution.py:36
  52.9 5.8 %collective-permute-start.10 = (bf16[128,128]{1,0:T(8,128)(2,1)S(1)}, bf16[128,128]{1,0:T(8,128)(2,1)S(1)}, u32[]{:S(2)}, u32[]{:S(2)}) collective-permute-start(bf16[128,128]{1,0:T(8,128)(2,1)S(1)} %copy-done.1), channel_id=1, source_target_pairs={{0,1},{1,2},{2,3},{3,0},{4,5},{5,6},{6,7},{7,4},{8,9},{9,10},{10,1... | collective-permute-start | bytes 98312 | tf_op jit(solution)/shard_map/ppermute | solution.py:36
  52.9 5.8 %collective-permute-start.11 = (bf16[128,128]{1,0:T(8,128)(2,1)S(1)}, bf16[128,128]{1,0:T(8,128)(2,1)S(1)}, u32[]{:S(2)}, u32[]{:S(2)}) collective-permute-start(bf16[128,128]{1,0:T(8,128)(2,1)S(1)} %copy-done.1), channel_id=1, source_target_pairs={{0,2},{1,3},{2,0},{3,1},{4,6},{5,7},{6,4},{7,5},{8,10},{9,11},{10,... | collective-permute-start | bytes 98312 | tf_op jit(solution)/shard_map/ppermute | solution.py:36
  58.7 2.8 %collective-permute-start.12 = (bf16[128,128]{1,0:T(8,128)(2,1)S(1)}, bf16[128,128]{1,0:T(8,128)(2,1)S(1)}, u32[]{:S(2)}, u32[]{:S(2)}) collective-permute-start(bf16[128,128]{1,0:T(8,128)(2,1)S(1)} %copy-done.1), channel_id=1, source_target_pairs={{0,3},{1,0},{2,1},{3,2},{4,7},{5,4},{6,5},{7,6},{8,11},{9,8},{10,9... | collective-permute-start | bytes 98312 | tf_op jit(solution)/shard_map/ppermute | solution.py:36
  63.4 4.6 %collective-permute-start.19 = (bf16[8,128,128]{2,1,0:T(8,128)(2,1)S(1)}, bf16[8,128,128]{2,1,0:T(8,128)(2,1)S(1)}, u32[]{:S(2)}, u32[]{:S(2)}) collective-permute-start(bf16[8,128,128]{2,1,0:T(8,128)(2,1)S(1)} %get-tuple-element.30), channel_id=1, source_target_pairs={{0,4},{4,0},{1,5},{5,1},{2,6},{6,2},{3,7},{7,3},{8,12},{12,8},{9,1... | collective-permute-start | bytes 786440 | tf_op jit(solution)/shard_map/ppermute | solution.py:36
  65.5 4.3 %collective-permute-start.17 = (bf16[8,128,128]{2,1,0:T(8,128)(2,1)S(1)}, bf16[8,128,128]{2,1,0:T(8,128)(2,1)S(1)}, u32[]{:S(2)}, u32[]{:S(2)}) collective-permute-start(bf16[8,128,128]{2,1,0:T(8,128)(2,1)S(1)} %get-tuple-element.28), channel_id=1, source_target_pairs={{0,4},{4,0},{1,5},{5,1},{2,6},{6,2},{3,7},{7,3},{8,12},{12,8},{9,1... | collective-permute-start | bytes 786440 | tf_op jit(solution)/shard_map/ppermute | solution.py:36
  66.2 5.0 %collective-permute-start.15 = (bf16[8,128,128]{2,1,0:T(8,128)(2,1)S(1)}, bf16[8,128,128]{2,1,0:T(8,128)(2,1)S(1)}, u32[]{:S(2)}, u32[]{:S(2)}) collective-permute-start(bf16[8,128,128]{2,1,0:T(8,128)(2,1)S(1)} %get-tuple-element.26), channel_id=1, source_target_pairs={{0,4},{4,0},{1,5},{5,1},{2,6},{6,2},{3,7},{7,3},{8,12},{12,8},{9,1... | collective-permute-start | bytes 786440 | tf_op jit(solution)/shard_map/ppermute | solution.py:36
  66.8 1.2 %collective-permute-start.14 = (bf16[80,128]{1,0:T(8,128)(2,1)S(1)}, bf16[80,128]{1,0:T(8,128)(2,1)S(1)}, u32[]{:S(2)}, u32[]{:S(2)}) collective-permute-start(bf16[80,128]{1,0:T(8,128)(2,1)S(1)} %get-tuple-element.24), channel_id=1, source_target_pairs={{0,4},{4,0},{1,5},{5,1},{2,6},{6,2},{3,7},{7,3},{8,12},{12,8},{9,1... | collective-permute-start | bytes 61448 | tf_op jit(solution)/shard_map/ppermute | solution.py:36
  68.1 8.0 %collective-permute-start.20 = (bf16[1104,128]{1,0:T(8,128)(2,1)S(1)}, bf16[1104,128]{1,0:T(8,128)(2,1)S(1)}, u32[]{:S(2)}, u32[]{:S(2)}) collective-permute-start(bf16[1104,128]{1,0:T(8,128)(2,1)S(1)} %pair_sum.7), channel_id=1, source_target_pairs={{0,8},{8,16},{16,24},{24,0},{1,9},{9,17},{17,25},{25,1},{2,10},{10... | collective-permute-start | bytes 847880 | tf_op jit(solution)/shard_map/ppermute | solution.py:36
  69.8 9.3 %collective-permute-start.18 = (bf16[1104,128]{1,0:T(8,128)(2,1)S(1)}, bf16[1104,128]{1,0:T(8,128)(2,1)S(1)}, u32[]{:S(2)}, u32[]{:S(2)}) collective-permute-start(bf16[1104,128]{1,0:T(8,128)(2,1)S(1)} %pair_sum.6), channel_id=1, source_target_pairs={{0,16},{8,24},{16,0},{24,8},{1,17},{9,25},{17,1},{25,9},{2,18},{10... | collective-permute-start | bytes 847880 | tf_op jit(solution)/shard_map/ppermute | solution.py:36
  71.3 14.7 %collective-permute-start.16 = (bf16[1104,128]{1,0:T(8,128)(2,1)S(1)}, bf16[1104,128]{1,0:T(8,128)(2,1)S(1)}, u32[]{:S(2)}, u32[]{:S(2)}) collective-permute-start(bf16[1104,128]{1,0:T(8,128)(2,1)S(1)} %pair_sum.5), channel_id=1, source_target_pairs={{0,24},{8,0},{16,8},{24,16},{1,25},{9,1},{17,9},{25,17},{2,26},{10... | collective-permute-start | bytes 847880 | tf_op jit(solution)/shard_map/ppermute | solution.py:36
  72.3 2.2 %collective-permute-start.13 = (bf16[8,128,128]{2,1,0:T(8,128)(2,1)S(1)}, bf16[8,128,128]{2,1,0:T(8,128)(2,1)S(1)}, u32[]{:S(2)}, u32[]{:S(2)}) collective-permute-start(bf16[8,128,128]{2,1,0:T(8,128)(2,1)S(1)} %get-tuple-element.22), channel_id=1, source_target_pairs={{0,4},{4,0},{1,5},{5,1},{2,6},{6,2},{3,7},{7,3},{8,12},{12,8},{9,1... | collective-permute-start | bytes 786440 | tf_op jit(solution)/shard_map/ppermute | solution.py:36
  104.2 2.4 %collective-permute-start.21 = (f32[64,128]{1,0:T(8,128)S(1)}, f32[64,128]{1,0:T(8,128)S(1)}, u32[]{:S(2)}, u32[]{:S(2)}) collective-permute-start(f32[64,128]{1,0:T(8,128)S(1)} %get-tuple-element.32), channel_id=1, source_target_pairs={{0,4},{4,0},{1,5},{5,1},{2,6},{6,2},{3,7},{7,3},{8,12},{12,8},{9,1... | collective-permute-start | bytes 98312 | tf_op jit(solution)/shard_map/ppermute | solution.py:36

commit v2 on v1

v2 whole, which is shorter than its diff:
```python
import jax
import jax.numpy as jnp
from jax import lax
from jax.experimental import pallas as pl
from jax.experimental.pallas import tpu as pltpu
from jax.sharding import Mesh
from jax.sharding import PartitionSpec as P

Z, X, C, Q = 8, 4, 2, 4
T = 128
PANEL = Q * T
SLOTS = 128
PAY = T + 16
MSG = Z * T + PAY
BLK = T + PAY
F32 = jnp.float32
BF16 = jnp.bfloat16
ROW = ("z", "x", "core")
ALL = ("z", "x", "core", "rep")
SCALE = (Z * X * C * Q * T) ** -0.5

VMEM = pl.BlockSpec(memory_space=pltpu.VMEM)
SMEM = pl.BlockSpec(memory_space=pltpu.SMEM)


def params(mib):
    return pltpu.CompilerParams(vmem_limit_bytes=mib * 2**20)


def cost(flops, size):
    return pl.CostEstimate(flops=flops, bytes_accessed=size, transcendentals=0)


def shift(axis, size, by):
    return [(i, (i + by) % size) for i in range(size)]


def send(array, axis, size, by):
    return lax.ppermute(array, axis, shift(axis, size, by))


def densify_kernel(rows_ref, cols_ref, count_ref, me_ref, tiles_ref, dense_ref):
    def clear(p, carry):
        dense_ref[p] = jnp.zeros((PANEL, T), BF16)
        return carry

    lax.fori_loop(0, Z * X * C, clear, 0)
    x, core = me_ref[0], me_ref[1]

    def place(k, carry):
        col = cols_ref[k]
        z_col = col // (X * C)
        x_col = (col // C) % X
        core_col = col % C
        offset = (x - x_col + X) % X
        other = (core + core_col) % C
        position = (offset * C + other) * Z + z_col
        row = pl.multiple_of(rows_ref[k] * T, T)
        dense_ref[position, pl.ds(row, T), :] = tiles_ref[k]
        return carry

    lax.fori_loop(0, count_ref[0], place, 0)


def densify(rows, cols, count, me, tiles):
    return pl.pallas_call(
        densify_kernel,
        in_specs=[SMEM] * 4 + [VMEM],
        out_specs=VMEM,
        out_shape=jax.ShapeDtypeStruct((Z * X * C, PANEL, T), BF16),
        compiler_params=params(16),
        cost_estimate=cost(0, 12 * 2**20),
        name="densify",
    )(rows, cols, count, me, tiles)


def forward(dense, first, gathered, before=None, cotangent=None):
    last = before is not None
    count = len(gathered)

    def kernel(dense_ref, *refs):
        sources, out_ref, total = refs[:count], refs[-2], refs[-1]
        for n, source in enumerate(sources):
            panel = jnp.concatenate([dense_ref[(first + n) * Z + z] for z in range(Z)], axis=1)
            part = jnp.dot(panel, source[...].reshape(Z * T, T), preferred_element_type=F32)
            if n:
                part += total[...]
            elif last:
                part += refs[count][...]
            if n < count - 1:
                total[...] = part
            else:
                out_ref[:PANEL] = part.astype(out_ref.dtype)
        if last:
            out_ref[PANEL:] = refs[count + 1][...]

    extra = [before, cotangent] if last else []
    shape = jax.ShapeDtypeStruct((PANEL + T, T), BF16) if last else jax.ShapeDtypeStruct((PANEL, T), F32)
    return pl.pallas_call(
        kernel,
        in_specs=[VMEM] * (1 + count + len(extra)),
        out_specs=VMEM,
        out_shape=shape,
        scratch_shapes=[pltpu.VMEM((PANEL, T), F32)],
        compiler_params=params(16),
        cost_estimate=cost(2 * PANEL * T * T * Z * count, 2**20 * count),
        name="forward",
    )(dense, *gathered, *extra)


def tie(block, token):
    def kernel(block_ref, token_ref, out_ref):
        del block_ref, token_ref, out_ref

    return pl.pallas_call(
        kernel,
        in_specs=[VMEM] * 2,
        out_specs=VMEM,
        out_shape=jax.ShapeDtypeStruct(block.shape, block.dtype),
        input_output_aliases={0: 0},
        compiler_params=params(16),
        name="tie",
    )(block, token)


def split(value):
    high = value.astype(BF16)
    low = (value - high.astype(F32)).astype(BF16)
    return high, low


def pack_bias(ref, start, value):
    high, low = split(value)
    rows = lax.broadcasted_iota(jnp.int32, (16, T), 0)
    packed = jnp.where(rows == 0, high.astype(F32), jnp.where(rows == 1, low.astype(F32), 0.0))
    ref[start:start + 16, :] = packed.astype(BF16)


def middle_kernel(me_ref, p0, p1, p2, p3, weight_ref, bias_ref, out_ref, back_ref, pay_ref, pre, cot):
    rep = me_ref[2]
    for n, source in enumerate((p0, p1, p2, p3)):
        cot[(rep - n + Q) % Q] = source[PANEL:]
    get = lambda ref: ref[:PANEL].astype(F32)
    total = (get(p0) + get(p2)) + (get(p1) + get(p3))
    aggregated = total.astype(BF16)
    preact = jnp.dot(aggregated, weight_ref[...], preferred_element_type=F32) + bias_ref[...]
    pre[...] = preact.reshape(Q, T, T)
    sig = jax.nn.sigmoid(preact)
    cotangent = cot[...].reshape(PANEL, T).astype(F32)
    grad_pre = (cotangent * sig * (1.0 + preact * (1.0 - sig))).astype(BF16)
    own = pre[rep]
    out_ref[...] = (own * jax.nn.sigmoid(own)).astype(BF16)
    back = lax.dot_general(weight_ref[...], grad_pre, (((1,), (1,)), ((), ())), preferred_element_type=F32)
    back_ref[...] = back.astype(BF16)
    terms = lax.dot_general(aggregated, grad_pre, (((0,), (0,)), ((), ())), preferred_element_type=F32)
    bias_sum = jnp.sum(grad_pre.astype(F32), axis=0, keepdims=True)
    pay_ref[:T] = terms.astype(BF16)
    pack_bias(pay_ref, T, bias_sum)


def middle(me, partials, weight, bias):
    return pl.pallas_call(
        middle_kernel,
        in_specs=[SMEM] + [VMEM] * 6,
        out_specs=[VMEM] * 3,
        out_shape=[
            jax.ShapeDtypeStruct((T, T), BF16),
            jax.ShapeDtypeStruct((T, PANEL), BF16),
            jax.ShapeDtypeStruct((PAY, T), BF16),
        ],
        scratch_shapes=[pltpu.VMEM((Q, T, T), F32), pltpu.VMEM((Q, T, T), BF16)],
        compiler_params=params(16),
        cost_estimate=cost(6 * PANEL * T * T, 2**20),
        name="middle",
    )(me, *partials, weight, bias)


def backward(dense, back, chunk, pay=None):
    carries = pay is not None

    def kernel(dense_ref, back_ref, *refs):
        mine_ref, theirs_ref = refs[-2:]
        for n, ref in enumerate((mine_ref, theirs_ref)):
            for z in range(0, Z, 2):
                at = (chunk * C + n) * Z + z
                pair = jnp.concatenate([dense_ref[at], dense_ref[at + 1]], axis=1)
                part = jnp.dot(back_ref[...], pair, preferred_element_type=F32).astype(BF16)
                ref[z * T:z * T + T] = part[:, :T]
                ref[z * T + T:z * T + 2 * T] = part[:, T:]
        if carries:
            mine_ref[Z * T:] = refs[0][...]
            theirs_ref[Z * T:] = refs[0][...]

    rows = MSG if carries else Z * T
    extra = [pay] if carries else []
    return pl.pallas_call(
        kernel,
        in_specs=[VMEM] * (2 + len(extra)),
        out_specs=[VMEM] * 2,
        out_shape=[jax.ShapeDtypeStruct((rows, T), BF16)] * 2,
        compiler_params=params(16),
        cost_estimate=cost(2 * PANEL * T * T * Z * C, 2**21),
        name="backward",
    )(dense, back, *extra)


def bias_of(ref, start):
    pair = ref[start:start + 16, :].astype(F32)
    return pair[0:1] + pair[1:2]


def pair_sum(mine, theirs, pay=None):
    carried = pay is None

    def kernel(mine_ref, theirs_ref, *refs):
        out_ref = refs[-1]
        rows = Z * T + (T if carried else 0)
        total = mine_ref[:rows].astype(F32) + theirs_ref[:rows].astype(F32)
        out_ref[:rows] = total.astype(BF16)
        if carried:
            pack_bias(out_ref, rows, bias_of(mine_ref, rows) + bias_of(theirs_ref, rows))
        else:
            out_ref[rows:] = refs[0][rows:]

    extra = [] if carried else [pay]
    return pl.pallas_call(
        kernel,
        in_specs=[VMEM] * (2 + len(extra)),
        out_specs=VMEM,
        out_shape=jax.ShapeDtypeStruct((MSG, T), BF16),
        compiler_params=params(16),
        cost_estimate=cost(0, 2**20),
        name="pair_sum",
    )(mine, theirs, *extra)


def line_sum(s0, s1, s2, s3):
    def kernel(r0, r1, r2, r3, out_ref):
        def add(a, b):
            get = lambda r: r[a:b].astype(F32)
            return (get(r0) + get(r2)) + (get(r1) + get(r3))

        terms = add(Z * T, Z * T + T).astype(BF16)
        at = Z * T + T
        bias = (bias_of(r0, at) + bias_of(r2, at)) + (bias_of(r1, at) + bias_of(r3, at))
        for z in range(Z):
            out_ref[z, :T] = add(z * T, z * T + T).astype(BF16)
            out_ref[z, T:2 * T] = terms
            pack_bias(out_ref.at[z], 2 * T, bias)

    return pl.pallas_call(
        kernel,
        in_specs=[VMEM] * 4,
        out_specs=VMEM,
        out_shape=jax.ShapeDtypeStruct((Z, BLK, T), BF16),
        compiler_params=params(16),
        cost_estimate=cost(0, 2**20),
        name="line_sum",
    )(s0, s1, s2, s3)


def finish(received):
    def kernel(in_ref, grad_ref, weight_ref, bias_ref):
        total = in_ref[0, :2 * T].astype(F32)
        bias = bias_of(in_ref.at[0], 2 * T)
        for z in range(1, Z):
            total += in_ref[z, :2 * T].astype(F32)
            bias += bias_of(in_ref.at[z], 2 * T)
        grad_ref[...] = total[:T].T.astype(BF16)
        weight_ref[...] = total[T:] * SCALE
        bias_ref[...] = bias * SCALE

    return pl.pallas_call(
        kernel,
        in_specs=[VMEM],
        out_specs=[VMEM] * 3,
        out_shape=[
            jax.ShapeDtypeStruct((T, T), BF16),
            jax.ShapeDtypeStruct((T, T), F32),
            jax.ShapeDtypeStruct((1, T), F32),
        ],
        compiler_params=params(16),
        name="finish",
    )(received)


def body(features, weight, bias_terms, cotangent, tile_values, tile_rows, tile_cols, tile_count):
    x, core, rep = lax.axis_index("x"), lax.axis_index("core"), lax.axis_index("rep")
    me = jnp.stack([x, core, rep]).astype(jnp.int32)
    spread = jnp.broadcast_to(features, (Z, T, T))
    line = lax.all_to_all(spread, "z", 0, 0, tiled=True)
    dense = densify(tile_rows[0, 0], tile_cols[0, 0], tile_count[0], me, tile_values[0, 0])
    near = [line, send(line, "core", C, 1)]
    begun = forward(dense, 0, near)
    far = []
    for n in range(1, X):
        block = send(line, "x", X, n)
        if n > 1:
            block = tie(block, begun)
        far += [block, send(block, "core", C, 1)]
    partial = forward(dense, C, far, begun, cotangent)

    partials = [partial] + [send(partial, "rep", Q, n) for n in range(1, Q)]
    output, back, pay = middle(me, partials, weight, bias_terms.reshape(1, T))

    sums = {}
    for n in (1, 2, 3, 0):
        mine, theirs = backward(dense, back, n, pay if n == 1 else None)
        theirs = send(theirs, "core", C, 1)
        total = pair_sum(mine, theirs, None if n == 1 else first)
        if n == 1:
            first = total
        sums[n] = send(total, "x", X, -n) if n else total
    blocks = line_sum(sums[0], sums[1], sums[2], sums[3])
    received = lax.all_to_all(blocks, "z", 0, 0, tiled=True)
    grad_input, weight_grad, bias_grad = finish(received)
    return output, grad_input, weight_grad, bias_grad.reshape(T)


def solution(mesh):
    fine = Mesh(mesh.devices.reshape(Z, X, C, Q), ALL)
    return jax.shard_map(
        body,
        mesh=fine,
        in_specs=(
            P(ALL, None),
            P(),
            P(),
            P(ALL, None),
            P(ROW, "rep", None, None, None),
            P(ROW, "rep", None),
            P(ROW, "rep", None),
            P(ROW, "rep"),
        ),
        out_specs=(P(ALL, None), P(ALL, None), P(), P()),
        check_vma=False,
    )
```

time: 107 us -> 99.5 us (0.930); the launches traced: 107 us -> 98.4 us
  starting transfers between devices: 30.7 us -> 21 us
  blocking collectives: 35.6 us -> 39.1 us
  waiting for transfers between devices: 22.8 us -> 20.8 us
    ppermute x22 -> x17, starting transfers between devices: 30.7 us -> 21 us  [send(): return lax.ppermute(array, axis, shift(axis, size, by))]
    all_to_all x1, blocking collectives: 17.2 us -> 20.7 us  [body(): received = lax.all_to_all(blocks, 'z', 0, 0, tiled=True)]
    ppermute x22 -> x17, waiting for transfers between devices: 22.8 us -> 20.8 us  [send(): return lax.ppermute(array, axis, shift(axis, size, by))]
    pallas_call x11 -> x14, Pallas kernels: 10.8 us -> 10.8 us  [the longest x1 4.65 us: densify(): pl.pallas_call(densify_kernel, in_specs=[SMEM] * 4 + [VMEM], out_specs=VM...]
  transfers between devices with their start and end apart: 22 -> 17, of which waited for: 9 -> 10; matrix products, arithmetic and copies ran while one was open for 0% -> 0% of each run, Pallas kernels for 6% -> 7%
where the time goes in v2:
time: 99.5 us; the launch traced here: 98.4 us
  blocking collectives  39.1 us (39%)
  starting transfers between devices  21 us (21%)
  waiting for transfers between devices  20.8 us (21%)
  Pallas kernels  11.7 us (12%)
  local copies, waits for them, and re-layouts  4.31 us (4%)
  between operations  1.42 us (1%)
    ppermute x17, starting transfers between devices, send(): return lax.ppermute(array, axis, shift(axis, size, by))  21 us
    ppermute x17, waiting for transfers between devices, send(): return lax.ppermute(array, axis, shift(axis, size, by))  20.8 us
    all_to_all x1, blocking collectives, body(): received = lax.all_to_all(blocks, 'z', 0, 0, tiled=True)  20.7 us
    all_to_all x1, blocking collectives, body(): line = lax.all_to_all(spread, 'z', 0, 0, tiled=True)  18.4 us
    pallas_call x1, Pallas kernels, densify(): pl.pallas_call(densify_kernel, in_specs=[SMEM] * 4 + [VMEM], out_specs=VM...  4.65 us
    unnamed x12, local copies, waits for them, and re-layouts  3.52 us
    pallas_call x2, Pallas kernels, forward(): pl.pallas_call(kernel, in_specs=[VMEM] * (1 + count + len(extra)), out_sp...  2.49 us
  transfers between devices with their start and end apart: 17, of which 10 were waited for; matrix products, arithmetic and copies ran while one was open for 0% of the time, Pallas kernels for 7%

profile of v2, /device:TPU:3, one launch (start us, length us, event | category | flops | bytes accessed | tf_op | source)
XLA Modules:
  0.0 98.4 jit_solution(7512660352318770591)
XLA Ops:
  0.6 0.8 broadcast_in_dim.3
  1.4 18.4 %all_to_all.10.refs_0_ = bf16[8,128,128]{2,1,0:T(8,128)(2,1)S(1)} all-to-all(bf16[8,128,128]{2,1,0:T(8,128)(2,1)S(1)} %broadcast_in_dim.3), channel_id=1, replica_groups=mesh['z'=8,'x'=4,'core'=2,'rep'=4] {'z'}, dimensions={0} | all-to-all | bytes 524288 | tf_op jit(solution)/shard_map/all_to_all | solution.py:291
  19.8 2.5 %collective-permute-start.3 = (bf16[8,128,128]{2,1,0:T(8,128)(2,1)S(1)}, bf16[8,128,128]{2,1,0:T(8,128)(2,1)S(1)}, u32[]{:S(2)}, u32[]{:S(2)}) collective-permute-start(bf16[8,128,128]{2,1,0:T(8,128)(2,1)S(1)} %all_to_all.10.refs_0_), channel_id=1, source_target_pairs={{0,4},{4,0},{1,5},{5,1},{2,6},{6,2},{3,7},{7,3},{8,12},{12,8},{9,1... | collective-permute-start | bytes 786440 | tf_op jit(solution)/shard_map/ppermute | solution.py:39
  22.2 0.3 collective-permute-start.5
  22.5 2.1 %collective-permute-start.2 = (bf16[8,128,128]{2,1,0:T(8,128)(2,1)S(1)}, bf16[8,128,128]{2,1,0:T(8,128)(2,1)S(1)}, u32[]{:S(2)}, u32[]{:S(2)}) collective-permute-start(bf16[8,128,128]{2,1,0:T(8,128)(2,1)S(1)} %all_to_all.10.refs_0_), channel_id=1, source_target_pairs={{0,16},{8,24},{16,0},{24,8},{1,17},{9,25},{17,1},{25,9},{2,18},{10... | collective-permute-start | bytes 786440 | tf_op jit(solution)/shard_map/ppermute | solution.py:39
  24.6 1.5 %collective-permute-start = (bf16[8,128,128]{2,1,0:T(8,128)(2,1)S(1)}, bf16[8,128,128]{2,1,0:T(8,128)(2,1)S(1)}, u32[]{:S(2)}, u32[]{:S(2)}) collective-permute-start(bf16[8,128,128]{2,1,0:T(8,128)(2,1)S(1)} %all_to_all.10.refs_0_), channel_id=1, source_target_pairs={{0,8},{8,16},{16,24},{24,0},{1,9},{9,17},{17,25},{25,1},{2,10},{10... | collective-permute-start | bytes 786440 | tf_op jit(solution)/shard_map/ppermute | solution.py:39
  26.8 0.1 pad_add_fusion.me_ref
  26.9 2.2 %copy-done = bf16[1,1,128,128,128]{4,3,2,1,0:T(8,128)(2,1)S(1)} copy-done((bf16[1,1,128,128,128]{4,3,2,1,0:T(8,128)(2,1)S(1)}, bf16[1,1,128,128,128]{4,3,2,1,0:T(8,128)(2,1)}, u32[]{:S(2)}) %copy-start) | copy-done | bytes 4194328
  29.1 0.7 copy-done.4
  29.7 0.7 copy-done.5
  30.4 4.7 %densify.1.dense_ref = bf16[64,512,128]{2,1,0:T(8,128)(2,1)S(1)} custom-call(s32[128]{0:T(128)S(1)} %bitcast.12, s32[128]{0:T(128)S(1)} %bitcast.13, s32[1]{0:T(128)} %bitcast.9.count_ref, s32[3]{0:T(128)S(1)} %pad_add_fusion.me_ref, bf16[128,128,128]{2,1,0:T(8,128)(2,1)S(1)} %bitcast.10), custom_call_target="tpu_custom_call" | custom-call | bytes 12582912 | tf_op jit(solution)/shard_map/densify/pallas_call | solution.py:66
  35.0 0.0 copy-start.1
  35.1 0.7 forward.2.token_ref.refs_6_
  35.8 0.5 collective-permute-start.6
  36.3 0.4 collective-permute-done.2.block_ref
  36.7 0.8 collective-permute-start.4
  37.5 0.9 collective-permute-start.1
  38.4 0.3 collective-permute-done.4.refs_3_
  38.7 0.9 collective-permute-done.1.refs_1_
  39.6 1.8 %forward.3.p0 = bf16[640,128]{1,0:T(8,128)(2,1)S(1)} custom-call(bf16[64,512,128]{2,1,0:T(8,128)(2,1)S(1)} %densify.1.dense_ref, bf16[8,128,128]{2,1,0:T(8,128)(2,1)S(1)} %collective-permute-done.refs_0_, bf16[8,128,128]{2,1,0:T(8,128)(2,1)S(1)} %collective-permute-done.1.refs_1_, bf16[8,128,128]{2,1,0:T(8,128)(2,1)S(1)} %tie.2.refs_2_, ...), custom_call_target="tpu_custom_call" | custom-call | flops 805306368 | bytes 6291456 | tf_op jit(solution)/shard_map/forward/pallas_call | solution.py:99
  41.4 1.4 %collective-permute-start.7 = (bf16[640,128]{1,0:T(8,128)(2,1)S(1)}, bf16[640,128]{1,0:T(8,128)(2,1)S(1)}, u32[]{:S(2)}, u32[]{:S(2)}) collective-permute-start(bf16[640,128]{1,0:T(8,128)(2,1)S(1)} %forward.3.p0), channel_id=1, source_target_pairs={{0,1},{1,2},{2,3},{3,0},{4,5},{5,6},{6,7},{7,4},{8,9},{9,10},{10,1... | collective-permute-start | bytes 491528 | tf_op jit(solution)/shard_map/ppermute | solution.py:39
  42.7 2.6 %collective-permute-start.8 = (bf16[640,128]{1,0:T(8,128)(2,1)S(1)}, bf16[640,128]{1,0:T(8,128)(2,1)S(1)}, u32[]{:S(2)}, u32[]{:S(2)}) collective-permute-start(bf16[640,128]{1,0:T(8,128)(2,1)S(1)} %forward.3.p0), channel_id=1, source_target_pairs={{0,2},{1,3},{2,0},{3,1},{4,6},{5,7},{6,4},{7,5},{8,10},{9,11},{10,... | collective-permute-start | bytes 491528 | tf_op jit(solution)/shard_map/ppermute | solution.py:39
  45.4 1.1 %collective-permute-start.9 = (bf16[640,128]{1,0:T(8,128)(2,1)S(1)}, bf16[640,128]{1,0:T(8,128)(2,1)S(1)}, u32[]{:S(2)}, u32[]{:S(2)}) collective-permute-start(bf16[640,128]{1,0:T(8,128)(2,1)S(1)} %forward.3.p0), channel_id=1, source_target_pairs={{0,3},{1,0},{2,1},{3,2},{4,7},{5,4},{6,5},{7,6},{8,11},{9,8},{10,9... | collective-permute-start | bytes 491528 | tf_op jit(solution)/shard_map/ppermute | solution.py:39
  46.4 1.8 %collective-permute-done.7.p1 = bf16[640,128]{1,0:T(8,128)(2,1)S(1)} collective-permute-done((bf16[640,128]{1,0:T(8,128)(2,1)S(1)}, bf16[640,128]{1,0:T(8,128)(2,1)S(1)}, u32[]{:S(2)}, u32[]{:S(2)}) %collective-permute-start.7) | collective-permute-done | bytes 163872 | tf_op jit(solution)/shard_map/ppermute | solution.py:39
  48.2 4.6 %collective-permute-done.8.p2 = bf16[640,128]{1,0:T(8,128)(2,1)S(1)} collective-permute-done((bf16[640,128]{1,0:T(8,128)(2,1)S(1)}, bf16[640,128]{1,0:T(8,128)(2,1)S(1)}, u32[]{:S(2)}, u32[]{:S(2)}) %collective-permute-start.8) | collective-permute-done | bytes 163872 | tf_op jit(solution)/shard_map/ppermute | solution.py:39
  52.8 1.4 %middle.1 = (bf16[128,128]{1,0:T(8,128)(2,1)}, bf16[128,512]{1,0:T(8,128)(2,1)S(1)}, bf16[144,128]{1,0:T(8,128)(2,1)S(1)}) custom-call(s32[3]{0:T(128)S(1)} %pad_add_fusion.me_ref, bf16[640,128]{1,0:T(8,128)(2,1)S(1)} %forward.3.p0, bf16[640,128]{1,0:T(8,128)(2,1)S(1)} %collective-permute-done.7.p1, bf16[640,128]{1,0:T(8,128)(2,1)S(1)} %collective-permute-done.8.p2, ...), custom_call_target="tpu_custom_call" | custom-call | flops 50331648 | bytes 1048576 | tf_op jit(solution)/shard_map/middle/pallas_call | solution.py:162
  54.3 0.5 backward.5
  54.7 1.3 %collective-permute-start.11 = (bf16[1168,128]{1,0:T(8,128)(2,1)S(1)}, bf16[1168,128]{1,0:T(8,128)(2,1)S(1)}, u32[]{:S(2)}, u32[]{:S(2)}) collective-permute-start(bf16[1168,128]{1,0:T(8,128)(2,1)S(1)} %get-tuple-element.24), channel_id=1, source_target_pairs={{0,4},{4,0},{1,5},{5,1},{2,6},{6,2},{3,7},{7,3},{8,12},{12,8},{9,1... | collective-permute-start | bytes 897032 | tf_op jit(solution)/shard_map/ppermute | solution.py:39
  56.0 0.5 backward.7
  56.5 0.1 collective-permute-start.15
  56.6 0.5 backward.6
  57.1 0.6 collective-permute-start.13
  57.7 0.1 pair_sum.4.refs_0_
  57.8 0.4 collective-permute-done.15.theirs_ref
  58.1 0.1 pair_sum.7
  58.2 1.4 %collective-permute-start.16 = (bf16[1168,128]{1,0:T(8,128)(2,1)S(1)}, bf16[1168,128]{1,0:T(8,128)(2,1)S(1)}, u32[]{:S(2)}, u32[]{:S(2)}) collective-permute-start(bf16[1168,128]{1,0:T(8,128)(2,1)S(1)} %pair_sum.7), channel_id=1, source_target_pairs={{0,8},{8,16},{16,24},{24,0},{1,9},{9,17},{17,25},{25,1},{2,10},{10... | collective-permute-start | bytes 897032 | tf_op jit(solution)/shard_map/ppermute | solution.py:39
  59.6 0.1 pair_sum.6
  59.7 3.1 %collective-permute-start.14 = (bf16[1168,128]{1,0:T(8,128)(2,1)S(1)}, bf16[1168,128]{1,0:T(8,128)(2,1)S(1)}, u32[]{:S(2)}, u32[]{:S(2)}) collective-permute-start(bf16[1168,128]{1,0:T(8,128)(2,1)S(1)} %pair_sum.6), channel_id=1, source_target_pairs={{0,16},{8,24},{16,0},{24,8},{1,17},{9,25},{17,1},{25,9},{2,18},{10... | collective-permute-start | bytes 897032 | tf_op jit(solution)/shard_map/ppermute | solution.py:39
  62.8 0.5 backward.4
  63.3 0.9 collective-permute-start.10
  64.2 1.2 %collective-permute-done.10.theirs_ref = bf16[1024,128]{1,0:T(8,128)(2,1)S(1)} collective-permute-done((bf16[1024,128]{1,0:T(8,128)(2,1)S(1)}, bf16[1024,128]{1,0:T(8,128)(2,1)S(1)}, u32[]{:S(2)}, u32[]{:S(2)}) %collective-permute-start.10) | collective-permute-done | bytes 262176 | tf_op jit(solution)/shard_map/ppermute | solution.py:39
  65.4 0.1 pair_sum.5.r0
  65.5 2.7 %collective-permute-done.16.r3 = bf16[1168,128]{1,0:T(8,128)(2,1)S(1)} collective-permute-done((bf16[1168,128]{1,0:T(8,128)(2,1)S(1)}, bf16[1168,128]{1,0:T(8,128)(2,1)S(1)}, u32[]{:S(2)}, u32[]{:S(2)}) %collective-permute-start.16) | collective-permute-done | bytes 299040 | tf_op jit(solution)/shard_map/ppermute | solution.py:39
  68.2 1.5 %collective-permute-done.14.r2 = bf16[1168,128]{1,0:T(8,128)(2,1)S(1)} collective-permute-done((bf16[1168,128]{1,0:T(8,128)(2,1)S(1)}, bf16[1168,128]{1,0:T(8,128)(2,1)S(1)}, u32[]{:S(2)}, u32[]{:S(2)}) %collective-permute-start.14) | collective-permute-done | bytes 299040 | tf_op jit(solution)/shard_map/ppermute | solution.py:39
  69.8 7.0 %collective-permute-done.12.r1 = bf16[1168,128]{1,0:T(8,128)(2,1)S(1)} collective-permute-done((bf16[1168,128]{1,0:T(8,128)(2,1)S(1)}, bf16[1168,128]{1,0:T(8,128)(2,1)S(1)}, u32[]{:S(2)}, u32[]{:S(2)}) %collective-permute-start.12) | collective-permute-done | bytes 299040 | tf_op jit(solution)/shard_map/ppermute | solution.py:39
  76.8 0.2 line_sum.1
  77.0 20.7 %all_to_all.11.in_ref = bf16[8,272,128]{2,1,0:T(8,128)(2,1)S(1)} all-to-all(bf16[8,272,128]{2,1,0:T(8,128)(2,1)S(1)} %line_sum.1), channel_id=1, replica_groups=mesh['z'=8,'x'=4,'core'=2,'rep'=4] {'z'}, dimensions={0} | all-to-all | bytes 1114112 | tf_op jit(solution)/shard_map/all_to_all | solution.py:315
  97.7 0.7 finish.1
  (18 shorter events, 0.0 us)
Async XLA Ops:
  19.8 15.3 %collective-permute-start.3 = (bf16[8,128,128]{2,1,0:T(8,128)(2,1)S(1)}, bf16[8,128,128]{2,1,0:T(8,128)(2,1)S(1)}, u32[]{:S(2)}, u32[]{:S(2)}) collective-permute-start(bf16[8,128,128]{2,1,0:T(8,128)(2,1)S(1)} %all_to_all.10.refs_0_), channel_id=1, source_target_pairs={{0,4},{4,0},{1,5},{5,1},{2,6},{6,2},{3,7},{7,3},{8,12},{12,8},{9,1... | collective-permute-start | bytes 786440 | tf_op jit(solution)/shard_map/ppermute | solution.py:39
  22.2 13.6 %collective-permute-start.5 = (bf16[8,128,128]{2,1,0:T(8,128)(2,1)S(1)}, bf16[8,128,128]{2,1,0:T(8,128)(2,1)S(1)}, u32[]{:S(2)}, u32[]{:S(2)}) collective-permute-start(bf16[8,128,128]{2,1,0:T(8,128)(2,1)S(1)} %all_to_all.10.refs_0_), channel_id=1, source_target_pairs={{0,24},{8,0},{16,8},{24,16},{1,25},{9,1},{17,9},{25,17},{2,26},{10... | collective-permute-start | bytes 786440 | tf_op jit(solution)/shard_map/ppermute | solution.py:39
  22.5 14.2 %collective-permute-start.2 = (bf16[8,128,128]{2,1,0:T(8,128)(2,1)S(1)}, bf16[8,128,128]{2,1,0:T(8,128)(2,1)S(1)}, u32[]{:S(2)}, u32[]{:S(2)}) collective-permute-start(bf16[8,128,128]{2,1,0:T(8,128)(2,1)S(1)} %all_to_all.10.refs_0_), channel_id=1, source_target_pairs={{0,16},{8,24},{16,0},{24,8},{1,17},{9,25},{17,1},{25,9},{2,18},{10... | collective-permute-start | bytes 786440 | tf_op jit(solution)/shard_map/ppermute | solution.py:39
  24.6 12.9 %collective-permute-start = (bf16[8,128,128]{2,1,0:T(8,128)(2,1)S(1)}, bf16[8,128,128]{2,1,0:T(8,128)(2,1)S(1)}, u32[]{:S(2)}, u32[]{:S(2)}) collective-permute-start(bf16[8,128,128]{2,1,0:T(8,128)(2,1)S(1)} %all_to_all.10.refs_0_), channel_id=1, source_target_pairs={{0,8},{8,16},{16,24},{24,0},{1,9},{9,17},{17,25},{25,1},{2,10},{10... | collective-permute-start | bytes 786440 | tf_op jit(solution)/shard_map/ppermute | solution.py:39
  26.9 2.2 %copy-start = (bf16[1,1,128,128,128]{4,3,2,1,0:T(8,128)(2,1)S(1)}, bf16[1,1,128,128,128]{4,3,2,1,0:T(8,128)(2,1)}, u32[]{:S(2)}) copy-start(bf16[1,1,128,128,128]{4,3,2,1,0:T(8,128)(2,1)} %param.12) | copy-start | bytes 12582916
  29.1 0.7 copy-start.4
  29.7 0.7 copy-start.5
  35.0 4.5 %copy-start.1 = (bf16[128,128]{1,0:T(8,128)(2,1)S(1)}, bf16[128,128]{1,0:T(8,128)(2,1)}, u32[]{:S(2)}) copy-start(bf16[128,128]{1,0:T(8,128)(2,1)} %refs_7_.1) | copy-start | bytes 98308
  35.1 17.8 %copy-start.2 = (bf16[128,128]{1,0:T(8,128)(2,1)S(1)}, bf16[128,128]{1,0:T(8,128)(2,1)}, u32[]{:S(2)}) copy-start(bf16[128,128]{1,0:T(8,128)(2,1)} %weight_ref.1) | copy-start | bytes 98308
  35.1 17.8 %copy-start.3 = (f32[128]{0:T(128)S(1)}, f32[128]{0:T(128)}, u32[]{:S(2)}) copy-start(f32[128]{0:T(128)} %param.10) | copy-start | bytes 1540
  35.8 2.6 %collective-permute-start.6 = (bf16[8,128,128]{2,1,0:T(8,128)(2,1)S(1)}, bf16[8,128,128]{2,1,0:T(8,128)(2,1)S(1)}, u32[]{:S(2)}, u32[]{:S(2)}) collective-permute-start(bf16[8,128,128]{2,1,0:T(8,128)(2,1)S(1)} %tie.3.refs_4_), channel_id=1, source_target_pairs={{0,4},{4,0},{1,5},{5,1},{2,6},{6,2},{3,7},{7,3},{8,12},{12,8},{9,1... | collective-permute-start | bytes 786440 | tf_op jit(solution)/shard_map/ppermute | solution.py:39
  36.7 1.9 %collective-permute-start.4 = (bf16[8,128,128]{2,1,0:T(8,128)(2,1)S(1)}, bf16[8,128,128]{2,1,0:T(8,128)(2,1)S(1)}, u32[]{:S(2)}, u32[]{:S(2)}) collective-permute-start(bf16[8,128,128]{2,1,0:T(8,128)(2,1)S(1)} %tie.2.refs_2_), channel_id=1, source_target_pairs={{0,4},{4,0},{1,5},{5,1},{2,6},{6,2},{3,7},{7,3},{8,12},{12,8},{9,1... | collective-permute-start | bytes 786440 | tf_op jit(solution)/shard_map/ppermute | solution.py:39
  37.5 2.1 %collective-permute-start.1 = (bf16[8,128,128]{2,1,0:T(8,128)(2,1)S(1)}, bf16[8,128,128]{2,1,0:T(8,128)(2,1)S(1)}, u32[]{:S(2)}, u32[]{:S(2)}) collective-permute-start(bf16[8,128,128]{2,1,0:T(8,128)(2,1)S(1)} %collective-permute-done.refs_0_), channel_id=1, source_target_pairs={{0,4},{4,0},{1,5},{5,1},{2,6},{6,2},{3,7},{7,3},{8,12},{12,8},{9,1... | collective-permute-start | bytes 786440 | tf_op jit(solution)/shard_map/ppermute | solution.py:39
  41.4 6.8 %collective-permute-start.7 = (bf16[640,128]{1,0:T(8,128)(2,1)S(1)}, bf16[640,128]{1,0:T(8,128)(2,1)S(1)}, u32[]{:S(2)}, u32[]{:S(2)}) collective-permute-start(bf16[640,128]{1,0:T(8,128)(2,1)S(1)} %forward.3.p0), channel_id=1, source_target_pairs={{0,1},{1,2},{2,3},{3,0},{4,5},{5,6},{6,7},{7,4},{8,9},{9,10},{10,1... | collective-permute-start | bytes 491528 | tf_op jit(solution)/shard_map/ppermute | solution.py:39
  42.7 10.1 %collective-permute-start.8 = (bf16[640,128]{1,0:T(8,128)(2,1)S(1)}, bf16[640,128]{1,0:T(8,128)(2,1)S(1)}, u32[]{:S(2)}, u32[]{:S(2)}) collective-permute-start(bf16[640,128]{1,0:T(8,128)(2,1)S(1)} %forward.3.p0), channel_id=1, source_target_pairs={{0,2},{1,3},{2,0},{3,1},{4,6},{5,7},{6,4},{7,5},{8,10},{9,11},{10,... | collective-permute-start | bytes 491528 | tf_op jit(solution)/shard_map/ppermute | solution.py:39
  45.4 7.5 %collective-permute-start.9 = (bf16[640,128]{1,0:T(8,128)(2,1)S(1)}, bf16[640,128]{1,0:T(8,128)(2,1)S(1)}, u32[]{:S(2)}, u32[]{:S(2)}) collective-permute-start(bf16[640,128]{1,0:T(8,128)(2,1)S(1)} %forward.3.p0), channel_id=1, source_target_pairs={{0,3},{1,0},{2,1},{3,2},{4,7},{5,4},{6,5},{7,6},{8,11},{9,8},{10,9... | collective-permute-start | bytes 491528 | tf_op jit(solution)/shard_map/ppermute | solution.py:39
  54.7 2.9 %collective-permute-start.11 = (bf16[1168,128]{1,0:T(8,128)(2,1)S(1)}, bf16[1168,128]{1,0:T(8,128)(2,1)S(1)}, u32[]{:S(2)}, u32[]{:S(2)}) collective-permute-start(bf16[1168,128]{1,0:T(8,128)(2,1)S(1)} %get-tuple-element.24), channel_id=1, source_target_pairs={{0,4},{4,0},{1,5},{5,1},{2,6},{6,2},{3,7},{7,3},{8,12},{12,8},{9,1... | collective-permute-start | bytes 897032 | tf_op jit(solution)/shard_map/ppermute | solution.py:39
  56.5 1.6 %collective-permute-start.15 = (bf16[1024,128]{1,0:T(8,128)(2,1)S(1)}, bf16[1024,128]{1,0:T(8,128)(2,1)S(1)}, u32[]{:S(2)}, u32[]{:S(2)}) collective-permute-start(bf16[1024,128]{1,0:T(8,128)(2,1)S(1)} %get-tuple-element.28), channel_id=1, source_target_pairs={{0,4},{4,0},{1,5},{5,1},{2,6},{6,2},{3,7},{7,3},{8,12},{12,8},{9,1... | collective-permute-start | bytes 786440 | tf_op jit(solution)/shard_map/ppermute | solution.py:39
  57.1 2.5 %collective-permute-start.13 = (bf16[1024,128]{1,0:T(8,128)(2,1)S(1)}, bf16[1024,128]{1,0:T(8,128)(2,1)S(1)}, u32[]{:S(2)}, u32[]{:S(2)}) collective-permute-start(bf16[1024,128]{1,0:T(8,128)(2,1)S(1)} %get-tuple-element.26), channel_id=1, source_target_pairs={{0,4},{4,0},{1,5},{5,1},{2,6},{6,2},{3,7},{7,3},{8,12},{12,8},{9,1... | collective-permute-start | bytes 786440 | tf_op jit(solution)/shard_map/ppermute | solution.py:39
  58.2 10.0 %collective-permute-start.16 = (bf16[1168,128]{1,0:T(8,128)(2,1)S(1)}, bf16[1168,128]{1,0:T(8,128)(2,1)S(1)}, u32[]{:S(2)}, u32[]{:S(2)}) collective-permute-start(bf16[1168,128]{1,0:T(8,128)(2,1)S(1)} %pair_sum.7), channel_id=1, source_target_pairs={{0,8},{8,16},{16,24},{24,0},{1,9},{9,17},{17,25},{25,1},{2,10},{10... | collective-permute-start | bytes 897032 | tf_op jit(solution)/shard_map/ppermute | solution.py:39
  59.7 10.1 %collective-permute-start.14 = (bf16[1168,128]{1,0:T(8,128)(2,1)S(1)}, bf16[1168,128]{1,0:T(8,128)(2,1)S(1)}, u32[]{:S(2)}, u32[]{:S(2)}) collective-permute-start(bf16[1168,128]{1,0:T(8,128)(2,1)S(1)} %pair_sum.6), channel_id=1, source_target_pairs={{0,16},{8,24},{16,0},{24,8},{1,17},{9,25},{17,1},{25,9},{2,18},{10... | collective-permute-start | bytes 897032 | tf_op jit(solution)/shard_map/ppermute | solution.py:39
  62.8 14.0 %collective-permute-start.12 = (bf16[1168,128]{1,0:T(8,128)(2,1)S(1)}, bf16[1168,128]{1,0:T(8,128)(2,1)S(1)}, u32[]{:S(2)}, u32[]{:S(2)}) collective-permute-start(bf16[1168,128]{1,0:T(8,128)(2,1)S(1)} %pair_sum.4.refs_0_), channel_id=1, source_target_pairs={{0,24},{8,0},{16,8},{24,16},{1,25},{9,1},{17,9},{25,17},{2,26},{10... | collective-permute-start | bytes 897032 | tf_op jit(solution)/shard_map/ppermute | solution.py:39
  63.3 2.1 %collective-permute-start.10 = (bf16[1024,128]{1,0:T(8,128)(2,1)S(1)}, bf16[1024,128]{1,0:T(8,128)(2,1)S(1)}, u32[]{:S(2)}, u32[]{:S(2)}) collective-permute-start(bf16[1024,128]{1,0:T(8,128)(2,1)S(1)} %get-tuple-element.21), channel_id=1, source_target_pairs={{0,4},{4,0},{1,5},{5,1},{2,6},{6,2},{3,7},{7,3},{8,12},{12,8},{9,1... | collective-permute-start | bytes 786440 | tf_op jit(solution)/shard_map/ppermute | solution.py:39

commit v3 on v2

v3 whole, which is shorter than its diff:
```python
import jax
import jax.numpy as jnp
from jax import lax
from jax.experimental import pallas as pl
from jax.experimental.pallas import tpu as pltpu
from jax.sharding import Mesh
from jax.sharding import PartitionSpec as P

Z, X, C, Q = 8, 4, 2, 4
T = 128
PANEL = Q * T
SLOTS = 128
PAY = T + 16
MSG = Z * T + PAY
BLK = T + PAY
F32 = jnp.float32
BF16 = jnp.bfloat16
ROW = ("z", "x", "core")
ALL = ("z", "x", "core", "rep")
SCALE = (Z * X * C * Q * T) ** -0.5

VMEM = pl.BlockSpec(memory_space=pltpu.VMEM)
SMEM = pl.BlockSpec(memory_space=pltpu.SMEM)


def params(mib):
    return pltpu.CompilerParams(vmem_limit_bytes=mib * 2**20)


def cost(flops, size):
    return pl.CostEstimate(flops=flops, bytes_accessed=size, transcendentals=0)


def shift(axis, size, by):
    return [(i, (i + by) % size) for i in range(size)]


def send(array, axis, size, by):
    return lax.ppermute(array, axis, shift(axis, size, by))


def densify_kernel(rows_ref, cols_ref, count_ref, me_ref, tiles_ref, mine_ref, theirs_ref):
    def clear(p, carry):
        mine_ref[p] = jnp.zeros((PANEL, T), BF16)
        theirs_ref[p] = jnp.zeros((PANEL, T), BF16)
        return carry

    lax.fori_loop(0, Z * X, clear, 0)
    x, core = me_ref[0], me_ref[1]

    def place(k, carry):
        col = cols_ref[k]
        offset = (x - (col >> 1) + X) & (X - 1)
        at = offset * Z + (col >> 3)
        span = pl.ds(pl.multiple_of(rows_ref[k] * T, T), T)
        own = (col & 1) == core

        @pl.when(own)
        def _():
            mine_ref[at, span, :] = tiles_ref[k]

        @pl.when(jnp.logical_not(own))
        def _():
            theirs_ref[at, span, :] = tiles_ref[k]

        return carry

    lax.fori_loop(0, count_ref[0], place, 0)


def densify(rows, cols, count, me, tiles):
    return pl.pallas_call(
        densify_kernel,
        in_specs=[SMEM] * 4 + [VMEM],
        out_specs=[VMEM] * 2,
        out_shape=[jax.ShapeDtypeStruct((Z * X, PANEL, T), BF16)] * 2,
        compiler_params=params(16),
        cost_estimate=cost(0, 12 * 2**20),
        name="densify",
    )(rows, cols, count, me, tiles)


def forward(halves, sources, before, dtype, rider=None):
    count = len(sources)
    places = [(half, n) for half, n, _ in sources]
    extra = [array for array in (before, rider) if array is not None]

    def kernel(*refs):
        out_ref, total = refs[-2:]
        for i, (half, n) in enumerate(places):
            panel = jnp.concatenate([refs[half][n * Z + z] for z in range(Z)], axis=1)
            part = jnp.dot(panel, refs[2 + i][...].reshape(Z * T, T), preferred_element_type=F32)
            if i:
                part += total[...]
            elif before is not None:
                part += refs[2 + count][...]
            if i < count - 1:
                total[...] = part
            else:
                out_ref[:PANEL] = part.astype(dtype)
        if rider is not None:
            out_ref[PANEL:] = refs[3 + count][...]

    return pl.pallas_call(
        kernel,
        in_specs=[VMEM] * (2 + count + len(extra)),
        out_specs=VMEM,
        out_shape=jax.ShapeDtypeStruct((PANEL if rider is None else PANEL + T, T), dtype),
        scratch_shapes=[pltpu.VMEM((PANEL, T), F32)],
        compiler_params=params(16),
        cost_estimate=cost(2 * PANEL * T * T * Z * count, 2**20 * count),
        name="forward",
    )(*halves, *(block for _, _, block in sources), *extra)


def tie(block, token):
    def kernel(block_ref, token_ref, out_ref):
        del block_ref, token_ref, out_ref

    return pl.pallas_call(
        kernel,
        in_specs=[VMEM] * 2,
        out_specs=VMEM,
        out_shape=jax.ShapeDtypeStruct(block.shape, block.dtype),
        input_output_aliases={0: 0},
        compiler_params=params(16),
        name="tie",
    )(block, token)


def split(value):
    high = value.astype(BF16)
    low = (value - high.astype(F32)).astype(BF16)
    return high, low


def pack_bias(ref, start, value):
    high, low = split(value)
    rows = lax.broadcasted_iota(jnp.int32, (16, T), 0)
    packed = jnp.where(rows == 0, high.astype(F32), jnp.where(rows == 1, low.astype(F32), 0.0))
    ref[start:start + 16, :] = packed.astype(BF16)


def middle_kernel(me_ref, p0, p1, p2, p3, weight_ref, bias_ref, out_ref, give_ref, pre, cot):
    rep = me_ref[2]
    for n, source in enumerate((p0, p1, p2, p3)):
        cot[(rep - n + Q) % Q] = source[PANEL:]
    get = lambda ref: ref[:PANEL].astype(F32)
    total = (get(p0) + get(p2)) + (get(p1) + get(p3))
    aggregated = total.astype(BF16)
    preact = jnp.dot(aggregated, weight_ref[...], preferred_element_type=F32) + bias_ref[...]
    pre[...] = preact.reshape(Q, T, T)
    sig = jax.nn.sigmoid(preact)
    cotangent = cot[...].reshape(PANEL, T).astype(F32)
    grad_pre = (cotangent * sig * (1.0 + preact * (1.0 - sig))).astype(BF16)
    own = pre[rep]
    out_ref[...] = (own * jax.nn.sigmoid(own)).astype(BF16)
    back = lax.dot_general(weight_ref[...], grad_pre, (((1,), (1,)), ((), ())), preferred_element_type=F32)
    for r in range(Q):
        give_ref[r * T:(r + 1) * T] = back[:, r * T:(r + 1) * T].astype(BF16)
    terms = lax.dot_general(aggregated, grad_pre, (((0,), (0,)), ((), ())), preferred_element_type=F32)
    bias_sum = jnp.sum(grad_pre.astype(F32), axis=0, keepdims=True)
    give_ref[PANEL:PANEL + T] = terms.astype(BF16)
    pack_bias(give_ref, PANEL + T, bias_sum)


def middle(me, partials, weight, bias):
    return pl.pallas_call(
        middle_kernel,
        in_specs=[SMEM] + [VMEM] * 6,
        out_specs=[VMEM] * 2,
        out_shape=[
            jax.ShapeDtypeStruct((T, T), BF16),
            jax.ShapeDtypeStruct((PANEL + PAY, T), BF16),
        ],
        scratch_shapes=[pltpu.VMEM((Q, T, T), F32), pltpu.VMEM((Q, T, T), BF16)],
        compiler_params=params(16),
        cost_estimate=cost(6 * PANEL * T * T, 2**20),
        name="middle",
    )(me, *partials, weight, bias)


def bias_of(ref, start):
    pair = ref[start:start + 16, :].astype(F32)
    return pair[0:1] + pair[1:2]


def backward(mine, other, give, got, chunk):
    def kernel(mine_ref, other_ref, give_ref, got_ref, out_ref):
        wide = lambda ref: jnp.concatenate([ref[r * T:(r + 1) * T] for r in range(Q)], axis=1)
        sides = [(wide(give_ref), mine_ref), (wide(got_ref), other_ref)]
        for z in range(0, Z, 2):
            at = chunk * Z + z
            part = None
            for back, ref in sides:
                pair = jnp.concatenate([ref[at], ref[at + 1]], axis=1)
                term = jnp.dot(back, pair, preferred_element_type=F32)
                part = term if part is None else part + term
            part = part.astype(BF16)
            out_ref[z * T:z * T + T] = part[:, :T]
            out_ref[z * T + T:z * T + 2 * T] = part[:, T:]
        terms = give_ref[PANEL:PANEL + T].astype(F32) + got_ref[PANEL:PANEL + T].astype(F32)
        out_ref[Z * T:Z * T + T] = terms.astype(BF16)
        pack_bias(out_ref, Z * T + T, bias_of(give_ref, PANEL + T) + bias_of(got_ref, PANEL + T))

    return pl.pallas_call(
        kernel,
        in_specs=[VMEM] * 4,
        out_specs=VMEM,
        out_shape=jax.ShapeDtypeStruct((MSG, T), BF16),
        compiler_params=params(16),
        cost_estimate=cost(4 * PANEL * T * T * Z, 2**21),
        name="backward",
    )(mine, other, give, got)


def line_sum(s0, s1, s2, s3):
    def kernel(r0, r1, r2, r3, out_ref):
        def add(a, b):
            get = lambda r: r[a:b].astype(F32)
            return (get(r0) + get(r2)) + (get(r1) + get(r3))

        terms = add(Z * T, Z * T + T).astype(BF16)
        at = Z * T + T
        bias = (bias_of(r0, at) + bias_of(r2, at)) + (bias_of(r1, at) + bias_of(r3, at))
        for z in range(Z):
            out_ref[z, :T] = add(z * T, z * T + T).astype(BF16)
            out_ref[z, T:2 * T] = terms
            pack_bias(out_ref.at[z], 2 * T, bias)

    return pl.pallas_call(
        kernel,
        in_specs=[VMEM] * 4,
        out_specs=VMEM,
        out_shape=jax.ShapeDtypeStruct((Z, BLK, T), BF16),
        compiler_params=params(16),
        cost_estimate=cost(0, 2**20),
        name="line_sum",
    )(s0, s1, s2, s3)


def finish(received):
    def kernel(in_ref, grad_ref, weight_ref, bias_ref):
        total = in_ref[0, :2 * T].astype(F32)
        bias = bias_of(in_ref.at[0], 2 * T)
        for z in range(1, Z):
            total += in_ref[z, :2 * T].astype(F32)
            bias += bias_of(in_ref.at[z], 2 * T)
        grad_ref[...] = total[:T].T.astype(BF16)
        weight_ref[...] = total[T:] * SCALE
        bias_ref[...] = bias * SCALE

    return pl.pallas_call(
        kernel,
        in_specs=[VMEM],
        out_specs=[VMEM] * 3,
        out_shape=[
            jax.ShapeDtypeStruct((T, T), BF16),
            jax.ShapeDtypeStruct((T, T), F32),
            jax.ShapeDtypeStruct((1, T), F32),
        ],
        compiler_params=params(16),
        name="finish",
    )(received)


def body(features, weight, bias_terms, cotangent, tile_values, tile_rows, tile_cols, tile_count):
    x, core, rep = lax.axis_index("x"), lax.axis_index("core"), lax.axis_index("rep")
    me = jnp.stack([x, core, rep]).astype(jnp.int32)
    spread = jnp.broadcast_to(features, (Z, T, T))
    line = lax.all_to_all(spread, "z", 0, 0, tiled=True)
    halves = densify(tile_rows[0, 0], tile_cols[0, 0], tile_count[0], me, tile_values[0, 0])
    near = [(0, 0, line), (1, 0, send(line, "core", C, 1))]
    begun = forward(halves, near, None, F32)
    far = []
    for n in range(1, X):
        block = send(line, "x", X, n)
        if n > 1:
            block = tie(block, begun)
        far += [(0, n, block), (1, n, send(block, "core", C, 1))]
    begun = forward(halves, far[:-1], begun, F32)
    partial = forward(halves, far[-1:], begun, BF16, cotangent)

    partials = [partial] + [send(partial, "rep", Q, n) for n in range(1, Q)]
    mine, theirs = halves
    other = send(tie(theirs, partial), "core", C, 1)
    output, give = middle(me, partials, weight, bias_terms.reshape(1, T))
    got = send(give, "core", C, 1)

    sums = {}
    for n in (1, 2, 3, 0):
        total = backward(mine, other, give, got, n)
        sums[n] = send(total, "x", X, -n) if n else total
    blocks = line_sum(sums[0], sums[1], sums[2], sums[3])
    received = lax.all_to_all(blocks, "z", 0, 0, tiled=True)
    grad_input, weight_grad, bias_grad = finish(received)
    return output, grad_input, weight_grad, bias_grad.reshape(T)


def solution(mesh):
    fine = Mesh(mesh.devices.reshape(Z, X, C, Q), ALL)
    return jax.shard_map(
        body,
        mesh=fine,
        in_specs=(
            P(ALL, None),
            P(),
            P(),
            P(ALL, None),
            P(ROW, "rep", None, None, None),
            P(ROW, "rep", None),
            P(ROW, "rep", None),
            P(ROW, "rep"),
        ),
        out_specs=(P(ALL, None), P(ALL, None), P(), P()),
        check_vma=False,
    )
```

time: 99.5 us -> 97.2 us (0.977)
  starting transfers between devices: 21 us -> 16.4 us
  waiting for transfers between devices: 20.8 us -> 25 us
  Pallas kernels: 11.7 us -> 10.5 us
    ppermute x17 -> x15, starting transfers between devices: 21 us -> 16.4 us  [send(): return lax.ppermute(array, axis, shift(axis, size, by))]
    ppermute x17 -> x15, waiting for transfers between devices: 20.8 us -> 25 us  [send(): return lax.ppermute(array, axis, shift(axis, size, by))]
    pallas_call x11 -> x8, Pallas kernels: 9.33 us -> 8.17 us  [the longest x1 3.67 us: densify(): pl.pallas_call(densify_kernel, in_specs=[SMEM] * 4 + [VMEM], out_specs=[V...]
  transfers between devices with their start and end apart: 17 -> 15, of which waited for: 10 -> 8; matrix products, arithmetic and copies ran while one was open for 0% -> 0% of each run, Pallas kernels for 7% -> 9%
where the time goes in v3:
time: 97.2 us; the launch traced here: 96.8 us
  blocking collectives  39.1 us (40%)
  waiting for transfers between devices  25 us (26%)
  starting transfers between devices  16.4 us (17%)
  Pallas kernels  10.5 us (11%)
  local copies, waits for them, and re-layouts  4.31 us (4%)
  between operations  1.43 us (1%)
    ppermute x15, waiting for transfers between devices, send(): return lax.ppermute(array, axis, shift(axis, size, by))  25 us
    all_to_all x1, blocking collectives, body(): received = lax.all_to_all(blocks, 'z', 0, 0, tiled=True)  20.7 us
    all_to_all x1, blocking collectives, body(): line = lax.all_to_all(spread, 'z', 0, 0, tiled=True)  18.4 us
    ppermute x15, starting transfers between devices, send(): return lax.ppermute(array, axis, shift(axis, size, by))  16.4 us
    pallas_call x1, Pallas kernels, densify(): pl.pallas_call(densify_kernel, in_specs=[SMEM] * 4 + [VMEM], out_specs=[V...  3.67 us
    unnamed x12, local copies, waits for them, and re-layouts  3.52 us
    pallas_call x3, Pallas kernels, forward(): pl.pallas_call(kernel, in_specs=[VMEM] * (2 + count + len(extra)), out_sp...  2.67 us
  transfers between devices with their start and end apart: 15, of which 8 were waited for; matrix products, arithmetic and copies ran while one was open for 0% of the time, Pallas kernels for 9%

profile of v3, /device:TPU:3, one launch (start us, length us, event | category | flops | bytes accessed | tf_op | source)
XLA Modules:
  0.0 96.8 jit_solution(2883046008294426249)
XLA Ops:
  0.6 0.8 broadcast_in_dim.3
  1.4 18.4 %all_to_all.10.refs_2_ = bf16[8,128,128]{2,1,0:T(8,128)(2,1)S(1)} all-to-all(bf16[8,128,128]{2,1,0:T(8,128)(2,1)S(1)} %broadcast_in_dim.3), channel_id=1, replica_groups=mesh['z'=8,'x'=4,'core'=2,'rep'=4] {'z'}, dimensions={0} | all-to-all | bytes 524288 | tf_op jit(solution)/shard_map/all_to_all | solution.py:271
  19.8 2.5 %collective-permute-start.1 = (bf16[8,128,128]{2,1,0:T(8,128)(2,1)S(1)}, bf16[8,128,128]{2,1,0:T(8,128)(2,1)S(1)}, u32[]{:S(2)}, u32[]{:S(2)}) collective-permute-start(bf16[8,128,128]{2,1,0:T(8,128)(2,1)S(1)} %all_to_all.10.refs_2_), channel_id=1, source_target_pairs={{0,4},{4,0},{1,5},{5,1},{2,6},{6,2},{3,7},{7,3},{8,12},{12,8},{9,1... | collective-permute-start | bytes 786440 | tf_op jit(solution)/shard_map/ppermute | solution.py:39
  22.2 1.8 %collective-permute-start.5 = (bf16[8,128,128]{2,1,0:T(8,128)(2,1)S(1)}, bf16[8,128,128]{2,1,0:T(8,128)(2,1)S(1)}, u32[]{:S(2)}, u32[]{:S(2)}) collective-permute-start(bf16[8,128,128]{2,1,0:T(8,128)(2,1)S(1)} %all_to_all.10.refs_2_), channel_id=1, source_target_pairs={{0,16},{8,24},{16,0},{24,8},{1,17},{9,25},{17,1},{25,9},{2,18},{10... | collective-permute-start | bytes 786440 | tf_op jit(solution)/shard_map/ppermute | solution.py:39
  24.1 0.0 collective-permute-start.3
  24.1 1.5 %collective-permute-start = (bf16[8,128,128]{2,1,0:T(8,128)(2,1)S(1)}, bf16[8,128,128]{2,1,0:T(8,128)(2,1)S(1)}, u32[]{:S(2)}, u32[]{:S(2)}) collective-permute-start(bf16[8,128,128]{2,1,0:T(8,128)(2,1)S(1)} %all_to_all.10.refs_2_), channel_id=1, source_target_pairs={{0,24},{8,0},{16,8},{24,16},{1,25},{9,1},{17,9},{25,17},{2,26},{10... | collective-permute-start | bytes 786440 | tf_op jit(solution)/shard_map/ppermute | solution.py:39
  26.2 0.1 pad_add_fusion.me_ref
  26.3 2.2 %copy-done = bf16[1,1,128,128,128]{4,3,2,1,0:T(8,128)(2,1)S(1)} copy-done((bf16[1,1,128,128,128]{4,3,2,1,0:T(8,128)(2,1)S(1)}, bf16[1,1,128,128,128]{4,3,2,1,0:T(8,128)(2,1)}, u32[]{:S(2)}) %copy-start) | copy-done | bytes 4194328
  28.5 0.7 copy-done.4
  29.1 0.7 copy-done.5
  29.8 3.7 %densify.1 = (bf16[32,512,128]{2,1,0:T(8,128)(2,1)S(1)}, bf16[32,512,128]{2,1,0:T(8,128)(2,1)S(1)}) custom-call(s32[128]{0:T(128)S(1)} %bitcast.12, s32[128]{0:T(128)S(1)} %bitcast.13, s32[1]{0:T(128)} %bitcast.9.count_ref, s32[3]{0:T(128)S(1)} %pad_add_fusion.me_ref, bf16[128,128,128]{2,1,0:T(8,128)(2,1)S(1)} %bitcast.10), custom_call_target="tpu_custom_call" | custom-call | bytes 12582912 | tf_op jit(solution)/shard_map/densify/pallas_call | solution.py:72
  33.5 0.0 collective-permute-done.1.refs_3_
  33.5 0.7 forward.3.token_ref.refs_7_
  34.2 0.0 collective-permute-done.5.block_ref
  34.2 0.7 collective-permute-start.6
  34.9 2.5 %collective-permute-done.3.refs_2_ = bf16[8,128,128]{2,1,0:T(8,128)(2,1)S(1)} collective-permute-done((bf16[8,128,128]{2,1,0:T(8,128)(2,1)S(1)}, bf16[8,128,128]{2,1,0:T(8,128)(2,1)S(1)}, u32[]{:S(2)}, u32[]{:S(2)}) %collective-permute-start.3) | collective-permute-done | bytes 262176 | tf_op jit(solution)/shard_map/ppermute | solution.py:39
  37.4 0.8 collective-permute-start.4
  38.2 0.0 collective-permute-done.block_ref
  38.2 0.1 collective-permute-start.2
  38.3 0.0 collective-permute-done.6.refs_5_
  38.3 1.1 %collective-permute-done.4.refs_3_ = bf16[8,128,128]{2,1,0:T(8,128)(2,1)S(1)} collective-permute-done((bf16[8,128,128]{2,1,0:T(8,128)(2,1)S(1)}, bf16[8,128,128]{2,1,0:T(8,128)(2,1)S(1)}, u32[]{:S(2)}, u32[]{:S(2)}) %collective-permute-start.4) | collective-permute-done | bytes 262176 | tf_op jit(solution)/shard_map/ppermute | solution.py:39
  39.3 1.5 %forward.4.refs_3_ = f32[512,128]{1,0:T(8,128)S(1)} custom-call(bf16[32,512,128]{2,1,0:T(8,128)(2,1)S(1)} %get-tuple-element.11.refs_0_.mine_ref, bf16[32,512,128]{2,1,0:T(8,128)(2,1)S(1)} %get-tuple-element.12.refs_1_.block_ref, bf16[8,128,128]{2,1,0:T(8,128)(2,1)S(1)} %collective-permute-done.3.refs_2_, ...), custom_call_target="tpu_custom_call" | custom-call | flops 671088640 | bytes 5242880 | tf_op jit(solution)/shard_map/forward/pallas_call | solution.py:104
  40.8 0.0 collective-permute-done.2.refs_2_
  40.9 0.4 forward.5.p0.token_ref
  41.3 0.0 copy-start.2
  41.3 0.0 copy-start.3
  41.4 0.5 collective-permute-start.10
  41.8 1.3 %collective-permute-start.7 = (bf16[640,128]{1,0:T(8,128)(2,1)S(1)}, bf16[640,128]{1,0:T(8,128)(2,1)S(1)}, u32[]{:S(2)}, u32[]{:S(2)}) collective-permute-start(bf16[640,128]{1,0:T(8,128)(2,1)S(1)} %forward.5.p0.token_ref), channel_id=1, source_target_pairs={{0,1},{1,2},{2,3},{3,0},{4,5},{5,6},{6,7},{7,4},{8,9},{9,10},{10,1... | collective-permute-start | bytes 491528 | tf_op jit(solution)/shard_map/ppermute | solution.py:39
  43.1 2.6 %collective-permute-start.8 = (bf16[640,128]{1,0:T(8,128)(2,1)S(1)}, bf16[640,128]{1,0:T(8,128)(2,1)S(1)}, u32[]{:S(2)}, u32[]{:S(2)}) collective-permute-start(bf16[640,128]{1,0:T(8,128)(2,1)S(1)} %forward.5.p0.token_ref), channel_id=1, source_target_pairs={{0,2},{1,3},{2,0},{3,1},{4,6},{5,7},{6,4},{7,5},{8,10},{9,11},{10,... | collective-permute-start | bytes 491528 | tf_op jit(solution)/shard_map/ppermute | solution.py:39
  45.7 1.1 %collective-permute-start.9 = (bf16[640,128]{1,0:T(8,128)(2,1)S(1)}, bf16[640,128]{1,0:T(8,128)(2,1)S(1)}, u32[]{:S(2)}, u32[]{:S(2)}) collective-permute-start(bf16[640,128]{1,0:T(8,128)(2,1)S(1)} %forward.5.p0.token_ref), channel_id=1, source_target_pairs={{0,3},{1,0},{2,1},{3,2},{4,7},{5,4},{6,5},{7,6},{8,11},{9,8},{10,9... | collective-permute-start | bytes 491528 | tf_op jit(solution)/shard_map/ppermute | solution.py:39
  46.8 2.0 %collective-permute-done.7.p1 = bf16[640,128]{1,0:T(8,128)(2,1)S(1)} collective-permute-done((bf16[640,128]{1,0:T(8,128)(2,1)S(1)}, bf16[640,128]{1,0:T(8,128)(2,1)S(1)}, u32[]{:S(2)}, u32[]{:S(2)}) %collective-permute-start.7) | collective-permute-done | bytes 163872 | tf_op jit(solution)/shard_map/ppermute | solution.py:39
  48.8 4.6 %collective-permute-done.8.p2 = bf16[640,128]{1,0:T(8,128)(2,1)S(1)} collective-permute-done((bf16[640,128]{1,0:T(8,128)(2,1)S(1)}, bf16[640,128]{1,0:T(8,128)(2,1)S(1)}, u32[]{:S(2)}, u32[]{:S(2)}) %collective-permute-start.8) | collective-permute-done | bytes 163872 | tf_op jit(solution)/shard_map/ppermute | solution.py:39
  53.5 1.4 %middle.1 = (bf16[128,128]{1,0:T(8,128)(2,1)}, bf16[656,128]{1,0:T(8,128)(2,1)S(1)}) custom-call(s32[3]{0:T(128)S(1)} %pad_add_fusion.me_ref, bf16[640,128]{1,0:T(8,128)(2,1)S(1)} %forward.5.p0.token_ref, bf16[640,128]{1,0:T(8,128)(2,1)S(1)} %collective-permute-done.7.p1, bf16[640,128]{1,0:T(8,128)(2,1)S(1)} %collective-permute-done.8.p2, ...), custom_call_target="tpu_custom_call" | custom-call | flops 50331648 | bytes 1048576 | tf_op jit(solution)/shard_map/middle/pallas_call | solution.py:168
  54.9 0.9 collective-permute-start.11
  55.8 1.0 %collective-permute-done.11.got_ref = bf16[656,128]{1,0:T(8,128)(2,1)S(1)} collective-permute-done((bf16[656,128]{1,0:T(8,128)(2,1)S(1)}, bf16[656,128]{1,0:T(8,128)(2,1)S(1)}, u32[]{:S(2)}, u32[]{:S(2)}) %collective-permute-start.11) | collective-permute-done | bytes 167968 | tf_op jit(solution)/shard_map/ppermute | solution.py:39
  56.9 0.5 backward.7
  57.3 0.3 collective-permute-start.14
  57.7 0.5 backward.6
  58.1 1.8 %collective-permute-start.13 = (bf16[1168,128]{1,0:T(8,128)(2,1)S(1)}, bf16[1168,128]{1,0:T(8,128)(2,1)S(1)}, u32[]{:S(2)}, u32[]{:S(2)}) collective-permute-start(bf16[1168,128]{1,0:T(8,128)(2,1)S(1)} %backward.6), channel_id=1, source_target_pairs={{0,16},{8,24},{16,0},{24,8},{1,17},{9,25},{17,1},{25,9},{2,18},{10... | collective-permute-start | bytes 897032 | tf_op jit(solution)/shard_map/ppermute | solution.py:39
  59.9 0.5 backward.5
  60.4 0.5 collective-permute-start.12
  60.9 0.5 backward.4.r0
  61.4 4.3 %collective-permute-done.14.r3 = bf16[1168,128]{1,0:T(8,128)(2,1)S(1)} collective-permute-done((bf16[1168,128]{1,0:T(8,128)(2,1)S(1)}, bf16[1168,128]{1,0:T(8,128)(2,1)S(1)}, u32[]{:S(2)}, u32[]{:S(2)}) %collective-permute-start.14) | collective-permute-done | bytes 299040 | tf_op jit(solution)/shard_map/ppermute | solution.py:39
  65.7 2.0 %collective-permute-done.13.r2 = bf16[1168,128]{1,0:T(8,128)(2,1)S(1)} collective-permute-done((bf16[1168,128]{1,0:T(8,128)(2,1)S(1)}, bf16[1168,128]{1,0:T(8,128)(2,1)S(1)}, u32[]{:S(2)}, u32[]{:S(2)}) %collective-permute-start.13) | collective-permute-done | bytes 299040 | tf_op jit(solution)/shard_map/ppermute | solution.py:39
  67.8 7.4 %collective-permute-done.12.r1 = bf16[1168,128]{1,0:T(8,128)(2,1)S(1)} collective-permute-done((bf16[1168,128]{1,0:T(8,128)(2,1)S(1)}, bf16[1168,128]{1,0:T(8,128)(2,1)S(1)}, u32[]{:S(2)}, u32[]{:S(2)}) %collective-permute-start.12) | collective-permute-done | bytes 299040 | tf_op jit(solution)/shard_map/ppermute | solution.py:39
  75.2 0.2 line_sum.1
  75.3 20.7 %all_to_all.11.in_ref = bf16[8,272,128]{2,1,0:T(8,128)(2,1)S(1)} all-to-all(bf16[8,272,128]{2,1,0:T(8,128)(2,1)S(1)} %line_sum.1), channel_id=1, replica_groups=mesh['z'=8,'x'=4,'core'=2,'rep'=4] {'z'}, dimensions={0} | all-to-all | bytes 1114112 | tf_op jit(solution)/shard_map/all_to_all | solution.py:295
  96.1 0.7 finish.1
  (12 shorter events, 0.0 us)
Async XLA Ops:
  19.8 13.7 %collective-permute-start.1 = (bf16[8,128,128]{2,1,0:T(8,128)(2,1)S(1)}, bf16[8,128,128]{2,1,0:T(8,128)(2,1)S(1)}, u32[]{:S(2)}, u32[]{:S(2)}) collective-permute-start(bf16[8,128,128]{2,1,0:T(8,128)(2,1)S(1)} %all_to_all.10.refs_2_), channel_id=1, source_target_pairs={{0,4},{4,0},{1,5},{5,1},{2,6},{6,2},{3,7},{7,3},{8,12},{12,8},{9,1... | collective-permute-start | bytes 786440 | tf_op jit(solution)/shard_map/ppermute | solution.py:39
  22.2 11.9 %collective-permute-start.5 = (bf16[8,128,128]{2,1,0:T(8,128)(2,1)S(1)}, bf16[8,128,128]{2,1,0:T(8,128)(2,1)S(1)}, u32[]{:S(2)}, u32[]{:S(2)}) collective-permute-start(bf16[8,128,128]{2,1,0:T(8,128)(2,1)S(1)} %all_to_all.10.refs_2_), channel_id=1, source_target_pairs={{0,16},{8,24},{16,0},{24,8},{1,17},{9,25},{17,1},{25,9},{2,18},{10... | collective-permute-start | bytes 786440 | tf_op jit(solution)/shard_map/ppermute | solution.py:39
  24.1 13.3 %collective-permute-start.3 = (bf16[8,128,128]{2,1,0:T(8,128)(2,1)S(1)}, bf16[8,128,128]{2,1,0:T(8,128)(2,1)S(1)}, u32[]{:S(2)}, u32[]{:S(2)}) collective-permute-start(bf16[8,128,128]{2,1,0:T(8,128)(2,1)S(1)} %all_to_all.10.refs_2_), channel_id=1, source_target_pairs={{0,8},{8,16},{16,24},{24,0},{1,9},{9,17},{17,25},{25,1},{2,10},{10... | collective-permute-start | bytes 786440 | tf_op jit(solution)/shard_map/ppermute | solution.py:39
  24.1 14.1 %collective-permute-start = (bf16[8,128,128]{2,1,0:T(8,128)(2,1)S(1)}, bf16[8,128,128]{2,1,0:T(8,128)(2,1)S(1)}, u32[]{:S(2)}, u32[]{:S(2)}) collective-permute-start(bf16[8,128,128]{2,1,0:T(8,128)(2,1)S(1)} %all_to_all.10.refs_2_), channel_id=1, source_target_pairs={{0,24},{8,0},{16,8},{24,16},{1,25},{9,1},{17,9},{25,17},{2,26},{10... | collective-permute-start | bytes 786440 | tf_op jit(solution)/shard_map/ppermute | solution.py:39
  26.3 2.2 %copy-start = (bf16[1,1,128,128,128]{4,3,2,1,0:T(8,128)(2,1)S(1)}, bf16[1,1,128,128,128]{4,3,2,1,0:T(8,128)(2,1)}, u32[]{:S(2)}) copy-start(bf16[1,1,128,128,128]{4,3,2,1,0:T(8,128)(2,1)} %param.12) | copy-start | bytes 12582916
  28.5 0.7 copy-start.4
  29.1 0.7 copy-start.5
  34.2 4.1 %collective-permute-start.6 = (bf16[8,128,128]{2,1,0:T(8,128)(2,1)S(1)}, bf16[8,128,128]{2,1,0:T(8,128)(2,1)S(1)}, u32[]{:S(2)}, u32[]{:S(2)}) collective-permute-start(bf16[8,128,128]{2,1,0:T(8,128)(2,1)S(1)} %tie.4.refs_4_), channel_id=1, source_target_pairs={{0,4},{4,0},{1,5},{5,1},{2,6},{6,2},{3,7},{7,3},{8,12},{12,8},{9,1... | collective-permute-start | bytes 786440 | tf_op jit(solution)/shard_map/ppermute | solution.py:39
  37.4 1.9 %collective-permute-start.4 = (bf16[8,128,128]{2,1,0:T(8,128)(2,1)S(1)}, bf16[8,128,128]{2,1,0:T(8,128)(2,1)S(1)}, u32[]{:S(2)}, u32[]{:S(2)}) collective-permute-start(bf16[8,128,128]{2,1,0:T(8,128)(2,1)S(1)} %collective-permute-done.3.refs_2_), channel_id=1, source_target_pairs={{0,4},{4,0},{1,5},{5,1},{2,6},{6,2},{3,7},{7,3},{8,12},{12,8},{9,1... | collective-permute-start | bytes 786440 | tf_op jit(solution)/shard_map/ppermute | solution.py:39
  38.2 2.7 %copy-start.1 = (bf16[128,128]{1,0:T(8,128)(2,1)S(1)}, bf16[128,128]{1,0:T(8,128)(2,1)}, u32[]{:S(2)}) copy-start(bf16[128,128]{1,0:T(8,128)(2,1)} %refs_4_.1) | copy-start | bytes 98308
  38.2 2.7 %collective-permute-start.2 = (bf16[8,128,128]{2,1,0:T(8,128)(2,1)S(1)}, bf16[8,128,128]{2,1,0:T(8,128)(2,1)S(1)}, u32[]{:S(2)}, u32[]{:S(2)}) collective-permute-start(bf16[8,128,128]{2,1,0:T(8,128)(2,1)S(1)} %tie.3.refs_6_), channel_id=1, source_target_pairs={{0,4},{4,0},{1,5},{5,1},{2,6},{6,2},{3,7},{7,3},{8,12},{12,8},{9,1... | collective-permute-start | bytes 786440 | tf_op jit(solution)/shard_map/ppermute | solution.py:39
  41.3 12.1 %copy-start.2 = (bf16[128,128]{1,0:T(8,128)(2,1)S(1)}, bf16[128,128]{1,0:T(8,128)(2,1)}, u32[]{:S(2)}) copy-start(bf16[128,128]{1,0:T(8,128)(2,1)} %weight_ref.1) | copy-start | bytes 98308
  41.3 12.1 %copy-start.3 = (f32[128]{0:T(128)S(1)}, f32[128]{0:T(128)}, u32[]{:S(2)}) copy-start(f32[128]{0:T(128)} %param.10) | copy-start | bytes 1540
  41.4 15.5 %collective-permute-start.10 = (bf16[32,512,128]{2,1,0:T(8,128)(2,1)S(1)}, bf16[32,512,128]{2,1,0:T(8,128)(2,1)S(1)}, u32[]{:S(2)}, u32[]{:S(2)}) collective-permute-start(bf16[32,512,128]{2,1,0:T(8,128)(2,1)S(1)} %tie.5), channel_id=1, source_target_pairs={{0,4},{4,0},{1,5},{5,1},{2,6},{6,2},{3,7},{7,3},{8,12},{12,8},{9,1... | collective-permute-start | bytes 12582920 | tf_op jit(solution)/shard_map/ppermute | solution.py:39
  41.8 7.0 %collective-permute-start.7 = (bf16[640,128]{1,0:T(8,128)(2,1)S(1)}, bf16[640,128]{1,0:T(8,128)(2,1)S(1)}, u32[]{:S(2)}, u32[]{:S(2)}) collective-permute-start(bf16[640,128]{1,0:T(8,128)(2,1)S(1)} %forward.5.p0.token_ref), channel_id=1, source_target_pairs={{0,1},{1,2},{2,3},{3,0},{4,5},{5,6},{6,7},{7,4},{8,9},{9,10},{10,1... | collective-permute-start | bytes 491528 | tf_op jit(solution)/shard_map/ppermute | solution.py:39
  43.1 10.3 %collective-permute-start.8 = (bf16[640,128]{1,0:T(8,128)(2,1)S(1)}, bf16[640,128]{1,0:T(8,128)(2,1)S(1)}, u32[]{:S(2)}, u32[]{:S(2)}) collective-permute-start(bf16[640,128]{1,0:T(8,128)(2,1)S(1)} %forward.5.p0.token_ref), channel_id=1, source_target_pairs={{0,2},{1,3},{2,0},{3,1},{4,6},{5,7},{6,4},{7,5},{8,10},{9,11},{10,... | collective-permute-start | bytes 491528 | tf_op jit(solution)/shard_map/ppermute | solution.py:39
  45.7 7.7 %collective-permute-start.9 = (bf16[640,128]{1,0:T(8,128)(2,1)S(1)}, bf16[640,128]{1,0:T(8,128)(2,1)S(1)}, u32[]{:S(2)}, u32[]{:S(2)}) collective-permute-start(bf16[640,128]{1,0:T(8,128)(2,1)S(1)} %forward.5.p0.token_ref), channel_id=1, source_target_pairs={{0,3},{1,0},{2,1},{3,2},{4,7},{5,4},{6,5},{7,6},{8,11},{9,8},{10,9... | collective-permute-start | bytes 491528 | tf_op jit(solution)/shard_map/ppermute | solution.py:39
  54.9 2.0 %collective-permute-start.11 = (bf16[656,128]{1,0:T(8,128)(2,1)S(1)}, bf16[656,128]{1,0:T(8,128)(2,1)S(1)}, u32[]{:S(2)}, u32[]{:S(2)}) collective-permute-start(bf16[656,128]{1,0:T(8,128)(2,1)S(1)} %get-tuple-element.14.give_ref), channel_id=1, source_target_pairs={{0,4},{4,0},{1,5},{5,1},{2,6},{6,2},{3,7},{7,3},{8,12},{12,8},{9,1... | collective-permute-start | bytes 503816 | tf_op jit(solution)/shard_map/ppermute | solution.py:39
  57.3 8.4 %collective-permute-start.14 = (bf16[1168,128]{1,0:T(8,128)(2,1)S(1)}, bf16[1168,128]{1,0:T(8,128)(2,1)S(1)}, u32[]{:S(2)}, u32[]{:S(2)}) collective-permute-start(bf16[1168,128]{1,0:T(8,128)(2,1)S(1)} %backward.7), channel_id=1, source_target_pairs={{0,8},{8,16},{16,24},{24,0},{1,9},{9,17},{17,25},{25,1},{2,10},{10... | collective-permute-start | bytes 897032 | tf_op jit(solution)/shard_map/ppermute | solution.py:39
  58.1 9.6 %collective-permute-start.13 = (bf16[1168,128]{1,0:T(8,128)(2,1)S(1)}, bf16[1168,128]{1,0:T(8,128)(2,1)S(1)}, u32[]{:S(2)}, u32[]{:S(2)}) collective-permute-start(bf16[1168,128]{1,0:T(8,128)(2,1)S(1)} %backward.6), channel_id=1, source_target_pairs={{0,16},{8,24},{16,0},{24,8},{1,17},{9,25},{17,1},{25,9},{2,18},{10... | collective-permute-start | bytes 897032 | tf_op jit(solution)/shard_map/ppermute | solution.py:39
  60.4 14.8 %collective-permute-start.12 = (bf16[1168,128]{1,0:T(8,128)(2,1)S(1)}, bf16[1168,128]{1,0:T(8,128)(2,1)S(1)}, u32[]{:S(2)}, u32[]{:S(2)}) collective-permute-start(bf16[1168,128]{1,0:T(8,128)(2,1)S(1)} %backward.5), channel_id=1, source_target_pairs={{0,24},{8,0},{16,8},{24,16},{1,25},{9,1},{17,9},{25,17},{2,26},{10... | collective-permute-start | bytes 897032 | tf_op jit(solution)/shard_map/ppermute | solution.py:39

commit v4 on v3

--- a/solution.py
+++ b/solution.py
@@ -10,7 +10,8 @@
 T = 128
 PANEL = Q * T
 SLOTS = 128
-PAY = T + 16
+HALF = T // 2
+PAY = HALF + 16
 MSG = Z * T + PAY
 BLK = T + PAY
 F32 = jnp.float32
@@ -39,7 +40,7 @@
     return lax.ppermute(array, axis, shift(axis, size, by))
 
 
-def densify_kernel(rows_ref, cols_ref, count_ref, me_ref, tiles_ref, mine_ref, theirs_ref):
+def densify_kernel(me_ref, tiles_ref, mine_ref, theirs_ref):
     def clear(p, carry):
         mine_ref[p] = jnp.zeros((PANEL, T), BF16)
         theirs_ref[p] = jnp.zeros((PANEL, T), BF16)
@@ -49,10 +50,10 @@
     x, core = me_ref[0], me_ref[1]
 
     def place(k, carry):
-        col = cols_ref[k]
+        col = me_ref[4 + SLOTS + k]
         offset = (x - (col >> 1) + X) & (X - 1)
         at = offset * Z + (col >> 3)
-        span = pl.ds(pl.multiple_of(rows_ref[k] * T, T), T)
+        span = pl.ds(pl.multiple_of(me_ref[4 + k] * T, T), T)
         own = (col & 1) == core
 
         @pl.when(own)
@@ -65,19 +66,19 @@
 
         return carry
 
-    lax.fori_loop(0, count_ref[0], place, 0)
-
-
-def densify(rows, cols, count, me, tiles):
+    lax.fori_loop(0, me_ref[3], place, 0)
+
+
+def densify(me, tiles):
     return pl.pallas_call(
         densify_kernel,
-        in_specs=[SMEM] * 4 + [VMEM],
+        in_specs=[SMEM, VMEM],
         out_specs=[VMEM] * 2,
         out_shape=[jax.ShapeDtypeStruct((Z * X, PANEL, T), BF16)] * 2,
         compiler_params=params(16),
         cost_estimate=cost(0, 12 * 2**20),
         name="densify",
-    )(rows, cols, count, me, tiles)
+    )(me, tiles)
 
 
 def forward(halves, sources, before, dtype, rider=None):
@@ -141,8 +142,8 @@
     ref[start:start + 16, :] = packed.astype(BF16)
 
 
-def middle_kernel(me_ref, p0, p1, p2, p3, weight_ref, bias_ref, out_ref, give_ref, pre, cot):
-    rep = me_ref[2]
+def middle_kernel(me_ref, p0, p1, p2, p3, weight_ref, bias_ref, out_ref, give_ref, keep_ref, pre, cot, halves):
+    core, rep = me_ref[1], me_ref[2]
     for n, source in enumerate((p0, p1, p2, p3)):
         cot[(rep - n + Q) % Q] = source[PANEL:]
     get = lambda ref: ref[:PANEL].astype(F32)
@@ -160,20 +161,27 @@
         give_ref[r * T:(r + 1) * T] = back[:, r * T:(r + 1) * T].astype(BF16)
     terms = lax.dot_general(aggregated, grad_pre, (((0,), (0,)), ((), ())), preferred_element_type=F32)
     bias_sum = jnp.sum(grad_pre.astype(F32), axis=0, keepdims=True)
-    give_ref[PANEL:PANEL + T] = terms.astype(BF16)
-    pack_bias(give_ref, PANEL + T, bias_sum)
+    halves[...] = terms.reshape(C, HALF, T)
+    keep_ref[...] = halves[core]
+    give_ref[PANEL:PANEL + HALF] = halves[1 - core].astype(BF16)
+    pack_bias(give_ref, PANEL + HALF, bias_sum)
 
 
 def middle(me, partials, weight, bias):
     return pl.pallas_call(
         middle_kernel,
         in_specs=[SMEM] + [VMEM] * 6,
-        out_specs=[VMEM] * 2,
+        out_specs=[VMEM] * 3,
         out_shape=[
             jax.ShapeDtypeStruct((T, T), BF16),
             jax.ShapeDtypeStruct((PANEL + PAY, T), BF16),
+            jax.ShapeDtypeStruct((HALF, T), F32),
         ],
-        scratch_shapes=[pltpu.VMEM((Q, T, T), F32), pltpu.VMEM((Q, T, T), BF16)],
+        scratch_shapes=[
+            pltpu.VMEM((Q, T, T), F32),
+            pltpu.VMEM((Q, T, T), BF16),
+            pltpu.VMEM((C, HALF, T), F32),
+        ],
         compiler_params=params(16),
         cost_estimate=cost(6 * PANEL * T * T, 2**20),
         name="middle",
@@ -185,8 +193,8 @@
     return pair[0:1] + pair[1:2]
 
 
-def backward(mine, other, give, got, chunk):
-    def kernel(mine_ref, other_ref, give_ref, got_ref, out_ref):
+def backward(mine, other, give, got, keep, chunk):
+    def kernel(mine_ref, other_ref, give_ref, got_ref, keep_ref, out_ref):
         wide = lambda ref: jnp.concatenate([ref[r * T:(r + 1) * T] for r in range(Q)], axis=1)
         sides = [(wide(give_ref), mine_ref), (wide(got_ref), other_ref)]
         for z in range(0, Z, 2):
@@ -199,19 +207,20 @@
             part = part.astype(BF16)
             out_ref[z * T:z * T + T] = part[:, :T]
             out_ref[z * T + T:z * T + 2 * T] = part[:, T:]
-        terms = give_ref[PANEL:PANEL + T].astype(F32) + got_ref[PANEL:PANEL + T].astype(F32)
-        out_ref[Z * T:Z * T + T] = terms.astype(BF16)
-        pack_bias(out_ref, Z * T + T, bias_of(give_ref, PANEL + T) + bias_of(got_ref, PANEL + T))
-
-    return pl.pallas_call(
-        kernel,
-        in_specs=[VMEM] * 4,
+        terms = keep_ref[...] + got_ref[PANEL:PANEL + HALF].astype(F32)
+        out_ref[Z * T:Z * T + HALF] = terms.astype(BF16)
+        bias = bias_of(give_ref, PANEL + HALF) + bias_of(got_ref, PANEL + HALF)
+        pack_bias(out_ref, Z * T + HALF, bias)
+
+    return pl.pallas_call(
+        kernel,
+        in_specs=[VMEM] * 5,
         out_specs=VMEM,
         out_shape=jax.ShapeDtypeStruct((MSG, T), BF16),
         compiler_params=params(16),
         cost_estimate=cost(4 * PANEL * T * T * Z, 2**21),
         name="backward",
-    )(mine, other, give, got)
+    )(mine, other, give, got, keep)
 
 
 def line_sum(s0, s1, s2, s3):
@@ -220,13 +229,13 @@
             get = lambda r: r[a:b].astype(F32)
             return (get(r0) + get(r2)) + (get(r1) + get(r3))
 
-        terms = add(Z * T, Z * T + T).astype(BF16)
-        at = Z * T + T
+        terms = add(Z * T, Z * T + HALF).astype(BF16)
+        at = Z * T + HALF
         bias = (bias_of(r0, at) + bias_of(r2, at)) + (bias_of(r1, at) + bias_of(r3, at))
         for z in range(Z):
             out_ref[z, :T] = add(z * T, z * T + T).astype(BF16)
-            out_ref[z, T:2 * T] = terms
-            pack_bias(out_ref.at[z], 2 * T, bias)
+            out_ref[z, T:T + HALF] = terms
+            pack_bias(out_ref.at[z], T + HALF, bias)
 
     return pl.pallas_call(
         kernel,
@@ -239,37 +248,55 @@
     )(s0, s1, s2, s3)
 
 
-def finish(received):
-    def kernel(in_ref, grad_ref, weight_ref, bias_ref):
-        total = in_ref[0, :2 * T].astype(F32)
-        bias = bias_of(in_ref.at[0], 2 * T)
+def finish_terms(received):
+    def kernel(in_ref, half_ref, bias_ref):
+        total = in_ref[0, T:T + HALF].astype(F32)
+        bias = bias_of(in_ref.at[0], T + HALF)
         for z in range(1, Z):
-            total += in_ref[z, :2 * T].astype(F32)
-            bias += bias_of(in_ref.at[z], 2 * T)
-        grad_ref[...] = total[:T].T.astype(BF16)
-        weight_ref[...] = total[T:] * SCALE
+            total += in_ref[z, T:T + HALF].astype(F32)
+            bias += bias_of(in_ref.at[z], T + HALF)
+        half_ref[...] = total * SCALE
         bias_ref[...] = bias * SCALE
 
     return pl.pallas_call(
         kernel,
         in_specs=[VMEM],
-        out_specs=[VMEM] * 3,
+        out_specs=[VMEM] * 2,
         out_shape=[
-            jax.ShapeDtypeStruct((T, T), BF16),
-            jax.ShapeDtypeStruct((T, T), F32),
+            jax.ShapeDtypeStruct((HALF, T), F32),
             jax.ShapeDtypeStruct((1, T), F32),
         ],
         compiler_params=params(16),
-        name="finish",
+        cost_estimate=cost(0, 2**18),
+        name="finish_terms",
+    )(received)
+
+
+def finish_grad(received):
+    def kernel(in_ref, grad_ref):
+        total = in_ref[0, :T].astype(F32)
+        for z in range(1, Z):
+            total += in_ref[z, :T].astype(F32)
+        grad_ref[...] = total.T.astype(BF16)
+
+    return pl.pallas_call(
+        kernel,
+        in_specs=[VMEM],
+        out_specs=VMEM,
+        out_shape=jax.ShapeDtypeStruct((T, T), BF16),
+        compiler_params=params(16),
+        cost_estimate=cost(0, 2**22),
+        name="finish_grad",
     )(received)
 
 
 def body(features, weight, bias_terms, cotangent, tile_values, tile_rows, tile_cols, tile_count):
     x, core, rep = lax.axis_index("x"), lax.axis_index("core"), lax.axis_index("rep")
-    me = jnp.stack([x, core, rep]).astype(jnp.int32)
+    place = jnp.stack([x, core, rep, tile_count[0, 0]]).astype(jnp.int32)
+    me = jnp.concatenate([place, tile_rows[0, 0], tile_cols[0, 0]])
     spread = jnp.broadcast_to(features, (Z, T, T))
     line = lax.all_to_all(spread, "z", 0, 0, tiled=True)
-    halves = densify(tile_rows[0, 0], tile_cols[0, 0], tile_count[0], me, tile_values[0, 0])
+    halves = densify(me, tile_values[0, 0])
     near = [(0, 0, line), (1, 0, send(line, "core", C, 1))]
     begun = forward(halves, near, None, F32)
     far = []
@@ -283,17 +310,20 @@
 
     partials = [partial] + [send(partial, "rep", Q, n) for n in range(1, Q)]
     mine, theirs = halves
-    other = send(tie(theirs, partial), "core", C, 1)
-    output, give = middle(me, partials, weight, bias_terms.reshape(1, T))
+    fellow = send(tie(theirs, partial), "core", C, 1)
+    output, give, keep = middle(place, partials, weight, bias_terms.reshape(1, T))
     got = send(give, "core", C, 1)
 
     sums = {}
     for n in (1, 2, 3, 0):
-        total = backward(mine, other, give, got, n)
+        total = backward(mine, fellow, give, got, keep, n)
         sums[n] = send(total, "x", X, -n) if n else total
     blocks = line_sum(sums[0], sums[1], sums[2], sums[3])
     received = lax.all_to_all(blocks, "z", 0, 0, tiled=True)
-    grad_input, weight_grad, bias_grad = finish(received)
+    half, bias_grad = finish_terms(received)
+    other = send(half, "core", C, 1)
+    weight_grad = jnp.where(core == 0, jnp.concatenate([half, other]), jnp.concatenate([other, half]))
+    grad_input = finish_grad(received)
     return output, grad_input, weight_grad, bias_grad.reshape(T)
 
 

time: 97.2 us -> 95.8 us (0.986)
  blocking collectives: 39.1 us -> 36.5 us
  starting transfers between devices: 16.4 us -> 18.3 us
  waiting for transfers between devices: 25 us -> 24 us
    all_to_all x1, blocking collectives: 20.7 us -> 18.1 us  [body(): received = lax.all_to_all(blocks, 'z', 0, 0, tiled=True)]
    ppermute x15 -> x16, starting transfers between devices: 16.4 us -> 18.3 us  [send(): return lax.ppermute(array, axis, shift(axis, size, by))]
    unnamed x12 -> x8, local copies, waits for them, and re-layouts: 3.52 us -> 2.21 us
    ppermute x15 -> x16, waiting for transfers between devices: 25 us -> 24 us  [send(): return lax.ppermute(array, axis, shift(axis, size, by))]
    pallas_call x6 -> x7, Pallas kernels: 6.22 us -> 6.59 us  [the longest x1 3.52 us: densify(): pl.pallas_call(densify_kernel, in_specs=[SMEM, VMEM], out_specs=[VMEM] *...]
  transfers between devices with their start and end apart: 15 -> 16, of which waited for: 8 -> 9; matrix products, arithmetic and copies ran while one was open for 0% -> 1% of each run, Pallas kernels for 9% -> 10%
where the time goes in v4:
time: 95.8 us; the launch traced here: 95.5 us
  blocking collectives  36.5 us (38%)
  waiting for transfers between devices  24 us (25%)
  starting transfers between devices  18.3 us (19%)
  Pallas kernels  10.9 us (11%)
  local copies, waits for them, and re-layouts  3.75 us (4%)
  between operations  1.43 us (1%)
    ppermute x16, waiting for transfers between devices, send(): return lax.ppermute(array, axis, shift(axis, size, by))  24 us
    all_to_all x1, blocking collectives, body(): line = lax.all_to_all(spread, 'z', 0, 0, tiled=True)  18.4 us
    ppermute x16, starting transfers between devices, send(): return lax.ppermute(array, axis, shift(axis, size, by))  18.3 us
    all_to_all x1, blocking collectives, body(): received = lax.all_to_all(blocks, 'z', 0, 0, tiled=True)  18.1 us
    pallas_call x1, Pallas kernels, densify(): pl.pallas_call(densify_kernel, in_specs=[SMEM, VMEM], out_specs=[VMEM] *...  3.52 us
    pallas_call x3, Pallas kernels, forward(): pl.pallas_call(kernel, in_specs=[VMEM] * (2 + count + len(extra)), out_sp...  2.68 us
    unnamed x8, local copies, waits for them, and re-layouts  2.21 us
  transfers between devices with their start and end apart: 16, of which 9 were waited for; matrix products, arithmetic and copies ran while one was open for 1% of the time, Pallas kernels for 10%

profile of v4, /device:TPU:3, one launch (start us, length us, event | category | flops | bytes accessed | tf_op | source)
XLA Modules:
  0.0 95.5 jit_solution(8244187871874231885)
XLA Ops:
  0.6 0.8 broadcast_in_dim.3
  1.4 18.4 %all_to_all.10.refs_2_ = bf16[8,128,128]{2,1,0:T(8,128)(2,1)S(1)} all-to-all(bf16[8,128,128]{2,1,0:T(8,128)(2,1)S(1)} %broadcast_in_dim.3), channel_id=1, replica_groups=mesh['z'=8,'x'=4,'core'=2,'rep'=4] {'z'}, dimensions={0} | all-to-all | bytes 524288 | tf_op jit(solution)/shard_map/all_to_all | solution.py:298
  19.8 2.5 %collective-permute-start.1 = (bf16[8,128,128]{2,1,0:T(8,128)(2,1)S(1)}, bf16[8,128,128]{2,1,0:T(8,128)(2,1)S(1)}, u32[]{:S(2)}, u32[]{:S(2)}) collective-permute-start(bf16[8,128,128]{2,1,0:T(8,128)(2,1)S(1)} %all_to_all.10.refs_2_), channel_id=1, source_target_pairs={{0,4},{4,0},{1,5},{5,1},{2,6},{6,2},{3,7},{7,3},{8,12},{12,8},{9,1... | collective-permute-start | bytes 786440 | tf_op jit(solution)/shard_map/ppermute | solution.py:40
  22.2 1.8 %collective-permute-start.5 = (bf16[8,128,128]{2,1,0:T(8,128)(2,1)S(1)}, bf16[8,128,128]{2,1,0:T(8,128)(2,1)S(1)}, u32[]{:S(2)}, u32[]{:S(2)}) collective-permute-start(bf16[8,128,128]{2,1,0:T(8,128)(2,1)S(1)} %all_to_all.10.refs_2_), channel_id=1, source_target_pairs={{0,16},{8,24},{16,0},{24,8},{1,17},{9,25},{17,1},{25,9},{2,18},{10... | collective-permute-start | bytes 786440 | tf_op jit(solution)/shard_map/ppermute | solution.py:40
  24.1 0.0 collective-permute-start.3
  24.1 1.5 %collective-permute-start = (bf16[8,128,128]{2,1,0:T(8,128)(2,1)S(1)}, bf16[8,128,128]{2,1,0:T(8,128)(2,1)S(1)}, u32[]{:S(2)}, u32[]{:S(2)}) collective-permute-start(bf16[8,128,128]{2,1,0:T(8,128)(2,1)S(1)} %all_to_all.10.refs_2_), channel_id=1, source_target_pairs={{0,24},{8,0},{16,8},{24,16},{1,25},{9,1},{17,9},{25,17},{2,26},{10... | collective-permute-start | bytes 786440 | tf_op jit(solution)/shard_map/ppermute | solution.py:40
  26.2 0.8 concatenate.10.me_ref
  27.0 2.2 %copy-done = bf16[1,1,128,128,128]{4,3,2,1,0:T(8,128)(2,1)S(1)} copy-done((bf16[1,1,128,128,128]{4,3,2,1,0:T(8,128)(2,1)S(1)}, bf16[1,1,128,128,128]{4,3,2,1,0:T(8,128)(2,1)}, u32[]{:S(2)}) %copy-start) | copy-done | bytes 4194328
  29.1 3.5 %densify.1 = (bf16[32,512,128]{2,1,0:T(8,128)(2,1)S(1)}, bf16[32,512,128]{2,1,0:T(8,128)(2,1)S(1)}) custom-call(s32[260]{0:T(512)S(1)} %concatenate.10.me_ref, bf16[128,128,128]{2,1,0:T(8,128)(2,1)S(1)} %bitcast.11), custom_call_target="tpu_custom_call" | custom-call | bytes 12582912 | tf_op jit(solution)/shard_map/densify/pallas_call | solution.py:73
  32.7 0.7 forward.3.token_ref.refs_7_
  33.4 0.0 collective-permute-done.5.block_ref
  33.4 1.8 %collective-permute-start.6 = (bf16[8,128,128]{2,1,0:T(8,128)(2,1)S(1)}, bf16[8,128,128]{2,1,0:T(8,128)(2,1)S(1)}, u32[]{:S(2)}, u32[]{:S(2)}) collective-permute-start(bf16[8,128,128]{2,1,0:T(8,128)(2,1)S(1)} %tie.4.refs_4_), channel_id=1, source_target_pairs={{0,4},{4,0},{1,5},{5,1},{2,6},{6,2},{3,7},{7,3},{8,12},{12,8},{9,1... | collective-permute-start | bytes 786440 | tf_op jit(solution)/shard_map/ppermute | solution.py:40
  35.3 2.1 %collective-permute-done.3.refs_2_ = bf16[8,128,128]{2,1,0:T(8,128)(2,1)S(1)} collective-permute-done((bf16[8,128,128]{2,1,0:T(8,128)(2,1)S(1)}, bf16[8,128,128]{2,1,0:T(8,128)(2,1)S(1)}, u32[]{:S(2)}, u32[]{:S(2)}) %collective-permute-start.3) | collective-permute-done | bytes 262176 | tf_op jit(solution)/shard_map/ppermute | solution.py:40
  37.4 0.8 collective-permute-start.4
  38.2 0.0 collective-permute-done.block_ref
  38.2 0.1 collective-permute-start.2
  38.3 1.1 %collective-permute-done.4.refs_3_ = bf16[8,128,128]{2,1,0:T(8,128)(2,1)S(1)} collective-permute-done((bf16[8,128,128]{2,1,0:T(8,128)(2,1)S(1)}, bf16[8,128,128]{2,1,0:T(8,128)(2,1)S(1)}, u32[]{:S(2)}, u32[]{:S(2)}) %collective-permute-start.4) | collective-permute-done | bytes 262176 | tf_op jit(solution)/shard_map/ppermute | solution.py:40
  39.3 1.5 %forward.4.refs_3_ = f32[512,128]{1,0:T(8,128)S(1)} custom-call(bf16[32,512,128]{2,1,0:T(8,128)(2,1)S(1)} %get-tuple-element.11.refs_0_.mine_ref, bf16[32,512,128]{2,1,0:T(8,128)(2,1)S(1)} %get-tuple-element.12.refs_1_.block_ref, bf16[8,128,128]{2,1,0:T(8,128)(2,1)S(1)} %collective-permute-done.3.refs_2_, ...), custom_call_target="tpu_custom_call" | custom-call | flops 671088640 | bytes 5242880 | tf_op jit(solution)/shard_map/forward/pallas_call | solution.py:105
  40.9 0.4 forward.5.p0.token_ref
  41.3 0.0 copy-start.2
  41.3 0.0 copy-start.3
  41.4 0.5 collective-permute-start.10
  41.8 1.3 %collective-permute-start.7 = (bf16[640,128]{1,0:T(8,128)(2,1)S(1)}, bf16[640,128]{1,0:T(8,128)(2,1)S(1)}, u32[]{:S(2)}, u32[]{:S(2)}) collective-permute-start(bf16[640,128]{1,0:T(8,128)(2,1)S(1)} %forward.5.p0.token_ref), channel_id=1, source_target_pairs={{0,1},{1,2},{2,3},{3,0},{4,5},{5,6},{6,7},{7,4},{8,9},{9,10},{10,1... | collective-permute-start | bytes 491528 | tf_op jit(solution)/shard_map/ppermute | solution.py:40
  43.1 2.6 %collective-permute-start.8 = (bf16[640,128]{1,0:T(8,128)(2,1)S(1)}, bf16[640,128]{1,0:T(8,128)(2,1)S(1)}, u32[]{:S(2)}, u32[]{:S(2)}) collective-permute-start(bf16[640,128]{1,0:T(8,128)(2,1)S(1)} %forward.5.p0.token_ref), channel_id=1, source_target_pairs={{0,2},{1,3},{2,0},{3,1},{4,6},{5,7},{6,4},{7,5},{8,10},{9,11},{10,... | collective-permute-start | bytes 491528 | tf_op jit(solution)/shard_map/ppermute | solution.py:40
  45.7 1.1 %collective-permute-start.9 = (bf16[640,128]{1,0:T(8,128)(2,1)S(1)}, bf16[640,128]{1,0:T(8,128)(2,1)S(1)}, u32[]{:S(2)}, u32[]{:S(2)}) collective-permute-start(bf16[640,128]{1,0:T(8,128)(2,1)S(1)} %forward.5.p0.token_ref), channel_id=1, source_target_pairs={{0,3},{1,0},{2,1},{3,2},{4,7},{5,4},{6,5},{7,6},{8,11},{9,8},{10,9... | collective-permute-start | bytes 491528 | tf_op jit(solution)/shard_map/ppermute | solution.py:40
  46.8 0.1 pad_add_fusion.me_ref
  46.9 1.9 %collective-permute-done.7.p1 = bf16[640,128]{1,0:T(8,128)(2,1)S(1)} collective-permute-done((bf16[640,128]{1,0:T(8,128)(2,1)S(1)}, bf16[640,128]{1,0:T(8,128)(2,1)S(1)}, u32[]{:S(2)}, u32[]{:S(2)}) %collective-permute-start.7) | collective-permute-done | bytes 163872 | tf_op jit(solution)/shard_map/ppermute | solution.py:40
  48.8 4.6 %collective-permute-done.8.p2 = bf16[640,128]{1,0:T(8,128)(2,1)S(1)} collective-permute-done((bf16[640,128]{1,0:T(8,128)(2,1)S(1)}, bf16[640,128]{1,0:T(8,128)(2,1)S(1)}, u32[]{:S(2)}, u32[]{:S(2)}) %collective-permute-start.8) | collective-permute-done | bytes 163872 | tf_op jit(solution)/shard_map/ppermute | solution.py:40
  53.5 1.4 %middle.1 = (bf16[128,128]{1,0:T(8,128)(2,1)}, bf16[592,128]{1,0:T(8,128)(2,1)S(1)}, f32[64,128]{1,0:T(8,128)S(1)}) custom-call(s32[4]{0:T(128)S(1)} %pad_add_fusion.me_ref, bf16[640,128]{1,0:T(8,128)(2,1)S(1)} %forward.5.p0.token_ref, bf16[640,128]{1,0:T(8,128)(2,1)S(1)} %collective-permute-done.7.p1, bf16[640,128]{1,0:T(8,128)(2,1)S(1)} %collective-permute-done.8.p2, ...), custom_call_target="tpu_custom_call" | custom-call | flops 50331648 | bytes 1048576 | tf_op jit(solution)/shard_map/middle/pallas_call | solution.py:171
  54.9 1.0 collective-permute-start.11
  55.8 1.0 %collective-permute-done.11.got_ref = bf16[592,128]{1,0:T(8,128)(2,1)S(1)} collective-permute-done((bf16[592,128]{1,0:T(8,128)(2,1)S(1)}, bf16[592,128]{1,0:T(8,128)(2,1)S(1)}, u32[]{:S(2)}, u32[]{:S(2)}) %collective-permute-start.11) | collective-permute-done | bytes 151584 | tf_op jit(solution)/shard_map/ppermute | solution.py:40
  56.9 0.5 backward.7
  57.3 0.3 collective-permute-start.14
  57.7 0.5 backward.6
  58.1 2.0 %collective-permute-start.13 = (bf16[1104,128]{1,0:T(8,128)(2,1)S(1)}, bf16[1104,128]{1,0:T(8,128)(2,1)S(1)}, u32[]{:S(2)}, u32[]{:S(2)}) collective-permute-start(bf16[1104,128]{1,0:T(8,128)(2,1)S(1)} %backward.6), channel_id=1, source_target_pairs={{0,16},{8,24},{16,0},{24,8},{1,17},{9,25},{17,1},{25,9},{2,18},{10... | collective-permute-start | bytes 847880 | tf_op jit(solution)/shard_map/ppermute | solution.py:40
  60.1 0.5 backward.5
  60.6 0.5 collective-permute-start.12
  61.1 0.5 backward.4.r0
  61.5 3.8 %collective-permute-done.14.r3 = bf16[1104,128]{1,0:T(8,128)(2,1)S(1)} collective-permute-done((bf16[1104,128]{1,0:T(8,128)(2,1)S(1)}, bf16[1104,128]{1,0:T(8,128)(2,1)S(1)}, u32[]{:S(2)}, u32[]{:S(2)}) %collective-permute-start.14) | collective-permute-done | bytes 282656 | tf_op jit(solution)/shard_map/ppermute | solution.py:40
  65.4 2.2 %collective-permute-done.13.r2 = bf16[1104,128]{1,0:T(8,128)(2,1)S(1)} collective-permute-done((bf16[1104,128]{1,0:T(8,128)(2,1)S(1)}, bf16[1104,128]{1,0:T(8,128)(2,1)S(1)}, u32[]{:S(2)}, u32[]{:S(2)}) %collective-permute-start.13) | collective-permute-done | bytes 282656 | tf_op jit(solution)/shard_map/ppermute | solution.py:40
  67.6 7.0 %collective-permute-done.12.r1 = bf16[1104,128]{1,0:T(8,128)(2,1)S(1)} collective-permute-done((bf16[1104,128]{1,0:T(8,128)(2,1)S(1)}, bf16[1104,128]{1,0:T(8,128)(2,1)S(1)}, u32[]{:S(2)}, u32[]{:S(2)}) %collective-permute-start.12) | collective-permute-done | bytes 282656 | tf_op jit(solution)/shard_map/ppermute | solution.py:40
  74.6 0.2 line_sum.1
  74.8 18.1 %all_to_all.11.in_ref = bf16[8,208,128]{2,1,0:T(8,128)(2,1)S(1)} all-to-all(bf16[8,208,128]{2,1,0:T(8,128)(2,1)S(1)} %line_sum.1), channel_id=1, replica_groups=mesh['z'=8,'x'=4,'core'=2,'rep'=4] {'z'}, dimensions={0} | all-to-all | bytes 851968 | tf_op jit(solution)/shard_map/all_to_all | solution.py:322
  92.9 0.5 finish_terms.1
  93.4 0.6 collective-permute-start.15
  94.0 0.7 finish_grad.1
  94.8 0.1 collective-permute-done.15
  94.9 0.6 maximum_select_fusion
  (13 shorter events, 0.0 us)
Async XLA Ops:
  19.8 12.9 %collective-permute-start.1 = (bf16[8,128,128]{2,1,0:T(8,128)(2,1)S(1)}, bf16[8,128,128]{2,1,0:T(8,128)(2,1)S(1)}, u32[]{:S(2)}, u32[]{:S(2)}) collective-permute-start(bf16[8,128,128]{2,1,0:T(8,128)(2,1)S(1)} %all_to_all.10.refs_2_), channel_id=1, source_target_pairs={{0,4},{4,0},{1,5},{5,1},{2,6},{6,2},{3,7},{7,3},{8,12},{12,8},{9,1... | collective-permute-start | bytes 786440 | tf_op jit(solution)/shard_map/ppermute | solution.py:40
  22.2 11.2 %collective-permute-start.5 = (bf16[8,128,128]{2,1,0:T(8,128)(2,1)S(1)}, bf16[8,128,128]{2,1,0:T(8,128)(2,1)S(1)}, u32[]{:S(2)}, u32[]{:S(2)}) collective-permute-start(bf16[8,128,128]{2,1,0:T(8,128)(2,1)S(1)} %all_to_all.10.refs_2_), channel_id=1, source_target_pairs={{0,16},{8,24},{16,0},{24,8},{1,17},{9,25},{17,1},{25,9},{2,18},{10... | collective-permute-start | bytes 786440 | tf_op jit(solution)/shard_map/ppermute | solution.py:40
  24.1 13.3 %collective-permute-start.3 = (bf16[8,128,128]{2,1,0:T(8,128)(2,1)S(1)}, bf16[8,128,128]{2,1,0:T(8,128)(2,1)S(1)}, u32[]{:S(2)}, u32[]{:S(2)}) collective-permute-start(bf16[8,128,128]{2,1,0:T(8,128)(2,1)S(1)} %all_to_all.10.refs_2_), channel_id=1, source_target_pairs={{0,8},{8,16},{16,24},{24,0},{1,9},{9,17},{17,25},{25,1},{2,10},{10... | collective-permute-start | bytes 786440 | tf_op jit(solution)/shard_map/ppermute | solution.py:40
  24.1 14.1 %collective-permute-start = (bf16[8,128,128]{2,1,0:T(8,128)(2,1)S(1)}, bf16[8,128,128]{2,1,0:T(8,128)(2,1)S(1)}, u32[]{:S(2)}, u32[]{:S(2)}) collective-permute-start(bf16[8,128,128]{2,1,0:T(8,128)(2,1)S(1)} %all_to_all.10.refs_2_), channel_id=1, source_target_pairs={{0,24},{8,0},{16,8},{24,16},{1,25},{9,1},{17,9},{25,17},{2,26},{10... | collective-permute-start | bytes 786440 | tf_op jit(solution)/shard_map/ppermute | solution.py:40
  27.0 2.2 %copy-start = (bf16[1,1,128,128,128]{4,3,2,1,0:T(8,128)(2,1)S(1)}, bf16[1,1,128,128,128]{4,3,2,1,0:T(8,128)(2,1)}, u32[]{:S(2)}) copy-start(bf16[1,1,128,128,128]{4,3,2,1,0:T(8,128)(2,1)} %param.12) | copy-start | bytes 12582916
  33.4 4.8 %collective-permute-start.6 = (bf16[8,128,128]{2,1,0:T(8,128)(2,1)S(1)}, bf16[8,128,128]{2,1,0:T(8,128)(2,1)S(1)}, u32[]{:S(2)}, u32[]{:S(2)}) collective-permute-start(bf16[8,128,128]{2,1,0:T(8,128)(2,1)S(1)} %tie.4.refs_4_), channel_id=1, source_target_pairs={{0,4},{4,0},{1,5},{5,1},{2,6},{6,2},{3,7},{7,3},{8,12},{12,8},{9,1... | collective-permute-start | bytes 786440 | tf_op jit(solution)/shard_map/ppermute | solution.py:40
  37.4 1.9 %collective-permute-start.4 = (bf16[8,128,128]{2,1,0:T(8,128)(2,1)S(1)}, bf16[8,128,128]{2,1,0:T(8,128)(2,1)S(1)}, u32[]{:S(2)}, u32[]{:S(2)}) collective-permute-start(bf16[8,128,128]{2,1,0:T(8,128)(2,1)S(1)} %collective-permute-done.3.refs_2_), channel_id=1, source_target_pairs={{0,4},{4,0},{1,5},{5,1},{2,6},{6,2},{3,7},{7,3},{8,12},{12,8},{9,1... | collective-permute-start | bytes 786440 | tf_op jit(solution)/shard_map/ppermute | solution.py:40
  38.2 2.7 %copy-start.1 = (bf16[128,128]{1,0:T(8,128)(2,1)S(1)}, bf16[128,128]{1,0:T(8,128)(2,1)}, u32[]{:S(2)}) copy-start(bf16[128,128]{1,0:T(8,128)(2,1)} %refs_4_.1) | copy-start | bytes 98308
  38.2 2.7 %collective-permute-start.2 = (bf16[8,128,128]{2,1,0:T(8,128)(2,1)S(1)}, bf16[8,128,128]{2,1,0:T(8,128)(2,1)S(1)}, u32[]{:S(2)}, u32[]{:S(2)}) collective-permute-start(bf16[8,128,128]{2,1,0:T(8,128)(2,1)S(1)} %tie.3.refs_6_), channel_id=1, source_target_pairs={{0,4},{4,0},{1,5},{5,1},{2,6},{6,2},{3,7},{7,3},{8,12},{12,8},{9,1... | collective-permute-start | bytes 786440 | tf_op jit(solution)/shard_map/ppermute | solution.py:40
  41.3 12.1 %copy-start.2 = (bf16[128,128]{1,0:T(8,128)(2,1)S(1)}, bf16[128,128]{1,0:T(8,128)(2,1)}, u32[]{:S(2)}) copy-start(bf16[128,128]{1,0:T(8,128)(2,1)} %weight_ref.1) | copy-start | bytes 98308
  41.3 12.1 %copy-start.3 = (f32[128]{0:T(128)S(1)}, f32[128]{0:T(128)}, u32[]{:S(2)}) copy-start(f32[128]{0:T(128)} %param.10) | copy-start | bytes 1540
  41.4 15.5 %collective-permute-start.10 = (bf16[32,512,128]{2,1,0:T(8,128)(2,1)S(1)}, bf16[32,512,128]{2,1,0:T(8,128)(2,1)S(1)}, u32[]{:S(2)}, u32[]{:S(2)}) collective-permute-start(bf16[32,512,128]{2,1,0:T(8,128)(2,1)S(1)} %tie.5), channel_id=1, source_target_pairs={{0,4},{4,0},{1,5},{5,1},{2,6},{6,2},{3,7},{7,3},{8,12},{12,8},{9,1... | collective-permute-start | bytes 12582920 | tf_op jit(solution)/shard_map/ppermute | solution.py:40
  41.8 7.0 %collective-permute-start.7 = (bf16[640,128]{1,0:T(8,128)(2,1)S(1)}, bf16[640,128]{1,0:T(8,128)(2,1)S(1)}, u32[]{:S(2)}, u32[]{:S(2)}) collective-permute-start(bf16[640,128]{1,0:T(8,128)(2,1)S(1)} %forward.5.p0.token_ref), channel_id=1, source_target_pairs={{0,1},{1,2},{2,3},{3,0},{4,5},{5,6},{6,7},{7,4},{8,9},{9,10},{10,1... | collective-permute-start | bytes 491528 | tf_op jit(solution)/shard_map/ppermute | solution.py:40
  43.1 10.3 %collective-permute-start.8 = (bf16[640,128]{1,0:T(8,128)(2,1)S(1)}, bf16[640,128]{1,0:T(8,128)(2,1)S(1)}, u32[]{:S(2)}, u32[]{:S(2)}) collective-permute-start(bf16[640,128]{1,0:T(8,128)(2,1)S(1)} %forward.5.p0.token_ref), channel_id=1, source_target_pairs={{0,2},{1,3},{2,0},{3,1},{4,6},{5,7},{6,4},{7,5},{8,10},{9,11},{10,... | collective-permute-start | bytes 491528 | tf_op jit(solution)/shard_map/ppermute | solution.py:40
  45.7 7.7 %collective-permute-start.9 = (bf16[640,128]{1,0:T(8,128)(2,1)S(1)}, bf16[640,128]{1,0:T(8,128)(2,1)S(1)}, u32[]{:S(2)}, u32[]{:S(2)}) collective-permute-start(bf16[640,128]{1,0:T(8,128)(2,1)S(1)} %forward.5.p0.token_ref), channel_id=1, source_target_pairs={{0,3},{1,0},{2,1},{3,2},{4,7},{5,4},{6,5},{7,6},{8,11},{9,8},{10,9... | collective-permute-start | bytes 491528 | tf_op jit(solution)/shard_map/ppermute | solution.py:40
  54.9 2.0 %collective-permute-start.11 = (bf16[592,128]{1,0:T(8,128)(2,1)S(1)}, bf16[592,128]{1,0:T(8,128)(2,1)S(1)}, u32[]{:S(2)}, u32[]{:S(2)}) collective-permute-start(bf16[592,128]{1,0:T(8,128)(2,1)S(1)} %get-tuple-element.14.give_ref), channel_id=1, source_target_pairs={{0,4},{4,0},{1,5},{5,1},{2,6},{6,2},{3,7},{7,3},{8,12},{12,8},{9,1... | collective-permute-start | bytes 454664 | tf_op jit(solution)/shard_map/ppermute | solution.py:40
  57.3 8.0 %collective-permute-start.14 = (bf16[1104,128]{1,0:T(8,128)(2,1)S(1)}, bf16[1104,128]{1,0:T(8,128)(2,1)S(1)}, u32[]{:S(2)}, u32[]{:S(2)}) collective-permute-start(bf16[1104,128]{1,0:T(8,128)(2,1)S(1)} %backward.7), channel_id=1, source_target_pairs={{0,8},{8,16},{16,24},{24,0},{1,9},{9,17},{17,25},{25,1},{2,10},{10... | collective-permute-start | bytes 847880 | tf_op jit(solution)/shard_map/ppermute | solution.py:40
  58.1 9.5 %collective-permute-start.13 = (bf16[1104,128]{1,0:T(8,128)(2,1)S(1)}, bf16[1104,128]{1,0:T(8,128)(2,1)S(1)}, u32[]{:S(2)}, u32[]{:S(2)}) collective-permute-start(bf16[1104,128]{1,0:T(8,128)(2,1)S(1)} %backward.6), channel_id=1, source_target_pairs={{0,16},{8,24},{16,0},{24,8},{1,17},{9,25},{17,1},{25,9},{2,18},{10... | collective-permute-start | bytes 847880 | tf_op jit(solution)/shard_map/ppermute | solution.py:40
  60.6 14.1 %collective-permute-start.12 = (bf16[1104,128]{1,0:T(8,128)(2,1)S(1)}, bf16[1104,128]{1,0:T(8,128)(2,1)S(1)}, u32[]{:S(2)}, u32[]{:S(2)}) collective-permute-start(bf16[1104,128]{1,0:T(8,128)(2,1)S(1)} %backward.5), channel_id=1, source_target_pairs={{0,24},{8,0},{16,8},{24,16},{1,25},{9,1},{17,9},{25,17},{2,26},{10... | collective-permute-start | bytes 847880 | tf_op jit(solution)/shard_map/ppermute | solution.py:40
  93.4 1.5 %collective-permute-start.15 = (f32[64,128]{1,0:T(8,128)S(1)}, f32[64,128]{1,0:T(8,128)S(1)}, u32[]{:S(2)}, u32[]{:S(2)}) collective-permute-start(f32[64,128]{1,0:T(8,128)S(1)} %get-tuple-element.16), channel_id=1, source_target_pairs={{0,4},{4,0},{1,5},{5,1},{2,6},{6,2},{3,7},{7,3},{8,12},{12,8},{9,1... | collective-permute-start | bytes 98312 | tf_op jit(solution)/shard_map/ppermute | solution.py:40

commit v5 on v4

--- a/solution.py
+++ b/solution.py
@@ -142,7 +142,7 @@
     ref[start:start + 16, :] = packed.astype(BF16)
 
 
-def middle_kernel(me_ref, p0, p1, p2, p3, weight_ref, bias_ref, out_ref, give_ref, keep_ref, pre, cot, halves):
+def middle_kernel(me_ref, p0, p1, p2, p3, weight_ref, bias_ref, own_ref, give_ref, keep_ref, pre, cot, halves):
     core, rep = me_ref[1], me_ref[2]
     for n, source in enumerate((p0, p1, p2, p3)):
         cot[(rep - n + Q) % Q] = source[PANEL:]
@@ -154,8 +154,7 @@
     sig = jax.nn.sigmoid(preact)
     cotangent = cot[...].reshape(PANEL, T).astype(F32)
     grad_pre = (cotangent * sig * (1.0 + preact * (1.0 - sig))).astype(BF16)
-    own = pre[rep]
-    out_ref[...] = (own * jax.nn.sigmoid(own)).astype(BF16)
+    own_ref[...] = pre[rep]
     back = lax.dot_general(weight_ref[...], grad_pre, (((1,), (1,)), ((), ())), preferred_element_type=F32)
     for r in range(Q):
         give_ref[r * T:(r + 1) * T] = back[:, r * T:(r + 1) * T].astype(BF16)
@@ -173,7 +172,7 @@
         in_specs=[SMEM] + [VMEM] * 6,
         out_specs=[VMEM] * 3,
         out_shape=[
-            jax.ShapeDtypeStruct((T, T), BF16),
+            jax.ShapeDtypeStruct((T, T), F32),
             jax.ShapeDtypeStruct((PANEL + PAY, T), BF16),
             jax.ShapeDtypeStruct((HALF, T), F32),
         ],
@@ -193,8 +192,14 @@
     return pair[0:1] + pair[1:2]
 
 
-def backward(mine, other, give, got, keep, chunk):
-    def kernel(mine_ref, other_ref, give_ref, got_ref, keep_ref, out_ref):
+def backward(mine, other, give, got, keep, chunk, own=None):
+    def kernel(mine_ref, other_ref, give_ref, got_ref, keep_ref, *refs):
+        if own is None:
+            out_ref, = refs
+        else:
+            own_ref, out_ref, layer_ref = refs
+            preact = own_ref[...]
+            layer_ref[...] = (preact * jax.nn.sigmoid(preact)).astype(BF16)
         wide = lambda ref: jnp.concatenate([ref[r * T:(r + 1) * T] for r in range(Q)], axis=1)
         sides = [(wide(give_ref), mine_ref), (wide(got_ref), other_ref)]
         for z in range(0, Z, 2):
@@ -212,15 +217,16 @@
         bias = bias_of(give_ref, PANEL + HALF) + bias_of(got_ref, PANEL + HALF)
         pack_bias(out_ref, Z * T + HALF, bias)
 
-    return pl.pallas_call(
-        kernel,
-        in_specs=[VMEM] * 5,
-        out_specs=VMEM,
-        out_shape=jax.ShapeDtypeStruct((MSG, T), BF16),
+    extra = [] if own is None else [own]
+    return pl.pallas_call(
+        kernel,
+        in_specs=[VMEM] * (5 + len(extra)),
+        out_specs=[VMEM] * (1 + len(extra)),
+        out_shape=[jax.ShapeDtypeStruct((MSG, T), BF16)] + [jax.ShapeDtypeStruct((T, T), BF16)] * len(extra),
         compiler_params=params(16),
         cost_estimate=cost(4 * PANEL * T * T * Z, 2**21),
         name="backward",
-    )(mine, other, give, got, keep)
+    )(mine, other, give, got, keep, *extra)
 
 
 def line_sum(s0, s1, s2, s3):
@@ -249,13 +255,31 @@
 
 
 def finish_terms(received):
-    def kernel(in_ref, half_ref, bias_ref):
+    def kernel(in_ref, half_ref):
         total = in_ref[0, T:T + HALF].astype(F32)
+        for z in range(1, Z):
+            total += in_ref[z, T:T + HALF].astype(F32)
+        half_ref[...] = total * SCALE
+
+    return pl.pallas_call(
+        kernel,
+        in_specs=[VMEM],
+        out_specs=VMEM,
+        out_shape=jax.ShapeDtypeStruct((HALF, T), F32),
+        compiler_params=params(16),
+        cost_estimate=cost(0, 2**18),
+        name="finish_terms",
+    )(received)
+
+
+def finish_grad(received):
+    def kernel(in_ref, grad_ref, bias_ref):
+        total = in_ref[0, :T].astype(F32)
         bias = bias_of(in_ref.at[0], T + HALF)
         for z in range(1, Z):
-            total += in_ref[z, T:T + HALF].astype(F32)
+            total += in_ref[z, :T].astype(F32)
             bias += bias_of(in_ref.at[z], T + HALF)
-        half_ref[...] = total * SCALE
+        grad_ref[...] = total.T.astype(BF16)
         bias_ref[...] = bias * SCALE
 
     return pl.pallas_call(
@@ -263,27 +287,9 @@
         in_specs=[VMEM],
         out_specs=[VMEM] * 2,
         out_shape=[
-            jax.ShapeDtypeStruct((HALF, T), F32),
+            jax.ShapeDtypeStruct((T, T), BF16),
             jax.ShapeDtypeStruct((1, T), F32),
         ],
-        compiler_params=params(16),
-        cost_estimate=cost(0, 2**18),
-        name="finish_terms",
-    )(received)
-
-
-def finish_grad(received):
-    def kernel(in_ref, grad_ref):
-        total = in_ref[0, :T].astype(F32)
-        for z in range(1, Z):
-            total += in_ref[z, :T].astype(F32)
-        grad_ref[...] = total.T.astype(BF16)
-
-    return pl.pallas_call(
-        kernel,
-        in_specs=[VMEM],
-        out_specs=VMEM,
-        out_shape=jax.ShapeDtypeStruct((T, T), BF16),
         compiler_params=params(16),
         cost_estimate=cost(0, 2**22),
         name="finish_grad",
@@ -301,29 +307,29 @@
     begun = forward(halves, near, None, F32)
     far = []
     for n in range(1, X):
-        block = send(line, "x", X, n)
-        if n > 1:
-            block = tie(block, begun)
+        block = tie(send(line, "x", X, n), begun)
         far += [(0, n, block), (1, n, send(block, "core", C, 1))]
-    begun = forward(halves, far[:-1], begun, F32)
-    partial = forward(halves, far[-1:], begun, BF16, cotangent)
+    late = [far[3], far[5]]
+    begun = forward(halves, far[:3] + far[4:5], begun, F32)
+    partial = forward(halves, late, begun, BF16, cotangent)
 
     partials = [partial] + [send(partial, "rep", Q, n) for n in range(1, Q)]
     mine, theirs = halves
     fellow = send(tie(theirs, partial), "core", C, 1)
-    output, give, keep = middle(place, partials, weight, bias_terms.reshape(1, T))
+    own, give, keep = middle(place, partials, weight, bias_terms.reshape(1, T))
     got = send(give, "core", C, 1)
 
     sums = {}
-    for n in (1, 2, 3, 0):
-        total = backward(mine, fellow, give, got, keep, n)
-        sums[n] = send(total, "x", X, -n) if n else total
-    blocks = line_sum(sums[0], sums[1], sums[2], sums[3])
+    for n in (1, 2, 3):
+        total, = backward(mine, fellow, give, got, keep, n)
+        sums[n] = send(total, "x", X, -n)
+    sums[0], output = backward(mine, fellow, give, got, keep, 0, own)
+    blocks = line_sum(sums[0], sums[3], sums[2], sums[1])
     received = lax.all_to_all(blocks, "z", 0, 0, tiled=True)
-    half, bias_grad = finish_terms(received)
+    half = finish_terms(received)
     other = send(half, "core", C, 1)
     weight_grad = jnp.where(core == 0, jnp.concatenate([half, other]), jnp.concatenate([other, half]))
-    grad_input = finish_grad(received)
+    grad_input, bias_grad = finish_grad(received)
     return output, grad_input, weight_grad, bias_grad.reshape(T)
 
 

time: 95.8 us -> 95 us (level)
  waiting for transfers between devices: 24 us -> 21.5 us
  starting transfers between devices: 18.3 us -> 19.3 us
    ppermute x16, waiting for transfers between devices: 24 us -> 21.5 us  [send(): return lax.ppermute(array, axis, shift(axis, size, by))]
    pallas_call x1, Pallas kernels: 3.52 us -> 4.55 us  [densify(): pl.pallas_call(densify_kernel, in_specs=[SMEM, VMEM], out_specs=[VMEM] *...]
    ppermute x16, starting transfers between devices: 18.3 us -> 19.3 us  [send(): return lax.ppermute(array, axis, shift(axis, size, by))]
  transfers between devices with their start and end apart: 16 -> 16, of which waited for: 9 -> 8; matrix products, arithmetic and copies ran while one was open for 1% -> 1% of each run, Pallas kernels for 10% -> 11%
where the time goes in v5:
time: 95 us; the launch traced here: 94.7 us
  blocking collectives  36.5 us (38%)
  waiting for transfers between devices  21.5 us (23%)
  starting transfers between devices  19.3 us (20%)
  Pallas kernels  11.5 us (12%)
  local copies, waits for them, and re-layouts  3.75 us (4%)
  between operations  1.46 us (2%)
    ppermute x16, waiting for transfers between devices, send(): return lax.ppermute(array, axis, shift(axis, size, by))  21.5 us
    ppermute x16, starting transfers between devices, send(): return lax.ppermute(array, axis, shift(axis, size, by))  19.3 us
    all_to_all x1, blocking collectives, body(): line = lax.all_to_all(spread, 'z', 0, 0, tiled=True)  18.4 us
    all_to_all x1, blocking collectives, body(): received = lax.all_to_all(blocks, 'z', 0, 0, tiled=True)  18.1 us
    pallas_call x1, Pallas kernels, densify(): pl.pallas_call(densify_kernel, in_specs=[SMEM, VMEM], out_specs=[VMEM] *...  4.55 us
    pallas_call x3, Pallas kernels, forward(): pl.pallas_call(kernel, in_specs=[VMEM] * (2 + count + len(extra)), out_sp...  2.68 us
    pallas_call x4, Pallas kernels, backward(): pl.pallas_call(kernel, in_specs=[VMEM] * (5 + len(extra)), out_specs=[VME...  2.32 us
    unnamed x8, local copies, waits for them, and re-layouts  2.21 us
  transfers between devices with their start and end apart: 16, of which 8 were waited for; matrix products, arithmetic and copies ran while one was open for 1% of the time, Pallas kernels for 11%

profile of v5, /device:TPU:3, one launch (start us, length us, event | category | flops | bytes accessed | tf_op | source)
XLA Modules:
  0.0 94.7 jit_solution(15871017053462895715)
XLA Ops:
  0.6 0.8 broadcast_in_dim.3
  1.4 18.4 %all_to_all.10.refs_2_ = bf16[8,128,128]{2,1,0:T(8,128)(2,1)S(1)} all-to-all(bf16[8,128,128]{2,1,0:T(8,128)(2,1)S(1)} %broadcast_in_dim.3), channel_id=1, replica_groups=mesh['z'=8,'x'=4,'core'=2,'rep'=4] {'z'}, dimensions={0} | all-to-all | bytes 524288 | tf_op jit(solution)/shard_map/all_to_all | solution.py:304
  19.8 2.5 %collective-permute-start.1 = (bf16[8,128,128]{2,1,0:T(8,128)(2,1)S(1)}, bf16[8,128,128]{2,1,0:T(8,128)(2,1)S(1)}, u32[]{:S(2)}, u32[]{:S(2)}) collective-permute-start(bf16[8,128,128]{2,1,0:T(8,128)(2,1)S(1)} %all_to_all.10.refs_2_), channel_id=1, source_target_pairs={{0,4},{4,0},{1,5},{5,1},{2,6},{6,2},{3,7},{7,3},{8,12},{12,8},{9,1... | collective-permute-start | bytes 786440 | tf_op jit(solution)/shard_map/ppermute | solution.py:40
  22.2 1.2 %collective-permute-start.5 = (bf16[8,128,128]{2,1,0:T(8,128)(2,1)S(1)}, bf16[8,128,128]{2,1,0:T(8,128)(2,1)S(1)}, u32[]{:S(2)}, u32[]{:S(2)}) collective-permute-start(bf16[8,128,128]{2,1,0:T(8,128)(2,1)S(1)} %all_to_all.10.refs_2_), channel_id=1, source_target_pairs={{0,8},{8,16},{16,24},{24,0},{1,9},{9,17},{17,25},{25,1},{2,10},{10... | collective-permute-start | bytes 786440 | tf_op jit(solution)/shard_map/ppermute | solution.py:40
  23.5 0.8 collective-permute-start
  24.3 1.9 %collective-permute-start.3 = (bf16[8,128,128]{2,1,0:T(8,128)(2,1)S(1)}, bf16[8,128,128]{2,1,0:T(8,128)(2,1)S(1)}, u32[]{:S(2)}, u32[]{:S(2)}) collective-permute-start(bf16[8,128,128]{2,1,0:T(8,128)(2,1)S(1)} %all_to_all.10.refs_2_), channel_id=1, source_target_pairs={{0,24},{8,0},{16,8},{24,16},{1,25},{9,1},{17,9},{25,17},{2,26},{10... | collective-permute-start | bytes 786440 | tf_op jit(solution)/shard_map/ppermute | solution.py:40
  26.8 0.8 concatenate.10.me_ref
  27.6 2.2 %copy-done = bf16[1,1,128,128,128]{4,3,2,1,0:T(8,128)(2,1)S(1)} copy-done((bf16[1,1,128,128,128]{4,3,2,1,0:T(8,128)(2,1)S(1)}, bf16[1,1,128,128,128]{4,3,2,1,0:T(8,128)(2,1)}, u32[]{:S(2)}) %copy-start) | copy-done | bytes 4194328
  29.8 4.5 %densify.1 = (bf16[32,512,128]{2,1,0:T(8,128)(2,1)S(1)}, bf16[32,512,128]{2,1,0:T(8,128)(2,1)S(1)}) custom-call(s32[260]{0:T(512)S(1)} %concatenate.10.me_ref, bf16[128,128,128]{2,1,0:T(8,128)(2,1)S(1)} %bitcast.11), custom_call_target="tpu_custom_call" | custom-call | bytes 12582912 | tf_op jit(solution)/shard_map/densify/pallas_call | solution.py:73
  34.3 0.0 collective-permute-done.1.refs_3_
  34.3 0.7 forward.3.token_ref.refs_6_
  35.1 0.1 collective-permute-start.6
  35.2 0.0 collective-permute-done.block_ref
  35.2 0.5 collective-permute-start.2
  35.7 1.8 %collective-permute-done.3.block_ref = bf16[8,128,128]{2,1,0:T(8,128)(2,1)S(1)} collective-permute-done((bf16[8,128,128]{2,1,0:T(8,128)(2,1)S(1)}, bf16[8,128,128]{2,1,0:T(8,128)(2,1)S(1)}, u32[]{:S(2)}, u32[]{:S(2)}) %collective-permute-start.3) | collective-permute-done | bytes 262176 | tf_op jit(solution)/shard_map/ppermute | solution.py:40
  37.5 1.2 %collective-permute-start.4 = (bf16[8,128,128]{2,1,0:T(8,128)(2,1)S(1)}, bf16[8,128,128]{2,1,0:T(8,128)(2,1)S(1)}, u32[]{:S(2)}, u32[]{:S(2)}) collective-permute-start(bf16[8,128,128]{2,1,0:T(8,128)(2,1)S(1)} %tie.5.refs_5_), channel_id=1, source_target_pairs={{0,4},{4,0},{1,5},{5,1},{2,6},{6,2},{3,7},{7,3},{8,12},{12,8},{9,1... | collective-permute-start | bytes 786440 | tf_op jit(solution)/shard_map/ppermute | solution.py:40
  38.6 1.3 %forward.4.refs_4_ = f32[512,128]{1,0:T(8,128)S(1)} custom-call(bf16[32,512,128]{2,1,0:T(8,128)(2,1)S(1)} %get-tuple-element.13.refs_0_.mine_ref, bf16[32,512,128]{2,1,0:T(8,128)(2,1)S(1)} %get-tuple-element.14.refs_1_.block_ref, bf16[8,128,128]{2,1,0:T(8,128)(2,1)S(1)} %tie.6.refs_2_, bf16[8,128,128]{2,1,0:T(8,128)(2,1)S(1)} %collective-permute-done.6.refs_3_, ...), custom_call_target="tpu_custom_call" | custom-call | flops 536870912 | bytes 4194304 | tf_op jit(solution)/shard_map/forward/pallas_call | solution.py:105
  39.9 0.0 collective-permute-done.2.refs_2_
  39.9 0.7 forward.5.token_ref.p0
  40.6 0.0 copy-start.2
  40.7 0.0 copy-start.3
  40.7 0.3 collective-permute-start.7
  41.0 1.3 %collective-permute-start.8 = (bf16[640,128]{1,0:T(8,128)(2,1)S(1)}, bf16[640,128]{1,0:T(8,128)(2,1)S(1)}, u32[]{:S(2)}, u32[]{:S(2)}) collective-permute-start(bf16[640,128]{1,0:T(8,128)(2,1)S(1)} %forward.5.token_ref.p0), channel_id=1, source_target_pairs={{0,1},{1,2},{2,3},{3,0},{4,5},{5,6},{6,7},{7,4},{8,9},{9,10},{10,1... | collective-permute-start | bytes 491528 | tf_op jit(solution)/shard_map/ppermute | solution.py:40
  42.3 2.6 %collective-permute-start.9 = (bf16[640,128]{1,0:T(8,128)(2,1)S(1)}, bf16[640,128]{1,0:T(8,128)(2,1)S(1)}, u32[]{:S(2)}, u32[]{:S(2)}) collective-permute-start(bf16[640,128]{1,0:T(8,128)(2,1)S(1)} %forward.5.token_ref.p0), channel_id=1, source_target_pairs={{0,2},{1,3},{2,0},{3,1},{4,6},{5,7},{6,4},{7,5},{8,10},{9,11},{10,... | collective-permute-start | bytes 491528 | tf_op jit(solution)/shard_map/ppermute | solution.py:40
  44.9 1.1 %collective-permute-start.10 = (bf16[640,128]{1,0:T(8,128)(2,1)S(1)}, bf16[640,128]{1,0:T(8,128)(2,1)S(1)}, u32[]{:S(2)}, u32[]{:S(2)}) collective-permute-start(bf16[640,128]{1,0:T(8,128)(2,1)S(1)} %forward.5.token_ref.p0), channel_id=1, source_target_pairs={{0,3},{1,0},{2,1},{3,2},{4,7},{5,4},{6,5},{7,6},{8,11},{9,8},{10,9... | collective-permute-start | bytes 491528 | tf_op jit(solution)/shard_map/ppermute | solution.py:40
  46.0 0.1 pad_add_fusion.me_ref
  46.1 1.8 %collective-permute-done.8.p1 = bf16[640,128]{1,0:T(8,128)(2,1)S(1)} collective-permute-done((bf16[640,128]{1,0:T(8,128)(2,1)S(1)}, bf16[640,128]{1,0:T(8,128)(2,1)S(1)}, u32[]{:S(2)}, u32[]{:S(2)}) %collective-permute-start.8) | collective-permute-done | bytes 163872 | tf_op jit(solution)/shard_map/ppermute | solution.py:40
  47.9 4.6 %collective-permute-done.9.p2 = bf16[640,128]{1,0:T(8,128)(2,1)S(1)} collective-permute-done((bf16[640,128]{1,0:T(8,128)(2,1)S(1)}, bf16[640,128]{1,0:T(8,128)(2,1)S(1)}, u32[]{:S(2)}, u32[]{:S(2)}) %collective-permute-start.9) | collective-permute-done | bytes 163872 | tf_op jit(solution)/shard_map/ppermute | solution.py:40
  52.5 1.0 %middle.1 = (f32[128,128]{1,0:T(8,128)S(1)}, bf16[592,128]{1,0:T(8,128)(2,1)S(1)}, f32[64,128]{1,0:T(8,128)S(1)}) custom-call(s32[4]{0:T(128)S(1)} %pad_add_fusion.me_ref, bf16[640,128]{1,0:T(8,128)(2,1)S(1)} %forward.5.token_ref.p0, bf16[640,128]{1,0:T(8,128)(2,1)S(1)} %collective-permute-done.8.p1, bf16[640,128]{1,0:T(8,128)(2,1)S(1)} %collective-permute-done.9.p2, ...), custom_call_target="tpu_custom_call" | custom-call | flops 50331648 | bytes 1048576 | tf_op jit(solution)/shard_map/middle/pallas_call | solution.py:170
  53.5 1.2 %collective-permute-start.11 = (bf16[592,128]{1,0:T(8,128)(2,1)S(1)}, bf16[592,128]{1,0:T(8,128)(2,1)S(1)}, u32[]{:S(2)}, u32[]{:S(2)}) collective-permute-start(bf16[592,128]{1,0:T(8,128)(2,1)S(1)} %get-tuple-element.15.give_ref), channel_id=1, source_target_pairs={{0,4},{4,0},{1,5},{5,1},{2,6},{6,2},{3,7},{7,3},{8,12},{12,8},{9,1... | collective-permute-start | bytes 454664 | tf_op jit(solution)/shard_map/ppermute | solution.py:40
  54.7 1.0 %collective-permute-done.11.got_ref = bf16[592,128]{1,0:T(8,128)(2,1)S(1)} collective-permute-done((bf16[592,128]{1,0:T(8,128)(2,1)S(1)}, bf16[592,128]{1,0:T(8,128)(2,1)S(1)}, u32[]{:S(2)}, u32[]{:S(2)}) %collective-permute-start.11) | collective-permute-done | bytes 151584 | tf_op jit(solution)/shard_map/ppermute | solution.py:40
  55.7 0.0 collective-permute-done.7.other_ref
  55.7 0.5 backward.5
  56.2 1.1 %collective-permute-start.12 = (bf16[1104,128]{1,0:T(8,128)(2,1)S(1)}, bf16[1104,128]{1,0:T(8,128)(2,1)S(1)}, u32[]{:S(2)}, u32[]{:S(2)}) collective-permute-start(bf16[1104,128]{1,0:T(8,128)(2,1)S(1)} %backward.5), channel_id=1, source_target_pairs={{0,8},{8,16},{16,24},{24,0},{1,9},{9,17},{17,25},{25,1},{2,10},{10... | collective-permute-start | bytes 847880 | tf_op jit(solution)/shard_map/ppermute | solution.py:40
  57.2 0.5 backward.6
  57.7 1.8 %collective-permute-start.13 = (bf16[1104,128]{1,0:T(8,128)(2,1)S(1)}, bf16[1104,128]{1,0:T(8,128)(2,1)S(1)}, u32[]{:S(2)}, u32[]{:S(2)}) collective-permute-start(bf16[1104,128]{1,0:T(8,128)(2,1)S(1)} %backward.6), channel_id=1, source_target_pairs={{0,16},{8,24},{16,0},{24,8},{1,17},{9,25},{17,1},{25,9},{2,18},{10... | collective-permute-start | bytes 847880 | tf_op jit(solution)/shard_map/ppermute | solution.py:40
  59.5 0.5 backward.7
  60.0 1.1 %collective-permute-start.14 = (bf16[1104,128]{1,0:T(8,128)(2,1)S(1)}, bf16[1104,128]{1,0:T(8,128)(2,1)S(1)}, u32[]{:S(2)}, u32[]{:S(2)}) collective-permute-start(bf16[1104,128]{1,0:T(8,128)(2,1)S(1)} %backward.7), channel_id=1, source_target_pairs={{0,24},{8,0},{16,8},{24,16},{1,25},{9,1},{17,9},{25,17},{2,26},{10... | collective-permute-start | bytes 847880 | tf_op jit(solution)/shard_map/ppermute | solution.py:40
  61.1 1.0 %backward.4 = (bf16[1104,128]{1,0:T(8,128)(2,1)S(1)}, bf16[128,128]{1,0:T(8,128)(2,1)}) custom-call(bf16[32,512,128]{2,1,0:T(8,128)(2,1)S(1)} %get-tuple-element.13.refs_0_.mine_ref, bf16[32,512,128]{2,1,0:T(8,128)(2,1)S(1)} %collective-permute-done.7.other_ref, bf16[592,128]{1,0:T(8,128)(2,1)S(1)} %get-tuple-element.15.give_ref, ...), custom_call_target="tpu_custom_call" | custom-call | flops 268435456 | bytes 2097152 | tf_op jit(solution)/shard_map/backward/pallas_call | solution.py:221
  62.0 2.2 %collective-permute-done.12.r1 = bf16[1104,128]{1,0:T(8,128)(2,1)S(1)} collective-permute-done((bf16[1104,128]{1,0:T(8,128)(2,1)S(1)}, bf16[1104,128]{1,0:T(8,128)(2,1)S(1)}, u32[]{:S(2)}, u32[]{:S(2)}) %collective-permute-start.12) | collective-permute-done | bytes 282656 | tf_op jit(solution)/shard_map/ppermute | solution.py:40
  64.2 3.0 %collective-permute-done.13.r2 = bf16[1104,128]{1,0:T(8,128)(2,1)S(1)} collective-permute-done((bf16[1104,128]{1,0:T(8,128)(2,1)S(1)}, bf16[1104,128]{1,0:T(8,128)(2,1)S(1)}, u32[]{:S(2)}, u32[]{:S(2)}) %collective-permute-start.13) | collective-permute-done | bytes 282656 | tf_op jit(solution)/shard_map/ppermute | solution.py:40
  67.2 7.0 %collective-permute-done.14.r3 = bf16[1104,128]{1,0:T(8,128)(2,1)S(1)} collective-permute-done((bf16[1104,128]{1,0:T(8,128)(2,1)S(1)}, bf16[1104,128]{1,0:T(8,128)(2,1)S(1)}, u32[]{:S(2)}, u32[]{:S(2)}) %collective-permute-start.14) | collective-permute-done | bytes 282656 | tf_op jit(solution)/shard_map/ppermute | solution.py:40
  74.2 0.2 line_sum.1
  74.4 18.1 %all_to_all.11.in_ref = bf16[8,208,128]{2,1,0:T(8,128)(2,1)S(1)} all-to-all(bf16[8,208,128]{2,1,0:T(8,128)(2,1)S(1)} %line_sum.1), channel_id=1, replica_groups=mesh['z'=8,'x'=4,'core'=2,'rep'=4] {'z'}, dimensions={0} | all-to-all | bytes 851968 | tf_op jit(solution)/shard_map/all_to_all | solution.py:328
  92.5 0.7 collective-permute-start.15
  93.2 0.7 finish_grad.1
  93.9 0.1 collective-permute-done.15
  94.1 0.6 maximum_select_fusion
  (14 shorter events, 0.1 us)
Async XLA Ops:
  19.8 14.5 %collective-permute-start.1 = (bf16[8,128,128]{2,1,0:T(8,128)(2,1)S(1)}, bf16[8,128,128]{2,1,0:T(8,128)(2,1)S(1)}, u32[]{:S(2)}, u32[]{:S(2)}) collective-permute-start(bf16[8,128,128]{2,1,0:T(8,128)(2,1)S(1)} %all_to_all.10.refs_2_), channel_id=1, source_target_pairs={{0,4},{4,0},{1,5},{5,1},{2,6},{6,2},{3,7},{7,3},{8,12},{12,8},{9,1... | collective-permute-start | bytes 786440 | tf_op jit(solution)/shard_map/ppermute | solution.py:40
  22.2 12.8 %collective-permute-start.5 = (bf16[8,128,128]{2,1,0:T(8,128)(2,1)S(1)}, bf16[8,128,128]{2,1,0:T(8,128)(2,1)S(1)}, u32[]{:S(2)}, u32[]{:S(2)}) collective-permute-start(bf16[8,128,128]{2,1,0:T(8,128)(2,1)S(1)} %all_to_all.10.refs_2_), channel_id=1, source_target_pairs={{0,8},{8,16},{16,24},{24,0},{1,9},{9,17},{17,25},{25,1},{2,10},{10... | collective-permute-start | bytes 786440 | tf_op jit(solution)/shard_map/ppermute | solution.py:40
  23.5 11.7 %collective-permute-start = (bf16[8,128,128]{2,1,0:T(8,128)(2,1)S(1)}, bf16[8,128,128]{2,1,0:T(8,128)(2,1)S(1)}, u32[]{:S(2)}, u32[]{:S(2)}) collective-permute-start(bf16[8,128,128]{2,1,0:T(8,128)(2,1)S(1)} %all_to_all.10.refs_2_), channel_id=1, source_target_pairs={{0,16},{8,24},{16,0},{24,8},{1,17},{9,25},{17,1},{25,9},{2,18},{10... | collective-permute-start | bytes 786440 | tf_op jit(solution)/shard_map/ppermute | solution.py:40
  24.3 13.2 %collective-permute-start.3 = (bf16[8,128,128]{2,1,0:T(8,128)(2,1)S(1)}, bf16[8,128,128]{2,1,0:T(8,128)(2,1)S(1)}, u32[]{:S(2)}, u32[]{:S(2)}) collective-permute-start(bf16[8,128,128]{2,1,0:T(8,128)(2,1)S(1)} %all_to_all.10.refs_2_), channel_id=1, source_target_pairs={{0,24},{8,0},{16,8},{24,16},{1,25},{9,1},{17,9},{25,17},{2,26},{10... | collective-permute-start | bytes 786440 | tf_op jit(solution)/shard_map/ppermute | solution.py:40
  27.6 2.2 %copy-start = (bf16[1,1,128,128,128]{4,3,2,1,0:T(8,128)(2,1)S(1)}, bf16[1,1,128,128,128]{4,3,2,1,0:T(8,128)(2,1)}, u32[]{:S(2)}) copy-start(bf16[1,1,128,128,128]{4,3,2,1,0:T(8,128)(2,1)} %param.12) | copy-start | bytes 12582916
  35.1 3.6 %collective-permute-start.6 = (bf16[8,128,128]{2,1,0:T(8,128)(2,1)S(1)}, bf16[8,128,128]{2,1,0:T(8,128)(2,1)S(1)}, u32[]{:S(2)}, u32[]{:S(2)}) collective-permute-start(bf16[8,128,128]{2,1,0:T(8,128)(2,1)S(1)} %tie.6.refs_2_), channel_id=1, source_target_pairs={{0,4},{4,0},{1,5},{5,1},{2,6},{6,2},{3,7},{7,3},{8,12},{12,8},{9,1... | collective-permute-start | bytes 786440 | tf_op jit(solution)/shard_map/ppermute | solution.py:40
  35.2 4.7 %collective-permute-start.2 = (bf16[8,128,128]{2,1,0:T(8,128)(2,1)S(1)}, bf16[8,128,128]{2,1,0:T(8,128)(2,1)S(1)}, u32[]{:S(2)}, u32[]{:S(2)}) collective-permute-start(bf16[8,128,128]{2,1,0:T(8,128)(2,1)S(1)} %tie.4.refs_4_), channel_id=1, source_target_pairs={{0,4},{4,0},{1,5},{5,1},{2,6},{6,2},{3,7},{7,3},{8,12},{12,8},{9,1... | collective-permute-start | bytes 786440 | tf_op jit(solution)/shard_map/ppermute | solution.py:40
  37.5 2.5 %copy-start.1 = (bf16[128,128]{1,0:T(8,128)(2,1)S(1)}, bf16[128,128]{1,0:T(8,128)(2,1)}, u32[]{:S(2)}) copy-start(bf16[128,128]{1,0:T(8,128)(2,1)} %refs_5_.1) | copy-start | bytes 98308
  37.5 2.4 %collective-permute-start.4 = (bf16[8,128,128]{2,1,0:T(8,128)(2,1)S(1)}, bf16[8,128,128]{2,1,0:T(8,128)(2,1)S(1)}, u32[]{:S(2)}, u32[]{:S(2)}) collective-permute-start(bf16[8,128,128]{2,1,0:T(8,128)(2,1)S(1)} %tie.5.refs_5_), channel_id=1, source_target_pairs={{0,4},{4,0},{1,5},{5,1},{2,6},{6,2},{3,7},{7,3},{8,12},{12,8},{9,1... | collective-permute-start | bytes 786440 | tf_op jit(solution)/shard_map/ppermute | solution.py:40
  40.6 11.9 %copy-start.2 = (bf16[128,128]{1,0:T(8,128)(2,1)S(1)}, bf16[128,128]{1,0:T(8,128)(2,1)}, u32[]{:S(2)}) copy-start(bf16[128,128]{1,0:T(8,128)(2,1)} %weight_ref.1) | copy-start | bytes 98308
  40.7 11.9 %copy-start.3 = (f32[128]{0:T(128)S(1)}, f32[128]{0:T(128)}, u32[]{:S(2)}) copy-start(f32[128]{0:T(128)} %param.10) | copy-start | bytes 1540
  40.7 15.0 %collective-permute-start.7 = (bf16[32,512,128]{2,1,0:T(8,128)(2,1)S(1)}, bf16[32,512,128]{2,1,0:T(8,128)(2,1)S(1)}, u32[]{:S(2)}, u32[]{:S(2)}) collective-permute-start(bf16[32,512,128]{2,1,0:T(8,128)(2,1)S(1)} %tie.7), channel_id=1, source_target_pairs={{0,4},{4,0},{1,5},{5,1},{2,6},{6,2},{3,7},{7,3},{8,12},{12,8},{9,1... | collective-permute-start | bytes 12582920 | tf_op jit(solution)/shard_map/ppermute | solution.py:40
  41.0 6.9 %collective-permute-start.8 = (bf16[640,128]{1,0:T(8,128)(2,1)S(1)}, bf16[640,128]{1,0:T(8,128)(2,1)S(1)}, u32[]{:S(2)}, u32[]{:S(2)}) collective-permute-start(bf16[640,128]{1,0:T(8,128)(2,1)S(1)} %forward.5.token_ref.p0), channel_id=1, source_target_pairs={{0,1},{1,2},{2,3},{3,0},{4,5},{5,6},{6,7},{7,4},{8,9},{9,10},{10,1... | collective-permute-start | bytes 491528 | tf_op jit(solution)/shard_map/ppermute | solution.py:40
  42.3 10.2 %collective-permute-start.9 = (bf16[640,128]{1,0:T(8,128)(2,1)S(1)}, bf16[640,128]{1,0:T(8,128)(2,1)S(1)}, u32[]{:S(2)}, u32[]{:S(2)}) collective-permute-start(bf16[640,128]{1,0:T(8,128)(2,1)S(1)} %forward.5.token_ref.p0), channel_id=1, source_target_pairs={{0,2},{1,3},{2,0},{3,1},{4,6},{5,7},{6,4},{7,5},{8,10},{9,11},{10,... | collective-permute-start | bytes 491528 | tf_op jit(solution)/shard_map/ppermute | solution.py:40
  44.9 7.6 %collective-permute-start.10 = (bf16[640,128]{1,0:T(8,128)(2,1)S(1)}, bf16[640,128]{1,0:T(8,128)(2,1)S(1)}, u32[]{:S(2)}, u32[]{:S(2)}) collective-permute-start(bf16[640,128]{1,0:T(8,128)(2,1)S(1)} %forward.5.token_ref.p0), channel_id=1, source_target_pairs={{0,3},{1,0},{2,1},{3,2},{4,7},{5,4},{6,5},{7,6},{8,11},{9,8},{10,9... | collective-permute-start | bytes 491528 | tf_op jit(solution)/shard_map/ppermute | solution.py:40
  53.5 2.2 %collective-permute-start.11 = (bf16[592,128]{1,0:T(8,128)(2,1)S(1)}, bf16[592,128]{1,0:T(8,128)(2,1)S(1)}, u32[]{:S(2)}, u32[]{:S(2)}) collective-permute-start(bf16[592,128]{1,0:T(8,128)(2,1)S(1)} %get-tuple-element.15.give_ref), channel_id=1, source_target_pairs={{0,4},{4,0},{1,5},{5,1},{2,6},{6,2},{3,7},{7,3},{8,12},{12,8},{9,1... | collective-permute-start | bytes 454664 | tf_op jit(solution)/shard_map/ppermute | solution.py:40
  56.2 8.0 %collective-permute-start.12 = (bf16[1104,128]{1,0:T(8,128)(2,1)S(1)}, bf16[1104,128]{1,0:T(8,128)(2,1)S(1)}, u32[]{:S(2)}, u32[]{:S(2)}) collective-permute-start(bf16[1104,128]{1,0:T(8,128)(2,1)S(1)} %backward.5), channel_id=1, source_target_pairs={{0,8},{8,16},{16,24},{24,0},{1,9},{9,17},{17,25},{25,1},{2,10},{10... | collective-permute-start | bytes 847880 | tf_op jit(solution)/shard_map/ppermute | solution.py:40
  57.7 9.5 %collective-permute-start.13 = (bf16[1104,128]{1,0:T(8,128)(2,1)S(1)}, bf16[1104,128]{1,0:T(8,128)(2,1)S(1)}, u32[]{:S(2)}, u32[]{:S(2)}) collective-permute-start(bf16[1104,128]{1,0:T(8,128)(2,1)S(1)} %backward.6), channel_id=1, source_target_pairs={{0,16},{8,24},{16,0},{24,8},{1,17},{9,25},{17,1},{25,9},{2,18},{10... | collective-permute-start | bytes 847880 | tf_op jit(solution)/shard_map/ppermute | solution.py:40
  60.0 14.2 %collective-permute-start.14 = (bf16[1104,128]{1,0:T(8,128)(2,1)S(1)}, bf16[1104,128]{1,0:T(8,128)(2,1)S(1)}, u32[]{:S(2)}, u32[]{:S(2)}) collective-permute-start(bf16[1104,128]{1,0:T(8,128)(2,1)S(1)} %backward.7), channel_id=1, source_target_pairs={{0,24},{8,0},{16,8},{24,16},{1,25},{9,1},{17,9},{25,17},{2,26},{10... | collective-permute-start | bytes 847880 | tf_op jit(solution)/shard_map/ppermute | solution.py:40
  92.5 1.6 %collective-permute-start.15 = (f32[64,128]{1,0:T(8,128)S(1)}, f32[64,128]{1,0:T(8,128)S(1)}, u32[]{:S(2)}, u32[]{:S(2)}) collective-permute-start(f32[64,128]{1,0:T(8,128)S(1)} %finish_terms.1), channel_id=1, source_target_pairs={{0,4},{4,0},{1,5},{5,1},{2,6},{6,2},{3,7},{7,3},{8,12},{12,8},{9,1... | collective-permute-start | bytes 98312 | tf_op jit(solution)/shard_map/ppermute | solution.py:40

commit v6 on v5

--- a/solution.py
+++ b/solution.py
@@ -192,26 +192,53 @@
     return pair[0:1] + pair[1:2]
 
 
-def backward(mine, other, give, got, keep, chunk, own=None):
-    def kernel(mine_ref, other_ref, give_ref, got_ref, keep_ref, *refs):
+def wide(ref):
+    return jnp.concatenate([ref[r * T:(r + 1) * T] for r in range(Q)], axis=1)
+
+
+def products(back, panels_ref, chunk, z):
+    at = chunk * Z + z
+    pair = jnp.concatenate([panels_ref[at], panels_ref[at + 1]], axis=1)
+    return jnp.dot(back, pair, preferred_element_type=F32)
+
+
+def backward_own(mine, give):
+    def kernel(mine_ref, give_ref, out_ref):
+        back = wide(give_ref)
+
+        def step(chunk, carry):
+            for z in range(0, Z, 2):
+                part = products(back, mine_ref, chunk, z)
+                out_ref[chunk, z] = part[:, :T]
+                out_ref[chunk, z + 1] = part[:, T:]
+            return carry
+
+        lax.fori_loop(0, X, step, 0)
+
+    return pl.pallas_call(
+        kernel,
+        in_specs=[VMEM] * 2,
+        out_specs=VMEM,
+        out_shape=jax.ShapeDtypeStruct((X, Z, T, T), F32),
+        compiler_params=params(16),
+        cost_estimate=cost(2 * PANEL * T * T * Z * X, 2**22),
+        name="backward_own",
+    )(mine, give)
+
+
+def backward(begun, other, give, got, keep, chunk, own=None):
+    def kernel(begun_ref, other_ref, give_ref, got_ref, keep_ref, *refs):
         if own is None:
             out_ref, = refs
         else:
             own_ref, out_ref, layer_ref = refs
             preact = own_ref[...]
             layer_ref[...] = (preact * jax.nn.sigmoid(preact)).astype(BF16)
-        wide = lambda ref: jnp.concatenate([ref[r * T:(r + 1) * T] for r in range(Q)], axis=1)
-        sides = [(wide(give_ref), mine_ref), (wide(got_ref), other_ref)]
+        back = wide(got_ref)
         for z in range(0, Z, 2):
-            at = chunk * Z + z
-            part = None
-            for back, ref in sides:
-                pair = jnp.concatenate([ref[at], ref[at + 1]], axis=1)
-                term = jnp.dot(back, pair, preferred_element_type=F32)
-                part = term if part is None else part + term
-            part = part.astype(BF16)
-            out_ref[z * T:z * T + T] = part[:, :T]
-            out_ref[z * T + T:z * T + 2 * T] = part[:, T:]
+            part = products(back, other_ref, chunk, z)
+            out_ref[z * T:z * T + T] = (begun_ref[chunk, z] + part[:, :T]).astype(BF16)
+            out_ref[z * T + T:z * T + 2 * T] = (begun_ref[chunk, z + 1] + part[:, T:]).astype(BF16)
         terms = keep_ref[...] + got_ref[PANEL:PANEL + HALF].astype(F32)
         out_ref[Z * T:Z * T + HALF] = terms.astype(BF16)
         bias = bias_of(give_ref, PANEL + HALF) + bias_of(got_ref, PANEL + HALF)
@@ -224,9 +251,9 @@
         out_specs=[VMEM] * (1 + len(extra)),
         out_shape=[jax.ShapeDtypeStruct((MSG, T), BF16)] + [jax.ShapeDtypeStruct((T, T), BF16)] * len(extra),
         compiler_params=params(16),
-        cost_estimate=cost(4 * PANEL * T * T * Z, 2**21),
+        cost_estimate=cost(2 * PANEL * T * T * Z, 2**21),
         name="backward",
-    )(mine, other, give, got, keep, *extra)
+    )(begun, other, give, got, keep, *extra)
 
 
 def line_sum(s0, s1, s2, s3):
@@ -303,14 +330,14 @@
     spread = jnp.broadcast_to(features, (Z, T, T))
     line = lax.all_to_all(spread, "z", 0, 0, tiled=True)
     halves = densify(me, tile_values[0, 0])
-    near = [(0, 0, line), (1, 0, send(line, "core", C, 1))]
-    begun = forward(halves, near, None, F32)
+    begun = forward(halves, [(0, 0, line)], None, F32)
+    near = [(1, 0, send(line, "core", C, 1))]
     far = []
     for n in range(1, X):
         block = tie(send(line, "x", X, n), begun)
         far += [(0, n, block), (1, n, send(block, "core", C, 1))]
     late = [far[3], far[5]]
-    begun = forward(halves, far[:3] + far[4:5], begun, F32)
+    begun = forward(halves, near + far[:3] + far[4:5], begun, F32)
     partial = forward(halves, late, begun, BF16, cotangent)
 
     partials = [partial] + [send(partial, "rep", Q, n) for n in range(1, Q)]
@@ -319,11 +346,12 @@
     own, give, keep = middle(place, partials, weight, bias_terms.reshape(1, T))
     got = send(give, "core", C, 1)
 
+    ahead = backward_own(mine, give)
     sums = {}
     for n in (1, 2, 3):
-        total, = backward(mine, fellow, give, got, keep, n)
+        total, = backward(ahead, fellow, give, got, keep, n)
         sums[n] = send(total, "x", X, -n)
-    sums[0], output = backward(mine, fellow, give, got, keep, 0, own)
+    sums[0], output = backward(ahead, fellow, give, got, keep, 0, own)
     blocks = line_sum(sums[0], sums[3], sums[2], sums[1])
     received = lax.all_to_all(blocks, "z", 0, 0, tiled=True)
     half = finish_terms(received)

time: 95 us -> 93.4 us (0.983)
  waiting for transfers between devices: 21.5 us -> 19.3 us
  starting transfers between devices: 19.3 us -> 20.6 us
  blocking collectives: 36.5 us -> 35.2 us
    ppermute x16, waiting for transfers between devices: 21.5 us -> 19.3 us  [send(): return lax.ppermute(array, axis, shift(axis, size, by))]
    all_to_all x1, blocking collectives: 18.1 us -> 16.8 us  [body(): received = lax.all_to_all(blocks, 'z', 0, 0, tiled=True)]
    ppermute x16, starting transfers between devices: 19.3 us -> 20.6 us  [send(): return lax.ppermute(array, axis, shift(axis, size, by))]
    pallas_call x0 -> x1, Pallas kernels: none -> 1.24 us  [backward_own(): pl.pallas_call(kernel, in_specs=[VMEM] * 2, out_specs=VMEM, out_shape=jax...]
  transfers between devices with their start and end apart: 16 -> 16, of which waited for: 8 -> 6; matrix products, arithmetic and copies ran while one was open for 1% -> 1% of each run, Pallas kernels for 11% -> 11%
where the time goes in v6:
time: 93.4 us; the launch traced here: 92.4 us
  blocking collectives  35.2 us (38%)
  starting transfers between devices  20.6 us (22%)
  waiting for transfers between devices  19.3 us (21%)
  Pallas kernels  11.4 us (12%)
  local copies, waits for them, and re-layouts  3.75 us (4%)
  between operations  1.48 us (2%)
    ppermute x16, starting transfers between devices, send(): return lax.ppermute(array, axis, shift(axis, size, by))  20.6 us
    ppermute x16, waiting for transfers between devices, send(): return lax.ppermute(array, axis, shift(axis, size, by))  19.3 us
    all_to_all x1, blocking collectives, body(): line = lax.all_to_all(spread, 'z', 0, 0, tiled=True)  18.4 us
    all_to_all x1, blocking collectives, body(): received = lax.all_to_all(blocks, 'z', 0, 0, tiled=True)  16.8 us
    pallas_call x1, Pallas kernels, densify(): pl.pallas_call(densify_kernel, in_specs=[SMEM, VMEM], out_specs=[VMEM] *...  3.75 us
    pallas_call x3, Pallas kernels, forward(): pl.pallas_call(kernel, in_specs=[VMEM] * (2 + count + len(extra)), out_sp...  2.68 us
    unnamed x8, local copies, waits for them, and re-layouts  2.21 us
  transfers between devices with their start and end apart: 16, of which 6 were waited for; matrix products, arithmetic and copies ran while one was open for 1% of the time, Pallas kernels for 11%

profile of v6, /device:TPU:3, one launch (start us, length us, event | category | flops | bytes accessed | tf_op | source)
XLA Modules:
  0.0 92.4 jit_solution(17713573441058336584)
XLA Ops:
  0.6 0.8 broadcast_in_dim.3
  1.4 18.4 %all_to_all.10.refs_2_ = bf16[8,128,128]{2,1,0:T(8,128)(2,1)S(1)} all-to-all(bf16[8,128,128]{2,1,0:T(8,128)(2,1)S(1)} %broadcast_in_dim.3), channel_id=1, replica_groups=mesh['z'=8,'x'=4,'core'=2,'rep'=4] {'z'}, dimensions={0} | all-to-all | bytes 524288 | tf_op jit(solution)/shard_map/all_to_all | solution.py:331
  19.8 1.2 %collective-permute-start.5 = (bf16[8,128,128]{2,1,0:T(8,128)(2,1)S(1)}, bf16[8,128,128]{2,1,0:T(8,128)(2,1)S(1)}, u32[]{:S(2)}, u32[]{:S(2)}) collective-permute-start(bf16[8,128,128]{2,1,0:T(8,128)(2,1)S(1)} %all_to_all.10.refs_2_), channel_id=1, source_target_pairs={{0,8},{8,16},{16,24},{24,0},{1,9},{9,17},{17,25},{25,1},{2,10},{10... | collective-permute-start | bytes 786440 | tf_op jit(solution)/shard_map/ppermute | solution.py:40
  21.0 0.8 collective-permute-start
  21.8 1.9 %collective-permute-start.2 = (bf16[8,128,128]{2,1,0:T(8,128)(2,1)S(1)}, bf16[8,128,128]{2,1,0:T(8,128)(2,1)S(1)}, u32[]{:S(2)}, u32[]{:S(2)}) collective-permute-start(bf16[8,128,128]{2,1,0:T(8,128)(2,1)S(1)} %all_to_all.10.refs_2_), channel_id=1, source_target_pairs={{0,24},{8,0},{16,8},{24,16},{1,25},{9,1},{17,9},{25,17},{2,26},{10... | collective-permute-start | bytes 786440 | tf_op jit(solution)/shard_map/ppermute | solution.py:40
  24.3 0.8 concatenate.10.me_ref
  25.1 2.2 %copy-done = bf16[1,1,128,128,128]{4,3,2,1,0:T(8,128)(2,1)S(1)} copy-done((bf16[1,1,128,128,128]{4,3,2,1,0:T(8,128)(2,1)S(1)}, bf16[1,1,128,128,128]{4,3,2,1,0:T(8,128)(2,1)}, u32[]{:S(2)}) %copy-start) | copy-done | bytes 4194328
  27.3 3.7 %densify.1 = (bf16[32,512,128]{2,1,0:T(8,128)(2,1)S(1)}, bf16[32,512,128]{2,1,0:T(8,128)(2,1)S(1)}) custom-call(s32[260]{0:T(512)S(1)} %concatenate.10.me_ref, bf16[128,128,128]{2,1,0:T(8,128)(2,1)S(1)} %bitcast.11), custom_call_target="tpu_custom_call" | custom-call | bytes 12582912 | tf_op jit(solution)/shard_map/densify/pallas_call | solution.py:73
  31.0 3.0 %collective-permute-start.4 = (bf16[8,128,128]{2,1,0:T(8,128)(2,1)S(1)}, bf16[8,128,128]{2,1,0:T(8,128)(2,1)S(1)}, u32[]{:S(2)}, u32[]{:S(2)}) collective-permute-start(bf16[8,128,128]{2,1,0:T(8,128)(2,1)S(1)} %all_to_all.10.refs_2_), channel_id=1, source_target_pairs={{0,4},{4,0},{1,5},{5,1},{2,6},{6,2},{3,7},{7,3},{8,12},{12,8},{9,1... | collective-permute-start | bytes 786440 | tf_op jit(solution)/shard_map/ppermute | solution.py:40
  34.1 0.4 forward.3.token_ref.refs_7_
  34.5 0.0 collective-permute-done.5.block_ref
  34.5 0.1 collective-permute-start.6
  34.6 0.0 collective-permute-done.block_ref
  34.6 0.5 collective-permute-start.1
  35.1 1.0 %collective-permute-start.3 = (bf16[8,128,128]{2,1,0:T(8,128)(2,1)S(1)}, bf16[8,128,128]{2,1,0:T(8,128)(2,1)S(1)}, u32[]{:S(2)}, u32[]{:S(2)}) collective-permute-start(bf16[8,128,128]{2,1,0:T(8,128)(2,1)S(1)} %tie.5.refs_6_), channel_id=1, source_target_pairs={{0,4},{4,0},{1,5},{5,1},{2,6},{6,2},{3,7},{7,3},{8,12},{12,8},{9,1... | collective-permute-start | bytes 786440 | tf_op jit(solution)/shard_map/ppermute | solution.py:40
  36.2 1.5 %forward.4.refs_4_ = f32[512,128]{1,0:T(8,128)S(1)} custom-call(bf16[32,512,128]{2,1,0:T(8,128)(2,1)S(1)} %get-tuple-element.13.refs_0_.mine_ref, bf16[32,512,128]{2,1,0:T(8,128)(2,1)S(1)} %get-tuple-element.14.refs_1_.block_ref, bf16[8,128,128]{2,1,0:T(8,128)(2,1)S(1)} %collective-permute-done.4.refs_2_, bf16[8,128,128]{2,1,0:T(8,128)(2,1)S(1)} %tie.6.refs_3_, ...), custom_call_target="tpu_custom_call" | custom-call | flops 671088640 | bytes 5242880 | tf_op jit(solution)/shard_map/forward/pallas_call | solution.py:105
  37.7 0.0 collective-permute-done.3.refs_3_
  37.7 0.7 forward.5.p0.token_ref
  38.5 0.0 copy-start.2
  38.5 0.0 copy-start.3
  38.5 0.2 collective-permute-start.10
  38.7 1.4 %collective-permute-start.7 = (bf16[640,128]{1,0:T(8,128)(2,1)S(1)}, bf16[640,128]{1,0:T(8,128)(2,1)S(1)}, u32[]{:S(2)}, u32[]{:S(2)}) collective-permute-start(bf16[640,128]{1,0:T(8,128)(2,1)S(1)} %forward.5.p0.token_ref), channel_id=1, source_target_pairs={{0,1},{1,2},{2,3},{3,0},{4,5},{5,6},{6,7},{7,4},{8,9},{9,10},{10,1... | collective-permute-start | bytes 491528 | tf_op jit(solution)/shard_map/ppermute | solution.py:40
  40.1 3.6 %collective-permute-start.8 = (bf16[640,128]{1,0:T(8,128)(2,1)S(1)}, bf16[640,128]{1,0:T(8,128)(2,1)S(1)}, u32[]{:S(2)}, u32[]{:S(2)}) collective-permute-start(bf16[640,128]{1,0:T(8,128)(2,1)S(1)} %forward.5.p0.token_ref), channel_id=1, source_target_pairs={{0,2},{1,3},{2,0},{3,1},{4,6},{5,7},{6,4},{7,5},{8,10},{9,11},{10,... | collective-permute-start | bytes 491528 | tf_op jit(solution)/shard_map/ppermute | solution.py:40
  43.7 0.6 collective-permute-start.9
  44.3 0.1 pad_add_fusion.me_ref
  44.4 2.4 %collective-permute-done.7.p1 = bf16[640,128]{1,0:T(8,128)(2,1)S(1)} collective-permute-done((bf16[640,128]{1,0:T(8,128)(2,1)S(1)}, bf16[640,128]{1,0:T(8,128)(2,1)S(1)}, u32[]{:S(2)}, u32[]{:S(2)}) %collective-permute-start.7) | collective-permute-done | bytes 163872 | tf_op jit(solution)/shard_map/ppermute | solution.py:40
  46.7 4.4 %collective-permute-done.8.p2 = bf16[640,128]{1,0:T(8,128)(2,1)S(1)} collective-permute-done((bf16[640,128]{1,0:T(8,128)(2,1)S(1)}, bf16[640,128]{1,0:T(8,128)(2,1)S(1)}, u32[]{:S(2)}, u32[]{:S(2)}) %collective-permute-start.8) | collective-permute-done | bytes 163872 | tf_op jit(solution)/shard_map/ppermute | solution.py:40
  51.1 0.0 collective-permute-done.9.p3
  51.1 1.0 %middle.1 = (f32[128,128]{1,0:T(8,128)S(1)}, bf16[592,128]{1,0:T(8,128)(2,1)S(1)}, f32[64,128]{1,0:T(8,128)S(1)}) custom-call(s32[4]{0:T(128)S(1)} %pad_add_fusion.me_ref, bf16[640,128]{1,0:T(8,128)(2,1)S(1)} %forward.5.p0.token_ref, bf16[640,128]{1,0:T(8,128)(2,1)S(1)} %collective-permute-done.7.p1, bf16[640,128]{1,0:T(8,128)(2,1)S(1)} %collective-permute-done.8.p2, ...), custom_call_target="tpu_custom_call" | custom-call | flops 50331648 | bytes 1048576 | tf_op jit(solution)/shard_map/middle/pallas_call | solution.py:170
  52.1 1.3 %collective-permute-start.11 = (bf16[592,128]{1,0:T(8,128)(2,1)S(1)}, bf16[592,128]{1,0:T(8,128)(2,1)S(1)}, u32[]{:S(2)}, u32[]{:S(2)}) collective-permute-start(bf16[592,128]{1,0:T(8,128)(2,1)S(1)} %get-tuple-element.15.give_ref), channel_id=1, source_target_pairs={{0,4},{4,0},{1,5},{5,1},{2,6},{6,2},{3,7},{7,3},{8,12},{12,8},{9,1... | collective-permute-start | bytes 454664 | tf_op jit(solution)/shard_map/ppermute | solution.py:40
  53.4 1.2 %backward_own.1.begun_ref = f32[4,8,128,128]{3,2,1,0:T(8,128)S(1)} custom-call(bf16[32,512,128]{2,1,0:T(8,128)(2,1)S(1)} %get-tuple-element.13.refs_0_.mine_ref, bf16[592,128]{1,0:T(8,128)(2,1)S(1)} %get-tuple-element.15.give_ref), custom_call_target="tpu_custom_call" | custom-call | flops 536870912 | bytes 4194304 | tf_op jit(solution)/shard_map/backward_own/pallas_call | solution.py:218
  54.7 0.0 collective-permute-done.10.other_ref
  54.7 0.3 backward.5
  55.0 0.1 collective-permute-start.12
  55.1 0.3 backward.6
  55.4 2.6 %collective-permute-start.13 = (bf16[1104,128]{1,0:T(8,128)(2,1)S(1)}, bf16[1104,128]{1,0:T(8,128)(2,1)S(1)}, u32[]{:S(2)}, u32[]{:S(2)}) collective-permute-start(bf16[1104,128]{1,0:T(8,128)(2,1)S(1)} %backward.6), channel_id=1, source_target_pairs={{0,16},{8,24},{16,0},{24,8},{1,17},{9,25},{17,1},{25,9},{2,18},{10... | collective-permute-start | bytes 847880 | tf_op jit(solution)/shard_map/ppermute | solution.py:40
  58.0 0.3 backward.7
  58.4 0.1 collective-permute-start.14
  58.4 0.9 backward.4
  59.3 4.1 %collective-permute-done.12.r1 = bf16[1104,128]{1,0:T(8,128)(2,1)S(1)} collective-permute-done((bf16[1104,128]{1,0:T(8,128)(2,1)S(1)}, bf16[1104,128]{1,0:T(8,128)(2,1)S(1)}, u32[]{:S(2)}, u32[]{:S(2)}) %collective-permute-start.12) | collective-permute-done | bytes 282656 | tf_op jit(solution)/shard_map/ppermute | solution.py:40
  63.4 1.7 %collective-permute-done.13.r2 = bf16[1104,128]{1,0:T(8,128)(2,1)S(1)} collective-permute-done((bf16[1104,128]{1,0:T(8,128)(2,1)S(1)}, bf16[1104,128]{1,0:T(8,128)(2,1)S(1)}, u32[]{:S(2)}, u32[]{:S(2)}) %collective-permute-start.13) | collective-permute-done | bytes 282656 | tf_op jit(solution)/shard_map/ppermute | solution.py:40
  65.1 6.7 %collective-permute-done.14.r3 = bf16[1104,128]{1,0:T(8,128)(2,1)S(1)} collective-permute-done((bf16[1104,128]{1,0:T(8,128)(2,1)S(1)}, bf16[1104,128]{1,0:T(8,128)(2,1)S(1)}, u32[]{:S(2)}, u32[]{:S(2)}) %collective-permute-start.14) | collective-permute-done | bytes 282656 | tf_op jit(solution)/shard_map/ppermute | solution.py:40
  71.7 0.2 line_sum.1
  71.9 16.8 %all_to_all.11.in_ref = bf16[8,208,128]{2,1,0:T(8,128)(2,1)S(1)} all-to-all(bf16[8,208,128]{2,1,0:T(8,128)(2,1)S(1)} %line_sum.1), channel_id=1, replica_groups=mesh['z'=8,'x'=4,'core'=2,'rep'=4] {'z'}, dimensions={0} | all-to-all | bytes 851968 | tf_op jit(solution)/shard_map/all_to_all | solution.py:356
  88.7 2.1 %collective-permute-start.15 = (f32[64,128]{1,0:T(8,128)S(1)}, f32[64,128]{1,0:T(8,128)S(1)}, u32[]{:S(2)}, u32[]{:S(2)}) collective-permute-start(f32[64,128]{1,0:T(8,128)S(1)} %finish_terms.1), channel_id=1, source_target_pairs={{0,4},{4,0},{1,5},{5,1},{2,6},{6,2},{3,7},{7,3},{8,12},{12,8},{9,1... | collective-permute-start | bytes 98312 | tf_op jit(solution)/shard_map/ppermute | solution.py:40
  90.9 0.7 finish_grad.1
  91.6 0.1 collective-permute-done.15
  91.7 0.6 maximum_select_fusion
  (15 shorter events, 0.1 us)
Async XLA Ops:
  19.8 14.7 %collective-permute-start.5 = (bf16[8,128,128]{2,1,0:T(8,128)(2,1)S(1)}, bf16[8,128,128]{2,1,0:T(8,128)(2,1)S(1)}, u32[]{:S(2)}, u32[]{:S(2)}) collective-permute-start(bf16[8,128,128]{2,1,0:T(8,128)(2,1)S(1)} %all_to_all.10.refs_2_), channel_id=1, source_target_pairs={{0,8},{8,16},{16,24},{24,0},{1,9},{9,17},{17,25},{25,1},{2,10},{10... | collective-permute-start | bytes 786440 | tf_op jit(solution)/shard_map/ppermute | solution.py:40
  21.0 13.6 %collective-permute-start = (bf16[8,128,128]{2,1,0:T(8,128)(2,1)S(1)}, bf16[8,128,128]{2,1,0:T(8,128)(2,1)S(1)}, u32[]{:S(2)}, u32[]{:S(2)}) collective-permute-start(bf16[8,128,128]{2,1,0:T(8,128)(2,1)S(1)} %all_to_all.10.refs_2_), channel_id=1, source_target_pairs={{0,16},{8,24},{16,0},{24,8},{1,17},{9,25},{17,1},{25,9},{2,18},{10... | collective-permute-start | bytes 786440 | tf_op jit(solution)/shard_map/ppermute | solution.py:40
  21.8 13.3 %collective-permute-start.2 = (bf16[8,128,128]{2,1,0:T(8,128)(2,1)S(1)}, bf16[8,128,128]{2,1,0:T(8,128)(2,1)S(1)}, u32[]{:S(2)}, u32[]{:S(2)}) collective-permute-start(bf16[8,128,128]{2,1,0:T(8,128)(2,1)S(1)} %all_to_all.10.refs_2_), channel_id=1, source_target_pairs={{0,24},{8,0},{16,8},{24,16},{1,25},{9,1},{17,9},{25,17},{2,26},{10... | collective-permute-start | bytes 786440 | tf_op jit(solution)/shard_map/ppermute | solution.py:40
  25.1 2.2 %copy-start = (bf16[1,1,128,128,128]{4,3,2,1,0:T(8,128)(2,1)S(1)}, bf16[1,1,128,128,128]{4,3,2,1,0:T(8,128)(2,1)}, u32[]{:S(2)}) copy-start(bf16[1,1,128,128,128]{4,3,2,1,0:T(8,128)(2,1)} %param.12) | copy-start | bytes 12582916
  31.0 5.1 %collective-permute-start.4 = (bf16[8,128,128]{2,1,0:T(8,128)(2,1)S(1)}, bf16[8,128,128]{2,1,0:T(8,128)(2,1)S(1)}, u32[]{:S(2)}, u32[]{:S(2)}) collective-permute-start(bf16[8,128,128]{2,1,0:T(8,128)(2,1)S(1)} %all_to_all.10.refs_2_), channel_id=1, source_target_pairs={{0,4},{4,0},{1,5},{5,1},{2,6},{6,2},{3,7},{7,3},{8,12},{12,8},{9,1... | collective-permute-start | bytes 786440 | tf_op jit(solution)/shard_map/ppermute | solution.py:40
  34.5 1.6 %collective-permute-start.6 = (bf16[8,128,128]{2,1,0:T(8,128)(2,1)S(1)}, bf16[8,128,128]{2,1,0:T(8,128)(2,1)S(1)}, u32[]{:S(2)}, u32[]{:S(2)}) collective-permute-start(bf16[8,128,128]{2,1,0:T(8,128)(2,1)S(1)} %tie.6.refs_3_), channel_id=1, source_target_pairs={{0,4},{4,0},{1,5},{5,1},{2,6},{6,2},{3,7},{7,3},{8,12},{12,8},{9,1... | collective-permute-start | bytes 786440 | tf_op jit(solution)/shard_map/ppermute | solution.py:40
  34.6 3.1 %collective-permute-start.1 = (bf16[8,128,128]{2,1,0:T(8,128)(2,1)S(1)}, bf16[8,128,128]{2,1,0:T(8,128)(2,1)S(1)}, u32[]{:S(2)}, u32[]{:S(2)}) collective-permute-start(bf16[8,128,128]{2,1,0:T(8,128)(2,1)S(1)} %tie.4.refs_5_), channel_id=1, source_target_pairs={{0,4},{4,0},{1,5},{5,1},{2,6},{6,2},{3,7},{7,3},{8,12},{12,8},{9,1... | collective-permute-start | bytes 786440 | tf_op jit(solution)/shard_map/ppermute | solution.py:40
  35.1 2.6 %copy-start.1 = (bf16[128,128]{1,0:T(8,128)(2,1)S(1)}, bf16[128,128]{1,0:T(8,128)(2,1)}, u32[]{:S(2)}) copy-start(bf16[128,128]{1,0:T(8,128)(2,1)} %refs_5_.1) | copy-start | bytes 98308
  35.1 2.6 %collective-permute-start.3 = (bf16[8,128,128]{2,1,0:T(8,128)(2,1)S(1)}, bf16[8,128,128]{2,1,0:T(8,128)(2,1)S(1)}, u32[]{:S(2)}, u32[]{:S(2)}) collective-permute-start(bf16[8,128,128]{2,1,0:T(8,128)(2,1)S(1)} %tie.5.refs_6_), channel_id=1, source_target_pairs={{0,4},{4,0},{1,5},{5,1},{2,6},{6,2},{3,7},{7,3},{8,12},{12,8},{9,1... | collective-permute-start | bytes 786440 | tf_op jit(solution)/shard_map/ppermute | solution.py:40
  38.5 12.7 %copy-start.2 = (bf16[128,128]{1,0:T(8,128)(2,1)S(1)}, bf16[128,128]{1,0:T(8,128)(2,1)}, u32[]{:S(2)}) copy-start(bf16[128,128]{1,0:T(8,128)(2,1)} %weight_ref.1) | copy-start | bytes 98308
  38.5 12.6 %copy-start.3 = (f32[128]{0:T(128)S(1)}, f32[128]{0:T(128)}, u32[]{:S(2)}) copy-start(f32[128]{0:T(128)} %param.10) | copy-start | bytes 1540
  38.5 16.2 %collective-permute-start.10 = (bf16[32,512,128]{2,1,0:T(8,128)(2,1)S(1)}, bf16[32,512,128]{2,1,0:T(8,128)(2,1)S(1)}, u32[]{:S(2)}, u32[]{:S(2)}) collective-permute-start(bf16[32,512,128]{2,1,0:T(8,128)(2,1)S(1)} %tie.7), channel_id=1, source_target_pairs={{0,4},{4,0},{1,5},{5,1},{2,6},{6,2},{3,7},{7,3},{8,12},{12,8},{9,1... | collective-permute-start | bytes 12582920 | tf_op jit(solution)/shard_map/ppermute | solution.py:40
  38.7 8.0 %collective-permute-start.7 = (bf16[640,128]{1,0:T(8,128)(2,1)S(1)}, bf16[640,128]{1,0:T(8,128)(2,1)S(1)}, u32[]{:S(2)}, u32[]{:S(2)}) collective-permute-start(bf16[640,128]{1,0:T(8,128)(2,1)S(1)} %forward.5.p0.token_ref), channel_id=1, source_target_pairs={{0,1},{1,2},{2,3},{3,0},{4,5},{5,6},{6,7},{7,4},{8,9},{9,10},{10,1... | collective-permute-start | bytes 491528 | tf_op jit(solution)/shard_map/ppermute | solution.py:40
  40.1 11.0 %collective-permute-start.8 = (bf16[640,128]{1,0:T(8,128)(2,1)S(1)}, bf16[640,128]{1,0:T(8,128)(2,1)S(1)}, u32[]{:S(2)}, u32[]{:S(2)}) collective-permute-start(bf16[640,128]{1,0:T(8,128)(2,1)S(1)} %forward.5.p0.token_ref), channel_id=1, source_target_pairs={{0,2},{1,3},{2,0},{3,1},{4,6},{5,7},{6,4},{7,5},{8,10},{9,11},{10,... | collective-permute-start | bytes 491528 | tf_op jit(solution)/shard_map/ppermute | solution.py:40
  43.7 7.5 %collective-permute-start.9 = (bf16[640,128]{1,0:T(8,128)(2,1)S(1)}, bf16[640,128]{1,0:T(8,128)(2,1)S(1)}, u32[]{:S(2)}, u32[]{:S(2)}) collective-permute-start(bf16[640,128]{1,0:T(8,128)(2,1)S(1)} %forward.5.p0.token_ref), channel_id=1, source_target_pairs={{0,3},{1,0},{2,1},{3,2},{4,7},{5,4},{6,5},{7,6},{8,11},{9,8},{10,9... | collective-permute-start | bytes 491528 | tf_op jit(solution)/shard_map/ppermute | solution.py:40
  52.1 2.5 %collective-permute-start.11 = (bf16[592,128]{1,0:T(8,128)(2,1)S(1)}, bf16[592,128]{1,0:T(8,128)(2,1)S(1)}, u32[]{:S(2)}, u32[]{:S(2)}) collective-permute-start(bf16[592,128]{1,0:T(8,128)(2,1)S(1)} %get-tuple-element.15.give_ref), channel_id=1, source_target_pairs={{0,4},{4,0},{1,5},{5,1},{2,6},{6,2},{3,7},{7,3},{8,12},{12,8},{9,1... | collective-permute-start | bytes 454664 | tf_op jit(solution)/shard_map/ppermute | solution.py:40
  55.0 8.4 %collective-permute-start.12 = (bf16[1104,128]{1,0:T(8,128)(2,1)S(1)}, bf16[1104,128]{1,0:T(8,128)(2,1)S(1)}, u32[]{:S(2)}, u32[]{:S(2)}) collective-permute-start(bf16[1104,128]{1,0:T(8,128)(2,1)S(1)} %backward.5), channel_id=1, source_target_pairs={{0,8},{8,16},{16,24},{24,0},{1,9},{9,17},{17,25},{25,1},{2,10},{10... | collective-permute-start | bytes 847880 | tf_op jit(solution)/shard_map/ppermute | solution.py:40
  55.4 9.7 %collective-permute-start.13 = (bf16[1104,128]{1,0:T(8,128)(2,1)S(1)}, bf16[1104,128]{1,0:T(8,128)(2,1)S(1)}, u32[]{:S(2)}, u32[]{:S(2)}) collective-permute-start(bf16[1104,128]{1,0:T(8,128)(2,1)S(1)} %backward.6), channel_id=1, source_target_pairs={{0,16},{8,24},{16,0},{24,8},{1,17},{9,25},{17,1},{25,9},{2,18},{10... | collective-permute-start | bytes 847880 | tf_op jit(solution)/shard_map/ppermute | solution.py:40
  58.4 13.4 %collective-permute-start.14 = (bf16[1104,128]{1,0:T(8,128)(2,1)S(1)}, bf16[1104,128]{1,0:T(8,128)(2,1)S(1)}, u32[]{:S(2)}, u32[]{:S(2)}) collective-permute-start(bf16[1104,128]{1,0:T(8,128)(2,1)S(1)} %backward.7), channel_id=1, source_target_pairs={{0,24},{8,0},{16,8},{24,16},{1,25},{9,1},{17,9},{25,17},{2,26},{10... | collective-permute-start | bytes 847880 | tf_op jit(solution)/shard_map/ppermute | solution.py:40
  88.7 3.0 %collective-permute-start.15 = (f32[64,128]{1,0:T(8,128)S(1)}, f32[64,128]{1,0:T(8,128)S(1)}, u32[]{:S(2)}, u32[]{:S(2)}) collective-permute-start(f32[64,128]{1,0:T(8,128)S(1)} %finish_terms.1), channel_id=1, source_target_pairs={{0,4},{4,0},{1,5},{5,1},{2,6},{6,2},{3,7},{7,3},{8,12},{12,8},{9,1... | collective-permute-start | bytes 98312 | tf_op jit(solution)/shard_map/ppermute | solution.py:40

commit v7 on v6

--- a/solution.py
+++ b/solution.py
@@ -47,22 +47,17 @@
         return carry
 
     lax.fori_loop(0, Z * X, clear, 0)
-    x, core = me_ref[0], me_ref[1]
-
     def place(k, carry):
-        col = me_ref[4 + SLOTS + k]
-        offset = (x - (col >> 1) + X) & (X - 1)
-        at = offset * Z + (col >> 3)
-        span = pl.ds(pl.multiple_of(me_ref[4 + k] * T, T), T)
-        own = (col & 1) == core
-
-        @pl.when(own)
+        at = me_ref[4 + SLOTS + k]
+        span = pl.ds(pl.multiple_of(me_ref[4 + k], T), T)
+
+        @pl.when(at < Z * X)
         def _():
             mine_ref[at, span, :] = tiles_ref[k]
 
-        @pl.when(jnp.logical_not(own))
+        @pl.when(at >= Z * X)
         def _():
-            theirs_ref[at, span, :] = tiles_ref[k]
+            theirs_ref[at - Z * X, span, :] = tiles_ref[k]
 
         return carry
 
@@ -326,18 +321,21 @@
 def body(features, weight, bias_terms, cotangent, tile_values, tile_rows, tile_cols, tile_count):
     x, core, rep = lax.axis_index("x"), lax.axis_index("core"), lax.axis_index("rep")
     place = jnp.stack([x, core, rep, tile_count[0, 0]]).astype(jnp.int32)
-    me = jnp.concatenate([place, tile_rows[0, 0], tile_cols[0, 0]])
+    cols = tile_cols[0, 0]
+    half = (cols & 1) ^ core.astype(jnp.int32)
+    offset = (x.astype(jnp.int32) - (cols >> 1)) & (X - 1)
+    at = (half * X + offset) * Z + (cols >> 3)
+    me = jnp.concatenate([place, tile_rows[0, 0] * T, at])
     spread = jnp.broadcast_to(features, (Z, T, T))
     line = lax.all_to_all(spread, "z", 0, 0, tiled=True)
     halves = densify(me, tile_values[0, 0])
-    begun = forward(halves, [(0, 0, line)], None, F32)
-    near = [(1, 0, send(line, "core", C, 1))]
+    near = [(0, 0, line), (1, 0, send(line, "core", C, 1))]
     far = []
     for n in range(1, X):
-        block = tie(send(line, "x", X, n), begun)
+        block = tie(send(line, "x", X, n), halves[0])
         far += [(0, n, block), (1, n, send(block, "core", C, 1))]
     late = [far[3], far[5]]
-    begun = forward(halves, near + far[:3] + far[4:5], begun, F32)
+    begun = forward(halves, near + far[:3] + far[4:5], None, F32)
     partial = forward(halves, late, begun, BF16, cotangent)
 
     partials = [partial] + [send(partial, "rep", Q, n) for n in range(1, Q)]

time: 93.4 us -> 93.4 us (level)
  starting transfers between devices: 20.6 us -> 21.9 us
    ppermute x16, starting transfers between devices: 20.6 us -> 21.9 us  [send(): return lax.ppermute(array, axis, shift(axis, size, by))]
    pallas_call x3 -> x2, Pallas kernels: 2.68 us -> 2.51 us  [forward(): pl.pallas_call(kernel, in_specs=[VMEM] * (2 + count + len(extra)), out_sp...]
  transfers between devices with their start and end apart: 16 -> 16, of which waited for: 6 -> 7; matrix products, arithmetic and copies ran while one was open for 1% -> 1% of each run, Pallas kernels for 11% -> 10%
where the time goes in v7:
time: 93.4 us; the launch traced here: 93.2 us
  blocking collectives  35.3 us (38%)
  starting transfers between devices  21.9 us (23%)
  waiting for transfers between devices  19.6 us (21%)
  Pallas kernels  10.5 us (11%)
  local copies, waits for them, and re-layouts  3.08 us (3%)
  between operations  1.44 us (2%)
  other arithmetic  1.39 us (1%)
    ppermute x16, starting transfers between devices, send(): return lax.ppermute(array, axis, shift(axis, size, by))  21.9 us
    ppermute x16, waiting for transfers between devices, send(): return lax.ppermute(array, axis, shift(axis, size, by))  19.6 us
    all_to_all x1, blocking collectives, body(): line = lax.all_to_all(spread, 'z', 0, 0, tiled=True)  18.4 us
    all_to_all x1, blocking collectives, body(): received = lax.all_to_all(blocks, 'z', 0, 0, tiled=True)  16.9 us
    pallas_call x1, Pallas kernels, densify(): pl.pallas_call(densify_kernel, in_specs=[SMEM, VMEM], out_specs=[VMEM] *...  3 us
    pallas_call x2, Pallas kernels, forward(): pl.pallas_call(kernel, in_specs=[VMEM] * (2 + count + len(extra)), out_sp...  2.51 us
    unnamed x8, local copies, waits for them, and re-layouts  2.21 us
  transfers between devices with their start and end apart: 16, of which 7 were waited for; matrix products, arithmetic and copies ran while one was open for 1% of the time, Pallas kernels for 10%

profile of v7, /device:TPU:3, one launch (start us, length us, event | category | flops | bytes accessed | tf_op | source)
XLA Modules:
  0.0 93.2 jit_solution(11950695184117713848)
XLA Ops:
  0.6 0.8 broadcast_in_dim.3
  1.4 18.4 %all_to_all.10.refs_2_ = bf16[8,128,128]{2,1,0:T(8,128)(2,1)S(1)} all-to-all(bf16[8,128,128]{2,1,0:T(8,128)(2,1)S(1)} %broadcast_in_dim.3), channel_id=1, replica_groups=mesh['z'=8,'x'=4,'core'=2,'rep'=4] {'z'}, dimensions={0} | all-to-all | bytes 524288 | tf_op jit(solution)/shard_map/all_to_all | solution.py:330
  19.8 1.2 %collective-permute-start.5 = (bf16[8,128,128]{2,1,0:T(8,128)(2,1)S(1)}, bf16[8,128,128]{2,1,0:T(8,128)(2,1)S(1)}, u32[]{:S(2)}, u32[]{:S(2)}) collective-permute-start(bf16[8,128,128]{2,1,0:T(8,128)(2,1)S(1)} %all_to_all.10.refs_2_), channel_id=1, source_target_pairs={{0,8},{8,16},{16,24},{24,0},{1,9},{9,17},{17,25},{25,1},{2,10},{10... | collective-permute-start | bytes 786440 | tf_op jit(solution)/shard_map/ppermute | solution.py:40
  21.6 0.9 collective-permute-start
  22.6 1.9 %collective-permute-start.2 = (bf16[8,128,128]{2,1,0:T(8,128)(2,1)S(1)}, bf16[8,128,128]{2,1,0:T(8,128)(2,1)S(1)}, u32[]{:S(2)}, u32[]{:S(2)}) collective-permute-start(bf16[8,128,128]{2,1,0:T(8,128)(2,1)S(1)} %all_to_all.10.refs_2_), channel_id=1, source_target_pairs={{0,24},{8,0},{16,8},{24,16},{1,25},{9,1},{17,9},{25,17},{2,26},{10... | collective-permute-start | bytes 786440 | tf_op jit(solution)/shard_map/ppermute | solution.py:40
  24.4 0.7 add_bitcast_fusion
  25.1 0.1 concatenate.10.me_ref
  25.2 2.2 %copy-done = bf16[1,1,128,128,128]{4,3,2,1,0:T(8,128)(2,1)S(1)} copy-done((bf16[1,1,128,128,128]{4,3,2,1,0:T(8,128)(2,1)S(1)}, bf16[1,1,128,128,128]{4,3,2,1,0:T(8,128)(2,1)}, u32[]{:S(2)}) %copy-start) | copy-done | bytes 4194328
  27.4 3.0 %densify.1 = (bf16[32,512,128]{2,1,0:T(8,128)(2,1)S(1)}, bf16[32,512,128]{2,1,0:T(8,128)(2,1)S(1)}) custom-call(s32[260]{0:T(512)S(1)} %concatenate.10.me_ref, bf16[128,128,128]{2,1,0:T(8,128)(2,1)S(1)} %bitcast.13), custom_call_target="tpu_custom_call" | custom-call | bytes 12582912 | tf_op jit(solution)/shard_map/densify/pallas_call | solution.py:68
  30.4 3.5 %collective-permute-start.4 = (bf16[8,128,128]{2,1,0:T(8,128)(2,1)S(1)}, bf16[8,128,128]{2,1,0:T(8,128)(2,1)S(1)}, u32[]{:S(2)}, u32[]{:S(2)}) collective-permute-start(bf16[8,128,128]{2,1,0:T(8,128)(2,1)S(1)} %all_to_all.10.refs_2_), channel_id=1, source_target_pairs={{0,4},{4,0},{1,5},{5,1},{2,6},{6,2},{3,7},{7,3},{8,12},{12,8},{9,1... | collective-permute-start | bytes 786440 | tf_op jit(solution)/shard_map/ppermute | solution.py:40
  33.9 0.0 collective-permute-done.5.block_ref
  33.9 0.1 collective-permute-start.6
  34.0 0.0 collective-permute-done.block_ref
  34.0 0.8 collective-permute-start.1
  34.9 0.8 collective-permute-done.2.block_ref
  35.7 1.2 %collective-permute-start.3 = (bf16[8,128,128]{2,1,0:T(8,128)(2,1)S(1)}, bf16[8,128,128]{2,1,0:T(8,128)(2,1)S(1)}, u32[]{:S(2)}, u32[]{:S(2)}) collective-permute-start(bf16[8,128,128]{2,1,0:T(8,128)(2,1)S(1)} %tie.5.refs_7_), channel_id=1, source_target_pairs={{0,4},{4,0},{1,5},{5,1},{2,6},{6,2},{3,7},{7,3},{8,12},{12,8},{9,1... | collective-permute-start | bytes 786440 | tf_op jit(solution)/shard_map/ppermute | solution.py:40
  36.9 1.8 %forward.2.refs_4_ = f32[512,128]{1,0:T(8,128)S(1)} custom-call(bf16[32,512,128]{2,1,0:T(8,128)(2,1)S(1)} %get-tuple-element.13.token_ref.refs_0_.mine_ref, bf16[32,512,128]{2,1,0:T(8,128)(2,1)S(1)} %get-tuple-element.14.refs_1_.block_ref, bf16[8,128,128]{2,1,0:T(8,128)(2,1)S(1)} %all_to_all.10.refs_2_, ...), custom_call_target="tpu_custom_call" | custom-call | flops 805306368 | bytes 6291456 | tf_op jit(solution)/shard_map/forward/pallas_call | solution.py:100
  38.7 0.0 collective-permute-done.1.refs_2_
  38.7 0.7 forward.3.p0.token_ref
  39.5 0.0 copy-start.2
  39.5 0.0 copy-start.3
  39.5 0.1 collective-permute-start.10
  39.6 1.4 %collective-permute-start.7 = (bf16[640,128]{1,0:T(8,128)(2,1)S(1)}, bf16[640,128]{1,0:T(8,128)(2,1)S(1)}, u32[]{:S(2)}, u32[]{:S(2)}) collective-permute-start(bf16[640,128]{1,0:T(8,128)(2,1)S(1)} %forward.3.p0.token_ref), channel_id=1, source_target_pairs={{0,1},{1,2},{2,3},{3,0},{4,5},{5,6},{6,7},{7,4},{8,9},{9,10},{10,1... | collective-permute-start | bytes 491528 | tf_op jit(solution)/shard_map/ppermute | solution.py:40
  41.0 2.6 %collective-permute-start.8 = (bf16[640,128]{1,0:T(8,128)(2,1)S(1)}, bf16[640,128]{1,0:T(8,128)(2,1)S(1)}, u32[]{:S(2)}, u32[]{:S(2)}) collective-permute-start(bf16[640,128]{1,0:T(8,128)(2,1)S(1)} %forward.3.p0.token_ref), channel_id=1, source_target_pairs={{0,2},{1,3},{2,0},{3,1},{4,6},{5,7},{6,4},{7,5},{8,10},{9,11},{10,... | collective-permute-start | bytes 491528 | tf_op jit(solution)/shard_map/ppermute | solution.py:40
  43.6 1.1 %collective-permute-start.9 = (bf16[640,128]{1,0:T(8,128)(2,1)S(1)}, bf16[640,128]{1,0:T(8,128)(2,1)S(1)}, u32[]{:S(2)}, u32[]{:S(2)}) collective-permute-start(bf16[640,128]{1,0:T(8,128)(2,1)S(1)} %forward.3.p0.token_ref), channel_id=1, source_target_pairs={{0,3},{1,0},{2,1},{3,2},{4,7},{5,4},{6,5},{7,6},{8,11},{9,8},{10,9... | collective-permute-start | bytes 491528 | tf_op jit(solution)/shard_map/ppermute | solution.py:40
  44.7 0.1 pad_add_fusion.me_ref
  44.7 1.6 %collective-permute-done.7.p1 = bf16[640,128]{1,0:T(8,128)(2,1)S(1)} collective-permute-done((bf16[640,128]{1,0:T(8,128)(2,1)S(1)}, bf16[640,128]{1,0:T(8,128)(2,1)S(1)}, u32[]{:S(2)}, u32[]{:S(2)}) %collective-permute-start.7) | collective-permute-done | bytes 163872 | tf_op jit(solution)/shard_map/ppermute | solution.py:40
  46.4 4.6 %collective-permute-done.8.p2 = bf16[640,128]{1,0:T(8,128)(2,1)S(1)} collective-permute-done((bf16[640,128]{1,0:T(8,128)(2,1)S(1)}, bf16[640,128]{1,0:T(8,128)(2,1)S(1)}, u32[]{:S(2)}, u32[]{:S(2)}) %collective-permute-start.8) | collective-permute-done | bytes 163872 | tf_op jit(solution)/shard_map/ppermute | solution.py:40
  51.0 1.0 %middle.1 = (f32[128,128]{1,0:T(8,128)S(1)}, bf16[592,128]{1,0:T(8,128)(2,1)S(1)}, f32[64,128]{1,0:T(8,128)S(1)}) custom-call(s32[4]{0:T(128)S(1)} %pad_add_fusion.me_ref, bf16[640,128]{1,0:T(8,128)(2,1)S(1)} %forward.3.p0.token_ref, bf16[640,128]{1,0:T(8,128)(2,1)S(1)} %collective-permute-done.7.p1, bf16[640,128]{1,0:T(8,128)(2,1)S(1)} %collective-permute-done.8.p2, ...), custom_call_target="tpu_custom_call" | custom-call | flops 50331648 | bytes 1048576 | tf_op jit(solution)/shard_map/middle/pallas_call | solution.py:165
  52.0 1.3 %collective-permute-start.11 = (bf16[592,128]{1,0:T(8,128)(2,1)S(1)}, bf16[592,128]{1,0:T(8,128)(2,1)S(1)}, u32[]{:S(2)}, u32[]{:S(2)}) collective-permute-start(bf16[592,128]{1,0:T(8,128)(2,1)S(1)} %get-tuple-element.15.give_ref), channel_id=1, source_target_pairs={{0,4},{4,0},{1,5},{5,1},{2,6},{6,2},{3,7},{7,3},{8,12},{12,8},{9,1... | collective-permute-start | bytes 454664 | tf_op jit(solution)/shard_map/ppermute | solution.py:40
  53.4 1.2 %backward_own.1.begun_ref = f32[4,8,128,128]{3,2,1,0:T(8,128)S(1)} custom-call(bf16[32,512,128]{2,1,0:T(8,128)(2,1)S(1)} %get-tuple-element.13.token_ref.refs_0_.mine_ref, bf16[592,128]{1,0:T(8,128)(2,1)S(1)} %get-tuple-element.15.give_ref), custom_call_target="tpu_custom_call" | custom-call | flops 536870912 | bytes 4194304 | tf_op jit(solution)/shard_map/backward_own/pallas_call | solution.py:213
  54.6 0.0 collective-permute-done.11.got_ref
  54.6 0.3 backward.5
  54.9 1.1 %collective-permute-start.12 = (bf16[1104,128]{1,0:T(8,128)(2,1)S(1)}, bf16[1104,128]{1,0:T(8,128)(2,1)S(1)}, u32[]{:S(2)}, u32[]{:S(2)}) collective-permute-start(bf16[1104,128]{1,0:T(8,128)(2,1)S(1)} %backward.5), channel_id=1, source_target_pairs={{0,8},{8,16},{16,24},{24,0},{1,9},{9,17},{17,25},{25,1},{2,10},{10... | collective-permute-start | bytes 847880 | tf_op jit(solution)/shard_map/ppermute | solution.py:40
  56.0 0.3 backward.6
  56.4 1.7 %collective-permute-start.13 = (bf16[1104,128]{1,0:T(8,128)(2,1)S(1)}, bf16[1104,128]{1,0:T(8,128)(2,1)S(1)}, u32[]{:S(2)}, u32[]{:S(2)}) collective-permute-start(bf16[1104,128]{1,0:T(8,128)(2,1)S(1)} %backward.6), channel_id=1, source_target_pairs={{0,16},{8,24},{16,0},{24,8},{1,17},{9,25},{17,1},{25,9},{2,18},{10... | collective-permute-start | bytes 847880 | tf_op jit(solution)/shard_map/ppermute | solution.py:40
  58.1 0.3 backward.7
  58.4 1.0 %collective-permute-start.14 = (bf16[1104,128]{1,0:T(8,128)(2,1)S(1)}, bf16[1104,128]{1,0:T(8,128)(2,1)S(1)}, u32[]{:S(2)}, u32[]{:S(2)}) collective-permute-start(bf16[1104,128]{1,0:T(8,128)(2,1)S(1)} %backward.7), channel_id=1, source_target_pairs={{0,24},{8,0},{16,8},{24,16},{1,25},{9,1},{17,9},{25,17},{2,26},{10... | collective-permute-start | bytes 847880 | tf_op jit(solution)/shard_map/ppermute | solution.py:40
  59.4 0.9 backward.4
  60.3 3.0 %collective-permute-done.12.r1 = bf16[1104,128]{1,0:T(8,128)(2,1)S(1)} collective-permute-done((bf16[1104,128]{1,0:T(8,128)(2,1)S(1)}, bf16[1104,128]{1,0:T(8,128)(2,1)S(1)}, u32[]{:S(2)}, u32[]{:S(2)}) %collective-permute-start.12) | collective-permute-done | bytes 282656 | tf_op jit(solution)/shard_map/ppermute | solution.py:40
  63.3 2.6 %collective-permute-done.13.r2 = bf16[1104,128]{1,0:T(8,128)(2,1)S(1)} collective-permute-done((bf16[1104,128]{1,0:T(8,128)(2,1)S(1)}, bf16[1104,128]{1,0:T(8,128)(2,1)S(1)}, u32[]{:S(2)}, u32[]{:S(2)}) %collective-permute-start.13) | collective-permute-done | bytes 282656 | tf_op jit(solution)/shard_map/ppermute | solution.py:40
  66.0 6.7 %collective-permute-done.14.r3 = bf16[1104,128]{1,0:T(8,128)(2,1)S(1)} collective-permute-done((bf16[1104,128]{1,0:T(8,128)(2,1)S(1)}, bf16[1104,128]{1,0:T(8,128)(2,1)S(1)}, u32[]{:S(2)}, u32[]{:S(2)}) %collective-permute-start.14) | collective-permute-done | bytes 282656 | tf_op jit(solution)/shard_map/ppermute | solution.py:40
  72.7 0.2 line_sum.1
  72.8 16.9 %all_to_all.11.in_ref = bf16[8,208,128]{2,1,0:T(8,128)(2,1)S(1)} all-to-all(bf16[8,208,128]{2,1,0:T(8,128)(2,1)S(1)} %line_sum.1), channel_id=1, replica_groups=mesh['z'=8,'x'=4,'core'=2,'rep'=4] {'z'}, dimensions={0} | all-to-all | bytes 851968 | tf_op jit(solution)/shard_map/all_to_all | solution.py:354
  89.8 1.9 %collective-permute-start.15 = (f32[64,128]{1,0:T(8,128)S(1)}, f32[64,128]{1,0:T(8,128)S(1)}, u32[]{:S(2)}, u32[]{:S(2)}) collective-permute-start(f32[64,128]{1,0:T(8,128)S(1)} %finish_terms.1), channel_id=1, source_target_pairs={{0,4},{4,0},{1,5},{5,1},{2,6},{6,2},{3,7},{7,3},{8,12},{12,8},{9,1... | collective-permute-start | bytes 98312 | tf_op jit(solution)/shard_map/ppermute | solution.py:40
  91.7 0.7 finish_grad.1
  92.4 0.1 collective-permute-done.15
  92.6 0.6 maximum_select_fusion
  (15 shorter events, 0.0 us)
Async XLA Ops:
  19.8 14.1 %collective-permute-start.5 = (bf16[8,128,128]{2,1,0:T(8,128)(2,1)S(1)}, bf16[8,128,128]{2,1,0:T(8,128)(2,1)S(1)}, u32[]{:S(2)}, u32[]{:S(2)}) collective-permute-start(bf16[8,128,128]{2,1,0:T(8,128)(2,1)S(1)} %all_to_all.10.refs_2_), channel_id=1, source_target_pairs={{0,8},{8,16},{16,24},{24,0},{1,9},{9,17},{17,25},{25,1},{2,10},{10... | collective-permute-start | bytes 786440 | tf_op jit(solution)/shard_map/ppermute | solution.py:40
  21.6 12.4 %collective-permute-start = (bf16[8,128,128]{2,1,0:T(8,128)(2,1)S(1)}, bf16[8,128,128]{2,1,0:T(8,128)(2,1)S(1)}, u32[]{:S(2)}, u32[]{:S(2)}) collective-permute-start(bf16[8,128,128]{2,1,0:T(8,128)(2,1)S(1)} %all_to_all.10.refs_2_), channel_id=1, source_target_pairs={{0,16},{8,24},{16,0},{24,8},{1,17},{9,25},{17,1},{25,9},{2,18},{10... | collective-permute-start | bytes 786440 | tf_op jit(solution)/shard_map/ppermute | solution.py:40
  22.6 13.1 %collective-permute-start.2 = (bf16[8,128,128]{2,1,0:T(8,128)(2,1)S(1)}, bf16[8,128,128]{2,1,0:T(8,128)(2,1)S(1)}, u32[]{:S(2)}, u32[]{:S(2)}) collective-permute-start(bf16[8,128,128]{2,1,0:T(8,128)(2,1)S(1)} %all_to_all.10.refs_2_), channel_id=1, source_target_pairs={{0,24},{8,0},{16,8},{24,16},{1,25},{9,1},{17,9},{25,17},{2,26},{10... | collective-permute-start | bytes 786440 | tf_op jit(solution)/shard_map/ppermute | solution.py:40
  25.2 2.2 %copy-start = (bf16[1,1,128,128,128]{4,3,2,1,0:T(8,128)(2,1)S(1)}, bf16[1,1,128,128,128]{4,3,2,1,0:T(8,128)(2,1)}, u32[]{:S(2)}) copy-start(bf16[1,1,128,128,128]{4,3,2,1,0:T(8,128)(2,1)} %param.12) | copy-start | bytes 12582916
  30.4 6.5 %collective-permute-start.4 = (bf16[8,128,128]{2,1,0:T(8,128)(2,1)S(1)}, bf16[8,128,128]{2,1,0:T(8,128)(2,1)S(1)}, u32[]{:S(2)}, u32[]{:S(2)}) collective-permute-start(bf16[8,128,128]{2,1,0:T(8,128)(2,1)S(1)} %all_to_all.10.refs_2_), channel_id=1, source_target_pairs={{0,4},{4,0},{1,5},{5,1},{2,6},{6,2},{3,7},{7,3},{8,12},{12,8},{9,1... | collective-permute-start | bytes 786440 | tf_op jit(solution)/shard_map/ppermute | solution.py:40
  33.9 3.0 %collective-permute-start.6 = (bf16[8,128,128]{2,1,0:T(8,128)(2,1)S(1)}, bf16[8,128,128]{2,1,0:T(8,128)(2,1)S(1)}, u32[]{:S(2)}, u32[]{:S(2)}) collective-permute-start(bf16[8,128,128]{2,1,0:T(8,128)(2,1)S(1)} %tie.6.refs_4_), channel_id=1, source_target_pairs={{0,4},{4,0},{1,5},{5,1},{2,6},{6,2},{3,7},{7,3},{8,12},{12,8},{9,1... | collective-permute-start | bytes 786440 | tf_op jit(solution)/shard_map/ppermute | solution.py:40
  34.0 4.7 %collective-permute-start.1 = (bf16[8,128,128]{2,1,0:T(8,128)(2,1)S(1)}, bf16[8,128,128]{2,1,0:T(8,128)(2,1)S(1)}, u32[]{:S(2)}, u32[]{:S(2)}) collective-permute-start(bf16[8,128,128]{2,1,0:T(8,128)(2,1)S(1)} %tie.4.refs_6_), channel_id=1, source_target_pairs={{0,4},{4,0},{1,5},{5,1},{2,6},{6,2},{3,7},{7,3},{8,12},{12,8},{9,1... | collective-permute-start | bytes 786440 | tf_op jit(solution)/shard_map/ppermute | solution.py:40
  35.7 3.1 %collective-permute-start.3 = (bf16[8,128,128]{2,1,0:T(8,128)(2,1)S(1)}, bf16[8,128,128]{2,1,0:T(8,128)(2,1)S(1)}, u32[]{:S(2)}, u32[]{:S(2)}) collective-permute-start(bf16[8,128,128]{2,1,0:T(8,128)(2,1)S(1)} %tie.5.refs_7_), channel_id=1, source_target_pairs={{0,4},{4,0},{1,5},{5,1},{2,6},{6,2},{3,7},{7,3},{8,12},{12,8},{9,1... | collective-permute-start | bytes 786440 | tf_op jit(solution)/shard_map/ppermute | solution.py:40
  36.9 1.8 %copy-start.1 = (bf16[128,128]{1,0:T(8,128)(2,1)S(1)}, bf16[128,128]{1,0:T(8,128)(2,1)}, u32[]{:S(2)}) copy-start(bf16[128,128]{1,0:T(8,128)(2,1)} %refs_5_.1) | copy-start | bytes 98308
  39.5 11.5 %copy-start.2 = (bf16[128,128]{1,0:T(8,128)(2,1)S(1)}, bf16[128,128]{1,0:T(8,128)(2,1)}, u32[]{:S(2)}) copy-start(bf16[128,128]{1,0:T(8,128)(2,1)} %weight_ref.1) | copy-start | bytes 98308
  39.5 11.5 %copy-start.3 = (f32[128]{0:T(128)S(1)}, f32[128]{0:T(128)}, u32[]{:S(2)}) copy-start(f32[128]{0:T(128)} %param.10) | copy-start | bytes 1540
  39.5 15.1 %collective-permute-start.10 = (bf16[32,512,128]{2,1,0:T(8,128)(2,1)S(1)}, bf16[32,512,128]{2,1,0:T(8,128)(2,1)S(1)}, u32[]{:S(2)}, u32[]{:S(2)}) collective-permute-start(bf16[32,512,128]{2,1,0:T(8,128)(2,1)S(1)} %tie.7), channel_id=1, source_target_pairs={{0,4},{4,0},{1,5},{5,1},{2,6},{6,2},{3,7},{7,3},{8,12},{12,8},{9,1... | collective-permute-start | bytes 12582920 | tf_op jit(solution)/shard_map/ppermute | solution.py:40
  39.6 6.8 %collective-permute-start.7 = (bf16[640,128]{1,0:T(8,128)(2,1)S(1)}, bf16[640,128]{1,0:T(8,128)(2,1)S(1)}, u32[]{:S(2)}, u32[]{:S(2)}) collective-permute-start(bf16[640,128]{1,0:T(8,128)(2,1)S(1)} %forward.3.p0.token_ref), channel_id=1, source_target_pairs={{0,1},{1,2},{2,3},{3,0},{4,5},{5,6},{6,7},{7,4},{8,9},{9,10},{10,1... | collective-permute-start | bytes 491528 | tf_op jit(solution)/shard_map/ppermute | solution.py:40
  41.0 10.0 %collective-permute-start.8 = (bf16[640,128]{1,0:T(8,128)(2,1)S(1)}, bf16[640,128]{1,0:T(8,128)(2,1)S(1)}, u32[]{:S(2)}, u32[]{:S(2)}) collective-permute-start(bf16[640,128]{1,0:T(8,128)(2,1)S(1)} %forward.3.p0.token_ref), channel_id=1, source_target_pairs={{0,2},{1,3},{2,0},{3,1},{4,6},{5,7},{6,4},{7,5},{8,10},{9,11},{10,... | collective-permute-start | bytes 491528 | tf_op jit(solution)/shard_map/ppermute | solution.py:40
  43.6 7.4 %collective-permute-start.9 = (bf16[640,128]{1,0:T(8,128)(2,1)S(1)}, bf16[640,128]{1,0:T(8,128)(2,1)S(1)}, u32[]{:S(2)}, u32[]{:S(2)}) collective-permute-start(bf16[640,128]{1,0:T(8,128)(2,1)S(1)} %forward.3.p0.token_ref), channel_id=1, source_target_pairs={{0,3},{1,0},{2,1},{3,2},{4,7},{5,4},{6,5},{7,6},{8,11},{9,8},{10,9... | collective-permute-start | bytes 491528 | tf_op jit(solution)/shard_map/ppermute | solution.py:40
  52.0 2.6 %collective-permute-start.11 = (bf16[592,128]{1,0:T(8,128)(2,1)S(1)}, bf16[592,128]{1,0:T(8,128)(2,1)S(1)}, u32[]{:S(2)}, u32[]{:S(2)}) collective-permute-start(bf16[592,128]{1,0:T(8,128)(2,1)S(1)} %get-tuple-element.15.give_ref), channel_id=1, source_target_pairs={{0,4},{4,0},{1,5},{5,1},{2,6},{6,2},{3,7},{7,3},{8,12},{12,8},{9,1... | collective-permute-start | bytes 454664 | tf_op jit(solution)/shard_map/ppermute | solution.py:40
  54.9 8.4 %collective-permute-start.12 = (bf16[1104,128]{1,0:T(8,128)(2,1)S(1)}, bf16[1104,128]{1,0:T(8,128)(2,1)S(1)}, u32[]{:S(2)}, u32[]{:S(2)}) collective-permute-start(bf16[1104,128]{1,0:T(8,128)(2,1)S(1)} %backward.5), channel_id=1, source_target_pairs={{0,8},{8,16},{16,24},{24,0},{1,9},{9,17},{17,25},{25,1},{2,10},{10... | collective-permute-start | bytes 847880 | tf_op jit(solution)/shard_map/ppermute | solution.py:40
  56.4 9.6 %collective-permute-start.13 = (bf16[1104,128]{1,0:T(8,128)(2,1)S(1)}, bf16[1104,128]{1,0:T(8,128)(2,1)S(1)}, u32[]{:S(2)}, u32[]{:S(2)}) collective-permute-start(bf16[1104,128]{1,0:T(8,128)(2,1)S(1)} %backward.6), channel_id=1, source_target_pairs={{0,16},{8,24},{16,0},{24,8},{1,17},{9,25},{17,1},{25,9},{2,18},{10... | collective-permute-start | bytes 847880 | tf_op jit(solution)/shard_map/ppermute | solution.py:40
  58.4 14.2 %collective-permute-start.14 = (bf16[1104,128]{1,0:T(8,128)(2,1)S(1)}, bf16[1104,128]{1,0:T(8,128)(2,1)S(1)}, u32[]{:S(2)}, u32[]{:S(2)}) collective-permute-start(bf16[1104,128]{1,0:T(8,128)(2,1)S(1)} %backward.7), channel_id=1, source_target_pairs={{0,24},{8,0},{16,8},{24,16},{1,25},{9,1},{17,9},{25,17},{2,26},{10... | collective-permute-start | bytes 847880 | tf_op jit(solution)/shard_map/ppermute | solution.py:40
  89.8 2.8 %collective-permute-start.15 = (f32[64,128]{1,0:T(8,128)S(1)}, f32[64,128]{1,0:T(8,128)S(1)}, u32[]{:S(2)}, u32[]{:S(2)}) collective-permute-start(f32[64,128]{1,0:T(8,128)S(1)} %finish_terms.1), channel_id=1, source_target_pairs={{0,4},{4,0},{1,5},{5,1},{2,6},{6,2},{3,7},{7,3},{8,12},{12,8},{9,1... | collective-permute-start | bytes 98312 | tf_op jit(solution)/shard_map/ppermute | solution.py:40

commit v8 on v6

--- a/solution.py
+++ b/solution.py
@@ -334,7 +334,7 @@
     near = [(1, 0, send(line, "core", C, 1))]
     far = []
     for n in range(1, X):
-        block = tie(send(line, "x", X, n), begun)
+        block = tie(send(line, "x", X, n), halves[0])
         far += [(0, n, block), (1, n, send(block, "core", C, 1))]
     late = [far[3], far[5]]
     begun = forward(halves, near + far[:3] + far[4:5], begun, F32)

time: 93.4 us -> 93.4 us (level)
  transfers between devices with their start and end apart: 16 -> 16, of which waited for: 6 -> 6; matrix products, arithmetic and copies ran while one was open for 1% -> 1% of each run, Pallas kernels for 11% -> 12%
where the time goes in v8:
time: 93.4 us; the launch traced here: 92.8 us
  blocking collectives  35.2 us (38%)
  starting transfers between devices  20.8 us (22%)
  waiting for transfers between devices  18.9 us (20%)
  Pallas kernels  12 us (13%)
  local copies, waits for them, and re-layouts  3.75 us (4%)
  between operations  1.47 us (2%)
    ppermute x16, starting transfers between devices, send(): return lax.ppermute(array, axis, shift(axis, size, by))  20.8 us
    ppermute x16, waiting for transfers between devices, send(): return lax.ppermute(array, axis, shift(axis, size, by))  18.9 us
    all_to_all x1, blocking collectives, body(): line = lax.all_to_all(spread, 'z', 0, 0, tiled=True)  18.4 us
    all_to_all x1, blocking collectives, body(): received = lax.all_to_all(blocks, 'z', 0, 0, tiled=True)  16.9 us
    pallas_call x1, Pallas kernels, densify(): pl.pallas_call(densify_kernel, in_specs=[SMEM, VMEM], out_specs=[VMEM] *...  4.37 us
    pallas_call x3, Pallas kernels, forward(): pl.pallas_call(kernel, in_specs=[VMEM] * (2 + count + len(extra)), out_sp...  2.68 us
    unnamed x8, local copies, waits for them, and re-layouts  2.21 us
  transfers between devices with their start and end apart: 16, of which 6 were waited for; matrix products, arithmetic and copies ran while one was open for 1% of the time, Pallas kernels for 12%

profile of v8, /device:TPU:3, one launch (start us, length us, event | category | flops | bytes accessed | tf_op | source)
XLA Modules:
  0.0 92.8 jit_solution(3819494302086107821)
XLA Ops:
  0.6 0.8 broadcast_in_dim.3
  1.4 18.4 %all_to_all.10.refs_2_ = bf16[8,128,128]{2,1,0:T(8,128)(2,1)S(1)} all-to-all(bf16[8,128,128]{2,1,0:T(8,128)(2,1)S(1)} %broadcast_in_dim.3), channel_id=1, replica_groups=mesh['z'=8,'x'=4,'core'=2,'rep'=4] {'z'}, dimensions={0} | all-to-all | bytes 524288 | tf_op jit(solution)/shard_map/all_to_all | solution.py:331
  19.8 1.2 %collective-permute-start.5 = (bf16[8,128,128]{2,1,0:T(8,128)(2,1)S(1)}, bf16[8,128,128]{2,1,0:T(8,128)(2,1)S(1)}, u32[]{:S(2)}, u32[]{:S(2)}) collective-permute-start(bf16[8,128,128]{2,1,0:T(8,128)(2,1)S(1)} %all_to_all.10.refs_2_), channel_id=1, source_target_pairs={{0,8},{8,16},{16,24},{24,0},{1,9},{9,17},{17,25},{25,1},{2,10},{10... | collective-permute-start | bytes 786440 | tf_op jit(solution)/shard_map/ppermute | solution.py:40
  21.0 0.8 collective-permute-start
  21.8 1.9 %collective-permute-start.2 = (bf16[8,128,128]{2,1,0:T(8,128)(2,1)S(1)}, bf16[8,128,128]{2,1,0:T(8,128)(2,1)S(1)}, u32[]{:S(2)}, u32[]{:S(2)}) collective-permute-start(bf16[8,128,128]{2,1,0:T(8,128)(2,1)S(1)} %all_to_all.10.refs_2_), channel_id=1, source_target_pairs={{0,24},{8,0},{16,8},{24,16},{1,25},{9,1},{17,9},{25,17},{2,26},{10... | collective-permute-start | bytes 786440 | tf_op jit(solution)/shard_map/ppermute | solution.py:40
  24.3 0.8 concatenate.10.me_ref
  25.1 2.2 %copy-done = bf16[1,1,128,128,128]{4,3,2,1,0:T(8,128)(2,1)S(1)} copy-done((bf16[1,1,128,128,128]{4,3,2,1,0:T(8,128)(2,1)S(1)}, bf16[1,1,128,128,128]{4,3,2,1,0:T(8,128)(2,1)}, u32[]{:S(2)}) %copy-start) | copy-done | bytes 4194328
  27.3 4.4 %densify.1 = (bf16[32,512,128]{2,1,0:T(8,128)(2,1)S(1)}, bf16[32,512,128]{2,1,0:T(8,128)(2,1)S(1)}) custom-call(s32[260]{0:T(512)S(1)} %concatenate.10.me_ref, bf16[128,128,128]{2,1,0:T(8,128)(2,1)S(1)} %bitcast.11), custom_call_target="tpu_custom_call" | custom-call | bytes 12582912 | tf_op jit(solution)/shard_map/densify/pallas_call | solution.py:73
  31.7 3.0 %collective-permute-start.4 = (bf16[8,128,128]{2,1,0:T(8,128)(2,1)S(1)}, bf16[8,128,128]{2,1,0:T(8,128)(2,1)S(1)}, u32[]{:S(2)}, u32[]{:S(2)}) collective-permute-start(bf16[8,128,128]{2,1,0:T(8,128)(2,1)S(1)} %all_to_all.10.refs_2_), channel_id=1, source_target_pairs={{0,4},{4,0},{1,5},{5,1},{2,6},{6,2},{3,7},{7,3},{8,12},{12,8},{9,1... | collective-permute-start | bytes 786440 | tf_op jit(solution)/shard_map/ppermute | solution.py:40
  34.6 0.1 collective-permute-start.6
  34.8 0.0 collective-permute-done.block_ref
  34.8 0.4 collective-permute-start.1
  35.2 0.0 collective-permute-done.2.block_ref
  35.2 1.0 %collective-permute-start.3 = (bf16[8,128,128]{2,1,0:T(8,128)(2,1)S(1)}, bf16[8,128,128]{2,1,0:T(8,128)(2,1)S(1)}, u32[]{:S(2)}, u32[]{:S(2)}) collective-permute-start(bf16[8,128,128]{2,1,0:T(8,128)(2,1)S(1)} %tie.5.refs_6_), channel_id=1, source_target_pairs={{0,4},{4,0},{1,5},{5,1},{2,6},{6,2},{3,7},{7,3},{8,12},{12,8},{9,1... | collective-permute-start | bytes 786440 | tf_op jit(solution)/shard_map/ppermute | solution.py:40
  36.2 0.4 forward.3.refs_7_
  36.6 0.0 copy-start.1
  36.6 0.0 collective-permute-done.4.refs_2_
  36.6 0.0 collective-permute-done.6.refs_4_
  36.6 1.5 %forward.4.refs_4_ = f32[512,128]{1,0:T(8,128)S(1)} custom-call(bf16[32,512,128]{2,1,0:T(8,128)(2,1)S(1)} %get-tuple-element.13.token_ref.refs_0_.mine_ref, bf16[32,512,128]{2,1,0:T(8,128)(2,1)S(1)} %get-tuple-element.14.refs_1_.block_ref, bf16[8,128,128]{2,1,0:T(8,128)(2,1)S(1)} %collective-permute-done.4.refs_2_, bf16[8,128,128]{2,1,0:T(8,128)(2,1)S(1)} %tie.6.refs_3_, ...), custom_call_target="tpu_custom_call" | custom-call | flops 671088640 | bytes 5242880 | tf_op jit(solution)/shard_map/forward/pallas_call | solution.py:105
  38.2 0.7 forward.5.p0.token_ref
  38.9 0.0 copy-start.2
  38.9 0.0 copy-start.3
  39.0 0.1 collective-permute-start.10
  39.1 1.4 %collective-permute-start.7 = (bf16[640,128]{1,0:T(8,128)(2,1)S(1)}, bf16[640,128]{1,0:T(8,128)(2,1)S(1)}, u32[]{:S(2)}, u32[]{:S(2)}) collective-permute-start(bf16[640,128]{1,0:T(8,128)(2,1)S(1)} %forward.5.p0.token_ref), channel_id=1, source_target_pairs={{0,1},{1,2},{2,3},{3,0},{4,5},{5,6},{6,7},{7,4},{8,9},{9,10},{10,1... | collective-permute-start | bytes 491528 | tf_op jit(solution)/shard_map/ppermute | solution.py:40
  40.4 2.7 %collective-permute-start.8 = (bf16[640,128]{1,0:T(8,128)(2,1)S(1)}, bf16[640,128]{1,0:T(8,128)(2,1)S(1)}, u32[]{:S(2)}, u32[]{:S(2)}) collective-permute-start(bf16[640,128]{1,0:T(8,128)(2,1)S(1)} %forward.5.p0.token_ref), channel_id=1, source_target_pairs={{0,2},{1,3},{2,0},{3,1},{4,6},{5,7},{6,4},{7,5},{8,10},{9,11},{10,... | collective-permute-start | bytes 491528 | tf_op jit(solution)/shard_map/ppermute | solution.py:40
  43.1 1.0 %collective-permute-start.9 = (bf16[640,128]{1,0:T(8,128)(2,1)S(1)}, bf16[640,128]{1,0:T(8,128)(2,1)S(1)}, u32[]{:S(2)}, u32[]{:S(2)}) collective-permute-start(bf16[640,128]{1,0:T(8,128)(2,1)S(1)} %forward.5.p0.token_ref), channel_id=1, source_target_pairs={{0,3},{1,0},{2,1},{3,2},{4,7},{5,4},{6,5},{7,6},{8,11},{9,8},{10,9... | collective-permute-start | bytes 491528 | tf_op jit(solution)/shard_map/ppermute | solution.py:40
  44.1 0.1 pad_add_fusion.me_ref
  44.2 1.7 %collective-permute-done.7.p1 = bf16[640,128]{1,0:T(8,128)(2,1)S(1)} collective-permute-done((bf16[640,128]{1,0:T(8,128)(2,1)S(1)}, bf16[640,128]{1,0:T(8,128)(2,1)S(1)}, u32[]{:S(2)}, u32[]{:S(2)}) %collective-permute-start.7) | collective-permute-done | bytes 163872 | tf_op jit(solution)/shard_map/ppermute | solution.py:40
  45.9 4.6 %collective-permute-done.8.p2 = bf16[640,128]{1,0:T(8,128)(2,1)S(1)} collective-permute-done((bf16[640,128]{1,0:T(8,128)(2,1)S(1)}, bf16[640,128]{1,0:T(8,128)(2,1)S(1)}, u32[]{:S(2)}, u32[]{:S(2)}) %collective-permute-start.8) | collective-permute-done | bytes 163872 | tf_op jit(solution)/shard_map/ppermute | solution.py:40
  50.5 1.0 %middle.1 = (f32[128,128]{1,0:T(8,128)S(1)}, bf16[592,128]{1,0:T(8,128)(2,1)S(1)}, f32[64,128]{1,0:T(8,128)S(1)}) custom-call(s32[4]{0:T(128)S(1)} %pad_add_fusion.me_ref, bf16[640,128]{1,0:T(8,128)(2,1)S(1)} %forward.5.p0.token_ref, bf16[640,128]{1,0:T(8,128)(2,1)S(1)} %collective-permute-done.7.p1, bf16[640,128]{1,0:T(8,128)(2,1)S(1)} %collective-permute-done.8.p2, ...), custom_call_target="tpu_custom_call" | custom-call | flops 50331648 | bytes 1048576 | tf_op jit(solution)/shard_map/middle/pallas_call | solution.py:170
  51.5 1.3 %collective-permute-start.11 = (bf16[592,128]{1,0:T(8,128)(2,1)S(1)}, bf16[592,128]{1,0:T(8,128)(2,1)S(1)}, u32[]{:S(2)}, u32[]{:S(2)}) collective-permute-start(bf16[592,128]{1,0:T(8,128)(2,1)S(1)} %get-tuple-element.15.give_ref), channel_id=1, source_target_pairs={{0,4},{4,0},{1,5},{5,1},{2,6},{6,2},{3,7},{7,3},{8,12},{12,8},{9,1... | collective-permute-start | bytes 454664 | tf_op jit(solution)/shard_map/ppermute | solution.py:40
  52.8 1.2 %backward_own.1.begun_ref = f32[4,8,128,128]{3,2,1,0:T(8,128)S(1)} custom-call(bf16[32,512,128]{2,1,0:T(8,128)(2,1)S(1)} %get-tuple-element.13.token_ref.refs_0_.mine_ref, bf16[592,128]{1,0:T(8,128)(2,1)S(1)} %get-tuple-element.15.give_ref), custom_call_target="tpu_custom_call" | custom-call | flops 536870912 | bytes 4194304 | tf_op jit(solution)/shard_map/backward_own/pallas_call | solution.py:218
  54.1 0.3 backward.5
  54.4 1.1 %collective-permute-start.12 = (bf16[1104,128]{1,0:T(8,128)(2,1)S(1)}, bf16[1104,128]{1,0:T(8,128)(2,1)S(1)}, u32[]{:S(2)}, u32[]{:S(2)}) collective-permute-start(bf16[1104,128]{1,0:T(8,128)(2,1)S(1)} %backward.5), channel_id=1, source_target_pairs={{0,8},{8,16},{16,24},{24,0},{1,9},{9,17},{17,25},{25,1},{2,10},{10... | collective-permute-start | bytes 847880 | tf_op jit(solution)/shard_map/ppermute | solution.py:40
  55.5 0.3 backward.6
  55.8 2.3 %collective-permute-start.13 = (bf16[1104,128]{1,0:T(8,128)(2,1)S(1)}, bf16[1104,128]{1,0:T(8,128)(2,1)S(1)}, u32[]{:S(2)}, u32[]{:S(2)}) collective-permute-start(bf16[1104,128]{1,0:T(8,128)(2,1)S(1)} %backward.6), channel_id=1, source_target_pairs={{0,16},{8,24},{16,0},{24,8},{1,17},{9,25},{17,1},{25,9},{2,18},{10... | collective-permute-start | bytes 847880 | tf_op jit(solution)/shard_map/ppermute | solution.py:40
  58.1 0.3 backward.7
  58.4 0.4 collective-permute-start.14
  58.9 0.9 backward.4
  59.7 3.1 %collective-permute-done.12.r1 = bf16[1104,128]{1,0:T(8,128)(2,1)S(1)} collective-permute-done((bf16[1104,128]{1,0:T(8,128)(2,1)S(1)}, bf16[1104,128]{1,0:T(8,128)(2,1)S(1)}, u32[]{:S(2)}, u32[]{:S(2)}) %collective-permute-start.12) | collective-permute-done | bytes 282656 | tf_op jit(solution)/shard_map/ppermute | solution.py:40
  62.8 2.6 %collective-permute-done.13.r2 = bf16[1104,128]{1,0:T(8,128)(2,1)S(1)} collective-permute-done((bf16[1104,128]{1,0:T(8,128)(2,1)S(1)}, bf16[1104,128]{1,0:T(8,128)(2,1)S(1)}, u32[]{:S(2)}, u32[]{:S(2)}) %collective-permute-start.13) | collective-permute-done | bytes 282656 | tf_op jit(solution)/shard_map/ppermute | solution.py:40
  65.4 6.7 %collective-permute-done.14.r3 = bf16[1104,128]{1,0:T(8,128)(2,1)S(1)} collective-permute-done((bf16[1104,128]{1,0:T(8,128)(2,1)S(1)}, bf16[1104,128]{1,0:T(8,128)(2,1)S(1)}, u32[]{:S(2)}, u32[]{:S(2)}) %collective-permute-start.14) | collective-permute-done | bytes 282656 | tf_op jit(solution)/shard_map/ppermute | solution.py:40
  72.1 0.2 line_sum.1
  72.3 16.9 %all_to_all.11.in_ref = bf16[8,208,128]{2,1,0:T(8,128)(2,1)S(1)} all-to-all(bf16[8,208,128]{2,1,0:T(8,128)(2,1)S(1)} %line_sum.1), channel_id=1, replica_groups=mesh['z'=8,'x'=4,'core'=2,'rep'=4] {'z'}, dimensions={0} | all-to-all | bytes 851968 | tf_op jit(solution)/shard_map/all_to_all | solution.py:356
  89.2 2.1 %collective-permute-start.15 = (f32[64,128]{1,0:T(8,128)S(1)}, f32[64,128]{1,0:T(8,128)S(1)}, u32[]{:S(2)}, u32[]{:S(2)}) collective-permute-start(f32[64,128]{1,0:T(8,128)S(1)} %finish_terms.1), channel_id=1, source_target_pairs={{0,4},{4,0},{1,5},{5,1},{2,6},{6,2},{3,7},{7,3},{8,12},{12,8},{9,1... | collective-permute-start | bytes 98312 | tf_op jit(solution)/shard_map/ppermute | solution.py:40
  91.3 0.7 finish_grad.1
  92.1 0.1 collective-permute-done.15
  92.2 0.6 maximum_select_fusion
  (15 shorter events, 0.1 us)
Async XLA Ops:
  19.8 14.9 %collective-permute-start.5 = (bf16[8,128,128]{2,1,0:T(8,128)(2,1)S(1)}, bf16[8,128,128]{2,1,0:T(8,128)(2,1)S(1)}, u32[]{:S(2)}, u32[]{:S(2)}) collective-permute-start(bf16[8,128,128]{2,1,0:T(8,128)(2,1)S(1)} %all_to_all.10.refs_2_), channel_id=1, source_target_pairs={{0,8},{8,16},{16,24},{24,0},{1,9},{9,17},{17,25},{25,1},{2,10},{10... | collective-permute-start | bytes 786440 | tf_op jit(solution)/shard_map/ppermute | solution.py:40
  21.0 13.8 %collective-permute-start = (bf16[8,128,128]{2,1,0:T(8,128)(2,1)S(1)}, bf16[8,128,128]{2,1,0:T(8,128)(2,1)S(1)}, u32[]{:S(2)}, u32[]{:S(2)}) collective-permute-start(bf16[8,128,128]{2,1,0:T(8,128)(2,1)S(1)} %all_to_all.10.refs_2_), channel_id=1, source_target_pairs={{0,16},{8,24},{16,0},{24,8},{1,17},{9,25},{17,1},{25,9},{2,18},{10... | collective-permute-start | bytes 786440 | tf_op jit(solution)/shard_map/ppermute | solution.py:40
  21.8 13.3 %collective-permute-start.2 = (bf16[8,128,128]{2,1,0:T(8,128)(2,1)S(1)}, bf16[8,128,128]{2,1,0:T(8,128)(2,1)S(1)}, u32[]{:S(2)}, u32[]{:S(2)}) collective-permute-start(bf16[8,128,128]{2,1,0:T(8,128)(2,1)S(1)} %all_to_all.10.refs_2_), channel_id=1, source_target_pairs={{0,24},{8,0},{16,8},{24,16},{1,25},{9,1},{17,9},{25,17},{2,26},{10... | collective-permute-start | bytes 786440 | tf_op jit(solution)/shard_map/ppermute | solution.py:40
  25.1 2.2 %copy-start = (bf16[1,1,128,128,128]{4,3,2,1,0:T(8,128)(2,1)S(1)}, bf16[1,1,128,128,128]{4,3,2,1,0:T(8,128)(2,1)}, u32[]{:S(2)}) copy-start(bf16[1,1,128,128,128]{4,3,2,1,0:T(8,128)(2,1)} %param.12) | copy-start | bytes 12582916
  31.7 5.0 %collective-permute-start.4 = (bf16[8,128,128]{2,1,0:T(8,128)(2,1)S(1)}, bf16[8,128,128]{2,1,0:T(8,128)(2,1)S(1)}, u32[]{:S(2)}, u32[]{:S(2)}) collective-permute-start(bf16[8,128,128]{2,1,0:T(8,128)(2,1)S(1)} %all_to_all.10.refs_2_), channel_id=1, source_target_pairs={{0,4},{4,0},{1,5},{5,1},{2,6},{6,2},{3,7},{7,3},{8,12},{12,8},{9,1... | collective-permute-start | bytes 786440 | tf_op jit(solution)/shard_map/ppermute | solution.py:40
  34.6 2.0 %collective-permute-start.6 = (bf16[8,128,128]{2,1,0:T(8,128)(2,1)S(1)}, bf16[8,128,128]{2,1,0:T(8,128)(2,1)S(1)}, u32[]{:S(2)}, u32[]{:S(2)}) collective-permute-start(bf16[8,128,128]{2,1,0:T(8,128)(2,1)S(1)} %tie.6.refs_3_), channel_id=1, source_target_pairs={{0,4},{4,0},{1,5},{5,1},{2,6},{6,2},{3,7},{7,3},{8,12},{12,8},{9,1... | collective-permute-start | bytes 786440 | tf_op jit(solution)/shard_map/ppermute | solution.py:40
  34.8 3.4 %collective-permute-start.1 = (bf16[8,128,128]{2,1,0:T(8,128)(2,1)S(1)}, bf16[8,128,128]{2,1,0:T(8,128)(2,1)S(1)}, u32[]{:S(2)}, u32[]{:S(2)}) collective-permute-start(bf16[8,128,128]{2,1,0:T(8,128)(2,1)S(1)} %tie.4.refs_5_), channel_id=1, source_target_pairs={{0,4},{4,0},{1,5},{5,1},{2,6},{6,2},{3,7},{7,3},{8,12},{12,8},{9,1... | collective-permute-start | bytes 786440 | tf_op jit(solution)/shard_map/ppermute | solution.py:40
  35.2 3.0 %collective-permute-start.3 = (bf16[8,128,128]{2,1,0:T(8,128)(2,1)S(1)}, bf16[8,128,128]{2,1,0:T(8,128)(2,1)S(1)}, u32[]{:S(2)}, u32[]{:S(2)}) collective-permute-start(bf16[8,128,128]{2,1,0:T(8,128)(2,1)S(1)} %tie.5.refs_6_), channel_id=1, source_target_pairs={{0,4},{4,0},{1,5},{5,1},{2,6},{6,2},{3,7},{7,3},{8,12},{12,8},{9,1... | collective-permute-start | bytes 786440 | tf_op jit(solution)/shard_map/ppermute | solution.py:40
  36.6 1.6 %copy-start.1 = (bf16[128,128]{1,0:T(8,128)(2,1)S(1)}, bf16[128,128]{1,0:T(8,128)(2,1)}, u32[]{:S(2)}) copy-start(bf16[128,128]{1,0:T(8,128)(2,1)} %refs_5_.1) | copy-start | bytes 98308
  38.9 11.6 %copy-start.2 = (bf16[128,128]{1,0:T(8,128)(2,1)S(1)}, bf16[128,128]{1,0:T(8,128)(2,1)}, u32[]{:S(2)}) copy-start(bf16[128,128]{1,0:T(8,128)(2,1)} %weight_ref.1) | copy-start | bytes 98308
  38.9 11.6 %copy-start.3 = (f32[128]{0:T(128)S(1)}, f32[128]{0:T(128)}, u32[]{:S(2)}) copy-start(f32[128]{0:T(128)} %param.10) | copy-start | bytes 1540
  39.0 15.1 %collective-permute-start.10 = (bf16[32,512,128]{2,1,0:T(8,128)(2,1)S(1)}, bf16[32,512,128]{2,1,0:T(8,128)(2,1)S(1)}, u32[]{:S(2)}, u32[]{:S(2)}) collective-permute-start(bf16[32,512,128]{2,1,0:T(8,128)(2,1)S(1)} %tie.7), channel_id=1, source_target_pairs={{0,4},{4,0},{1,5},{5,1},{2,6},{6,2},{3,7},{7,3},{8,12},{12,8},{9,1... | collective-permute-start | bytes 12582920 | tf_op jit(solution)/shard_map/ppermute | solution.py:40
  39.1 6.8 %collective-permute-start.7 = (bf16[640,128]{1,0:T(8,128)(2,1)S(1)}, bf16[640,128]{1,0:T(8,128)(2,1)S(1)}, u32[]{:S(2)}, u32[]{:S(2)}) collective-permute-start(bf16[640,128]{1,0:T(8,128)(2,1)S(1)} %forward.5.p0.token_ref), channel_id=1, source_target_pairs={{0,1},{1,2},{2,3},{3,0},{4,5},{5,6},{6,7},{7,4},{8,9},{9,10},{10,1... | collective-permute-start | bytes 491528 | tf_op jit(solution)/shard_map/ppermute | solution.py:40
  40.4 10.1 %collective-permute-start.8 = (bf16[640,128]{1,0:T(8,128)(2,1)S(1)}, bf16[640,128]{1,0:T(8,128)(2,1)S(1)}, u32[]{:S(2)}, u32[]{:S(2)}) collective-permute-start(bf16[640,128]{1,0:T(8,128)(2,1)S(1)} %forward.5.p0.token_ref), channel_id=1, source_target_pairs={{0,2},{1,3},{2,0},{3,1},{4,6},{5,7},{6,4},{7,5},{8,10},{9,11},{10,... | collective-permute-start | bytes 491528 | tf_op jit(solution)/shard_map/ppermute | solution.py:40
  43.1 7.4 %collective-permute-start.9 = (bf16[640,128]{1,0:T(8,128)(2,1)S(1)}, bf16[640,128]{1,0:T(8,128)(2,1)S(1)}, u32[]{:S(2)}, u32[]{:S(2)}) collective-permute-start(bf16[640,128]{1,0:T(8,128)(2,1)S(1)} %forward.5.p0.token_ref), channel_id=1, source_target_pairs={{0,3},{1,0},{2,1},{3,2},{4,7},{5,4},{6,5},{7,6},{8,11},{9,8},{10,9... | collective-permute-start | bytes 491528 | tf_op jit(solution)/shard_map/ppermute | solution.py:40
  51.5 2.6 %collective-permute-start.11 = (bf16[592,128]{1,0:T(8,128)(2,1)S(1)}, bf16[592,128]{1,0:T(8,128)(2,1)S(1)}, u32[]{:S(2)}, u32[]{:S(2)}) collective-permute-start(bf16[592,128]{1,0:T(8,128)(2,1)S(1)} %get-tuple-element.15.give_ref), channel_id=1, source_target_pairs={{0,4},{4,0},{1,5},{5,1},{2,6},{6,2},{3,7},{7,3},{8,12},{12,8},{9,1... | collective-permute-start | bytes 454664 | tf_op jit(solution)/shard_map/ppermute | solution.py:40
  54.4 8.4 %collective-permute-start.12 = (bf16[1104,128]{1,0:T(8,128)(2,1)S(1)}, bf16[1104,128]{1,0:T(8,128)(2,1)S(1)}, u32[]{:S(2)}, u32[]{:S(2)}) collective-permute-start(bf16[1104,128]{1,0:T(8,128)(2,1)S(1)} %backward.5), channel_id=1, source_target_pairs={{0,8},{8,16},{16,24},{24,0},{1,9},{9,17},{17,25},{25,1},{2,10},{10... | collective-permute-start | bytes 847880 | tf_op jit(solution)/shard_map/ppermute | solution.py:40
  55.8 9.6 %collective-permute-start.13 = (bf16[1104,128]{1,0:T(8,128)(2,1)S(1)}, bf16[1104,128]{1,0:T(8,128)(2,1)S(1)}, u32[]{:S(2)}, u32[]{:S(2)}) collective-permute-start(bf16[1104,128]{1,0:T(8,128)(2,1)S(1)} %backward.6), channel_id=1, source_target_pairs={{0,16},{8,24},{16,0},{24,8},{1,17},{9,25},{17,1},{25,9},{2,18},{10... | collective-permute-start | bytes 847880 | tf_op jit(solution)/shard_map/ppermute | solution.py:40
  58.4 13.7 %collective-permute-start.14 = (bf16[1104,128]{1,0:T(8,128)(2,1)S(1)}, bf16[1104,128]{1,0:T(8,128)(2,1)S(1)}, u32[]{:S(2)}, u32[]{:S(2)}) collective-permute-start(bf16[1104,128]{1,0:T(8,128)(2,1)S(1)} %backward.7), channel_id=1, source_target_pairs={{0,24},{8,0},{16,8},{24,16},{1,25},{9,1},{17,9},{25,17},{2,26},{10... | collective-permute-start | bytes 847880 | tf_op jit(solution)/shard_map/ppermute | solution.py:40
  89.2 3.0 %collective-permute-start.15 = (f32[64,128]{1,0:T(8,128)S(1)}, f32[64,128]{1,0:T(8,128)S(1)}, u32[]{:S(2)}, u32[]{:S(2)}) collective-permute-start(f32[64,128]{1,0:T(8,128)S(1)} %finish_terms.1), channel_id=1, source_target_pairs={{0,4},{4,0},{1,5},{5,1},{2,6},{6,2},{3,7},{7,3},{8,12},{12,8},{9,1... | collective-permute-start | bytes 98312 | tf_op jit(solution)/shard_map/ppermute | solution.py:40
